TPU v7x, 32 devices: a whole 2x2x4 slice. The times are simulated.
32 devices in a mesh: row: 8 (over z, y), col: 4 (over x, core).
Axes of the slice: x: 2, y: 2, z: 4, core: 2. Of those that a mesh axis runs over, the one named last changes fastest.
Arguments:
- table: float32 [4, 256, 256], P('col', 'row'), may hold values from -4 to 4
- marginals: int32 [1024], replicated, may hold values from 64 to 4095
- visits: int32 [8, 4, 16], P('row', 'col'), may hold values from 0 to 3
- counts: int32 [8, 4, 16, 256, 256], P('row', 'col'), may hold values from 0 to 16, as said below
Outputs:
- gradient: float32 [4, 256, 256], P('col')
Inputs may be any that keep to these rules, and one draw needn't show every extreme that they name: `counts`: about half of the cells of every tile are zero.
All inputs are finite; a program needn't handle non-finite values.
Results may differ from a plain program's by a relative error of at most 0.0031.
Values may be sent and summed in bfloat16 or wider, within the bound.
No kernel may reach another device: no remote copies, remote signals or barrier semaphores. Data moves between devices by JAX's collectives and lax.ppermute only.
A program may use at most 128 MiB of HBM per device.

v0:
```python
import jax
import jax.numpy as jnp
from jax import lax
from jax.sharding import PartitionSpec as P

K = 16


LOSS_SCALE = 0.0625


def from_root(value, axis, source):
    kept = jnp.where(lax.axis_index(axis) == source, value, 0).astype(value.dtype)
    return lax.psum(kept, axis)


def tile_terms(row_vectors, col_vectors, count_tile, log_rows, log_cols, log_total):
    logits = lax.dot_general(
        row_vectors, col_vectors, (((1,), (1,)), ((), ())), preferred_element_type=jnp.float32
    )
    count_vals = count_tile.astype(jnp.float32)
    baseline = log_total - log_rows[:, None] - log_cols[None, :]
    margin = logits - baseline
    fitted = (0.1 + 0.25 * jnp.sqrt(count_vals)) * (margin - jnp.log(jnp.maximum(count_vals, 1.0)))
    soft_hinge = jax.nn.sigmoid(margin)
    grad_logits = (jnp.where(count_vals > 0, fitted, soft_hinge) * LOSS_SCALE).astype(jnp.bfloat16)
    row_term = jnp.dot(grad_logits, col_vectors, preferred_element_type=jnp.float32)
    col_term = lax.dot_general(
        grad_logits, row_vectors, (((0,), (0,)), ((), ())), preferred_element_type=jnp.float32
    )
    return (row_term, col_term)


def local(table, marginals, visits, counts):
    blocks = lax.axis_size("col")
    row_devices = lax.axis_size("row")
    own_block = lax.axis_index("row") % blocks
    pieces = table.astype(jnp.bfloat16)
    block_rows = pieces.shape[1] * row_devices
    embed_width = pieces.shape[2]
    log_marg = jnp.log(marginals.astype(jnp.float32)).reshape(blocks, block_rows)
    log_total = jnp.log(jnp.sum(marginals).astype(jnp.float32))
    visited = visits[0, 0]
    count_tiles = counts[0, 0]
    log_rows = log_marg[own_block]
    zero_block = jnp.zeros((block_rows, embed_width), jnp.float32)
    col_block = lax.all_gather(pieces, "row", axis=1, tiled=True)
    row_vectors = from_root(col_block, "col", own_block)[0]
    start_terms = jnp.zeros((K, block_rows, embed_width), jnp.float32)
    shards = lax.all_gather(col_block, "col", axis=0, tiled=True)
    visit_row_sum = zero_block
    visit_col_terms = start_terms
    for k in range(K):
        visit_id = visited[k]
        inside = (visit_id >= 0) & (visit_id < shards.shape[0])
        col_vectors = lax.dynamic_index_in_dim(
            shards, jnp.clip(visit_id, 0, shards.shape[0] - 1), 0, keepdims=False
        )

        def compute(vectors, tile_k=count_tiles[k], log_cols=log_marg[visit_id]):
            return tile_terms(row_vectors, vectors, tile_k, log_rows, log_cols, log_total)

        def skipped(vectors):
            return (zero_block, zero_block)

        row_term, col_term = lax.cond(inside, compute, skipped, col_vectors)
        visit_row_sum = visit_row_sum + row_term
        visit_col_terms = visit_col_terms.at[k].add(col_term)
    block_ids = jnp.arange(1 * lax.axis_size("col"), dtype=jnp.int32)
    result = jnp.zeros((1 * lax.axis_size("col"), block_rows, embed_width), jnp.float32)
    for dense_k in range(K):
        result = result + jnp.where(
            (block_ids == visited[dense_k])[:, None, None], visit_col_terms[dense_k][None], 0.0
        )
    result = result + jnp.where((block_ids == own_block)[:, None, None], visit_row_sum[None], 0.0)
    summed = lax.psum_scatter(result, "col", scatter_dimension=0, tiled=True)
    return lax.psum(summed, "row")


def solution(mesh):
    return jax.shard_map(
        local,
        mesh=mesh,
        in_specs=(
            P("col", "row", None),
            P(),
            P("row", "col", None),
            P("row", "col", None, None, None),
        ),
        out_specs=P("col", None, None),
        check_vma=False,
    )
```

profile of v0, /device:TPU:0, one launch (start us, length us, event | category | flops | bytes accessed | tf_op | source)
XLA Modules:
  0.0 386.6 jit_solution(15132513164715550980)
XLA Ops:
  7.3 32.3 %all_gather.6 = bf16[1,256,256]{2,1,0:T(8,128)(2,1)S(1)} all-gather(bf16[1,32,256]{2,1,0:T(8,128)(2,1)S(1)} %convert_element_type.204), channel_id=1, replica_groups=mesh['row'=8,'col'=4] {'row'}, dimensions={1}, use_global_device_ids=true | all-gather | bytes 147456 | tf_op jit(solution)/shard_map/all_gather | solution.py:47
  40.3 7.2 %all_gather.7 = bf16[4,256,256]{2,1,0:T(8,128)(2,1)S(1)} all-gather(bf16[1,256,256]{2,1,0:T(8,128)(2,1)S(1)} %all_gather.6), channel_id=1, replica_groups=mesh['row'=8,'col'=4] {'col'}, dimensions={0}, use_global_device_ids=true | all-gather | bytes 655360 | tf_op jit(solution)/shard_map/all_gather | solution.py:50
  86.9 12.2 %conditional.16 = (f32[256,256]{1,0:T(8,128)S(1)}, f32[16,256,256]{2,1,0:T(8,128)}) conditional(s32[]{:T(128)} %convert_element_type.203, () %tuple.261, (s32[1,1,16,256,256]{4,3,2,1,0:T(8,128)}, s32[]{:T(128)}, bf16[4,256,256]{2,1,0:T(8,128)(2,1)S(1)}, bf16[256,256]{1,0:T(8,128)(2,1)}, f32[]{:T(128)}, /*index=5*/f32[1,256]{1,0:T(1,128)S(1)}, ...), branch_computations={%region_2.3_spmd, %region_3.4_spmd} | conditional | flops 101646592 | bytes 15079546 | solution.py:66
  89.5 5.5 %copy.21 = s32[1,1,16,256,256]{3,4,2,1,0:T(8,128)} copy(s32[1,1,16,256,256]{4,3,2,1,0:T(8,128)} %get-tuple-element.1493) | data formatting | bytes 8388608 | tf_op jit(solution)/shard_map
  99.1 9.5 %conditional.17 = (f32[256,256]{1,0:T(8,128)S(1)}, f32[1,256,256]{2,1,0:T(8,128)S(1)}) conditional(s32[]{:T(128)} %convert_element_type.207, () %tuple.263, (s32[1,1,16,256,256]{4,3,2,1,0:T(8,128)}, s32[]{:T(128)}, bf16[4,256,256]{2,1,0:T(8,128)(2,1)S(1)}, bf16[256,256]{1,0:T(8,128)(2,1)}, f32[]{:T(128)}, /*index=5*/f32[1,256]{1,0:T(1,128)S(1)}, ...), branch_computations={%region_4.5_spmd, %region_5.6_spmd} | conditional | flops 101646592 | bytes 10623094 | solution.py:66
  101.4 5.5 %copy.22 = s32[1,1,16,256,256]{3,4,2,1,0:T(8,128)} copy(s32[1,1,16,256,256]{4,3,2,1,0:T(8,128)} %get-tuple-element.1500) | data formatting | bytes 8388608 | tf_op jit(solution)/shard_map
  109.3 9.9 %conditional.18 = (f32[256,256]{1,0:T(8,128)S(1)}, f32[1,256,256]{2,1,0:T(8,128)S(1)}) conditional(s32[]{:T(128)} %convert_element_type.208, () %tuple.265, (s32[1,1,16,256,256]{4,3,2,1,0:T(8,128)}, s32[]{:T(128)}, bf16[4,256,256]{2,1,0:T(8,128)(2,1)S(1)}, bf16[256,256]{1,0:T(8,128)(2,1)}, f32[]{:T(128)}, /*index=5*/f32[1,256]{1,0:T(1,128)S(1)}, ...), branch_computations={%region_6.7_spmd, %region_7.8_spmd} | conditional | flops 101646592 | bytes 10623094 | solution.py:66
  112.0 5.5 %copy.23 = s32[1,1,16,256,256]{3,4,2,1,0:T(8,128)} copy(s32[1,1,16,256,256]{4,3,2,1,0:T(8,128)} %get-tuple-element.1507) | data formatting | bytes 8388608 | tf_op jit(solution)/shard_map
  120.9 9.9 %conditional.19 = (f32[256,256]{1,0:T(8,128)S(1)}, f32[1,256,256]{2,1,0:T(8,128)S(1)}) conditional(s32[]{:T(128)} %convert_element_type.209, () %tuple.267, (s32[1,1,16,256,256]{4,3,2,1,0:T(8,128)}, s32[]{:T(128)}, bf16[4,256,256]{2,1,0:T(8,128)(2,1)S(1)}, bf16[256,256]{1,0:T(8,128)(2,1)}, f32[]{:T(128)}, /*index=5*/f32[1,256]{1,0:T(1,128)S(1)}, ...), branch_computations={%region_8.9_spmd, %region_9.10_spmd} | conditional | flops 101646592 | bytes 10623094 | solution.py:66
  132.5 9.7 %conditional.20 = (f32[256,256]{1,0:T(8,128)S(1)}, f32[1,256,256]{2,1,0:T(8,128)S(1)}) conditional(s32[]{:T(128)} %convert_element_type.210, () %tuple.269, (s32[1,1,16,256,256]{4,3,2,1,0:T(8,128)}, s32[]{:T(128)}, bf16[4,256,256]{2,1,0:T(8,128)(2,1)S(1)}, bf16[256,256]{1,0:T(8,128)(2,1)}, f32[]{:T(128)}, /*index=5*/f32[1,256]{1,0:T(1,128)S(1)}, ...), branch_computations={%region_10.11_spmd, %region_11.12_spmd} | conditional | flops 101646592 | bytes 10623094 | solution.py:66
  143.8 9.7 %conditional.21 = (f32[256,256]{1,0:T(8,128)S(1)}, f32[1,256,256]{2,1,0:T(8,128)S(1)}) conditional(s32[]{:T(128)} %convert_element_type.211, () %tuple.271, (s32[1,1,16,256,256]{4,3,2,1,0:T(8,128)}, s32[]{:T(128)}, bf16[4,256,256]{2,1,0:T(8,128)(2,1)S(1)}, bf16[256,256]{1,0:T(8,128)(2,1)}, f32[]{:T(128)}, /*index=5*/f32[1,256]{1,0:T(1,128)S(1)}, ...), branch_computations={%region_12.13_spmd, %region_13.14_spmd} | conditional | flops 101646592 | bytes 10623094 | solution.py:66
  155.2 9.5 %conditional.22 = (f32[256,256]{1,0:T(8,128)S(1)}, f32[1,256,256]{2,1,0:T(8,128)S(1)}) conditional(s32[]{:T(128)} %convert_element_type.212, () %tuple.273, (s32[1,1,16,256,256]{4,3,2,1,0:T(8,128)}, s32[]{:T(128)}, bf16[4,256,256]{2,1,0:T(8,128)(2,1)S(1)}, bf16[256,256]{1,0:T(8,128)(2,1)}, f32[]{:T(128)}, /*index=5*/f32[1,256]{1,0:T(1,128)S(1)}, ...), branch_computations={%region_14.15_spmd, %region_15.16_spmd} | conditional | flops 101646592 | bytes 10623094 | solution.py:66
  166.4 9.7 %conditional.23 = (f32[256,256]{1,0:T(8,128)S(1)}, f32[1,256,256]{2,1,0:T(8,128)S(1)}) conditional(s32[]{:T(128)} %convert_element_type.213, () %tuple.275, (s32[1,1,16,256,256]{4,3,2,1,0:T(8,128)}, s32[]{:T(128)}, bf16[4,256,256]{2,1,0:T(8,128)(2,1)S(1)}, bf16[256,256]{1,0:T(8,128)(2,1)}, f32[]{:T(128)}, /*index=5*/f32[1,256]{1,0:T(1,128)S(1)}, ...), branch_computations={%region_16.17_spmd, %region_17.18_spmd} | conditional | flops 101646592 | bytes 10623094 | solution.py:66
  177.8 10.0 %conditional.24 = (f32[256,256]{1,0:T(8,128)S(1)}, f32[1,256,256]{2,1,0:T(8,128)S(1)}) conditional(s32[]{:T(128)} %convert_element_type.214, () %tuple.277, (s32[1,1,16,256,256]{4,3,2,1,0:T(8,128)}, s32[]{:T(128)}, bf16[4,256,256]{2,1,0:T(8,128)(2,1)S(1)}, bf16[256,256]{1,0:T(8,128)(2,1)}, f32[]{:T(128)}, /*index=5*/f32[1,256]{1,0:T(1,128)S(1)}, ...), branch_computations={%region_18.19_spmd, %region_19.20_spmd} | conditional | flops 101646592 | bytes 10623094 | solution.py:66
  189.5 9.7 %conditional.25 = (f32[256,256]{1,0:T(8,128)S(1)}, f32[1,256,256]{2,1,0:T(8,128)S(1)}) conditional(s32[]{:T(128)} %convert_element_type.215, () %tuple.279, (s32[1,1,16,256,256]{4,3,2,1,0:T(8,128)}, s32[]{:T(128)}, bf16[4,256,256]{2,1,0:T(8,128)(2,1)S(1)}, bf16[256,256]{1,0:T(8,128)(2,1)}, f32[]{:T(128)}, /*index=5*/f32[1,256]{1,0:T(1,128)S(1)}, ...), branch_computations={%region_20.21_spmd, %region_21.22_spmd} | conditional | flops 101646592 | bytes 10623094 | solution.py:66
  200.9 9.4 %conditional.26 = (f32[256,256]{1,0:T(8,128)S(1)}, f32[1,256,256]{2,1,0:T(8,128)S(1)}) conditional(s32[]{:T(128)} %convert_element_type.216, () %tuple.281, (s32[1,1,16,256,256]{4,3,2,1,0:T(8,128)}, s32[]{:T(128)}, bf16[4,256,256]{2,1,0:T(8,128)(2,1)S(1)}, bf16[256,256]{1,0:T(8,128)(2,1)}, f32[]{:T(128)}, /*index=5*/f32[1,256]{1,0:T(1,128)S(1)}, ...), branch_computations={%region_22.23_spmd, %region_23.24_spmd} | conditional | flops 101646592 | bytes 10623094 | solution.py:66
  212.0 10.2 %conditional.27 = (f32[256,256]{1,0:T(8,128)S(1)}, f32[1,256,256]{2,1,0:T(8,128)S(1)}) conditional(s32[]{:T(128)} %convert_element_type.217, () %tuple.283, (s32[1,1,16,256,256]{4,3,2,1,0:T(8,128)}, s32[]{:T(128)}, bf16[4,256,256]{2,1,0:T(8,128)(2,1)S(1)}, bf16[256,256]{1,0:T(8,128)(2,1)}, f32[]{:T(128)}, /*index=5*/f32[1,256]{1,0:T(1,128)S(1)}, ...), branch_computations={%region_24.25_spmd, %region_25.26_spmd} | conditional | flops 101646592 | bytes 10623094 | solution.py:66
  224.1 11.4 %conditional.28 = (f32[256,256]{1,0:T(8,128)}, f32[1,256,256]{2,1,0:T(8,128)}) conditional(s32[]{:T(128)} %convert_element_type.218, () %tuple.285, (s32[1,1,16,256,256]{4,3,2,1,0:T(8,128)}, s32[]{:T(128)}, bf16[4,256,256]{2,1,0:T(8,128)(2,1)S(1)}, bf16[256,256]{1,0:T(8,128)(2,1)}, f32[]{:T(128)}, /*index=5*/f32[1,256]{1,0:T(1,128)S(1)}, ...), branch_computations={%region_26.27_spmd, %region_27.28_spmd} | conditional | flops 101646592 | bytes 10623094 | solution.py:66
  237.4 10.3 %conditional.29 = (f32[256,256]{1,0:T(8,128)S(1)}, f32[1,256,256]{2,1,0:T(8,128)S(1)}) conditional(s32[]{:T(128)} %convert_element_type.219, () %tuple.287, (s32[1,1,16,256,256]{4,3,2,1,0:T(8,128)}, s32[]{:T(128)}, bf16[4,256,256]{2,1,0:T(8,128)(2,1)S(1)}, bf16[256,256]{1,0:T(8,128)(2,1)}, f32[]{:T(128)}, /*index=5*/f32[1,256]{1,0:T(1,128)S(1)}, ...), branch_computations={%region_28.29_spmd, %region_29.30_spmd} | conditional | flops 101646592 | bytes 10623094 | solution.py:66
  248.5 10.5 %conditional.30 = (f32[256,256]{1,0:T(8,128)S(1)}, f32[1,256,256]{2,1,0:T(8,128)S(1)}) conditional(s32[]{:T(128)} %convert_element_type.220, () %tuple.289, (s32[1,1,16,256,256]{4,3,2,1,0:T(8,128)}, s32[]{:T(128)}, bf16[4,256,256]{2,1,0:T(8,128)(2,1)S(1)}, bf16[256,256]{1,0:T(8,128)(2,1)}, f32[]{:T(128)}, /*index=5*/f32[1,256]{1,0:T(1,128)S(1)}, ...), branch_computations={%region_30.31_spmd, %region_31.32_spmd} | conditional | flops 101646592 | bytes 10623094 | solution.py:66
  259.8 11.8 %conditional.31 = (f32[256,256]{1,0:T(8,128)}, f32[1,256,256]{2,1,0:T(8,128)}) conditional(s32[]{:T(128)} %convert_element_type.221, () %tuple.291, (s32[1,1,16,256,256]{4,3,2,1,0:T(8,128)}, s32[]{:T(128)}, bf16[4,256,256]{2,1,0:T(8,128)(2,1)S(1)}, bf16[256,256]{1,0:T(8,128)(2,1)}, f32[]{:T(128)}, /*index=5*/f32[1,256]{1,0:T(1,128)S(1)}, ...), branch_computations={%region_32.33_spmd, %region_33.34_spmd} | conditional | flops 101646592 | bytes 10631342 | solution.py:66
  263.0 5.5 %copy.36 = s32[1,1,16,256,256]{3,4,2,1,0:T(8,128)} copy(s32[1,1,16,256,256]{4,3,2,1,0:T(8,128)} %get-tuple-element.1598) | data formatting | bytes 8388608 | tf_op jit(solution)/shard_map
  279.1 25.3 %reduce-scatter.2.cloned.1.call-done = f32[1,256,256]{2,1,0:T(8,128)} async-done(((f32[4,256,256]{2,1,0:T(8,128)}), f32[1,256,256]{2,1,0:T(8,128)}) %reduce-scatter.2.cloned.1.call-update) | async-done | bytes 262160 | tf_op jit(solution)/shard_map/reduce_scatter | solution.py:76
  304.5 73.9 %all-reduce.6.cloned.1.call-done = f32[1,256,256]{2,1,0:T(8,128)} async-done(((f32[1,256,256]{2,1,0:T(8,128)}), f32[1,256,256]{2,1,0:T(8,128)}) %all-reduce.6.cloned.1.call-update) | async-done | bytes 262160 | tf_op jit(solution)/shard_map/psum | solution.py:77
  (200 shorter events, 151.2 us)
Async XLA Ops:
  6.5 80.4 %all-reduce.4.cloned.1.call-start = ((), (), s32[]{:S(2)}) async-start(), calls=%async_computation.1 | async-start | bytes 262144 | tf_op jit(solution)/shard_map/psum | solution.py:14
  40.3 264.1 %reduce-scatter.2.cloned.1.call-start = ((), (), s32[]{:S(2)}) async-start(), calls=%async_computation.2 | async-start | bytes 1310720 | tf_op jit(solution)/shard_map/reduce_scatter | solution.py:76
  89.5 5.5 %copy-start = (bf16[256,256]{1,0:T(8,128)(2,1)S(1)}, bf16[256,256]{1,0:T(8,128)(2,1)}, u32[]{:S(2)}) copy-start(bf16[256,256]{1,0:T(8,128)(2,1)} %get-tuple-element.1208) | copy-start | bytes 393220 | tf_op jit(solution)/shard_map/cond
  101.4 5.5 %copy-start.1 = (bf16[256,256]{1,0:T(8,128)(2,1)S(1)}, bf16[256,256]{1,0:T(8,128)(2,1)}, u32[]{:S(2)}) copy-start(bf16[256,256]{1,0:T(8,128)(2,1)} %get-tuple-element.1215) | copy-start | bytes 393220 | tf_op jit(solution)/shard_map/cond
  112.0 5.5 %copy-start.2 = (bf16[256,256]{1,0:T(8,128)(2,1)S(1)}, bf16[256,256]{1,0:T(8,128)(2,1)}, u32[]{:S(2)}) copy-start(bf16[256,256]{1,0:T(8,128)(2,1)} %get-tuple-element.1222) | copy-start | bytes 393220 | tf_op jit(solution)/shard_map/cond
  123.6 5.5 %copy-start.3 = (bf16[256,256]{1,0:T(8,128)(2,1)S(1)}, bf16[256,256]{1,0:T(8,128)(2,1)}, u32[]{:S(2)}) copy-start(bf16[256,256]{1,0:T(8,128)(2,1)} %get-tuple-element.1229) | copy-start | bytes 393220 | tf_op jit(solution)/shard_map/cond
  135.0 5.5 %copy-start.4 = (bf16[256,256]{1,0:T(8,128)(2,1)S(1)}, bf16[256,256]{1,0:T(8,128)(2,1)}, u32[]{:S(2)}) copy-start(bf16[256,256]{1,0:T(8,128)(2,1)} %get-tuple-element.1236) | copy-start | bytes 393220 | tf_op jit(solution)/shard_map/cond
  146.3 5.5 %copy-start.5 = (bf16[256,256]{1,0:T(8,128)(2,1)S(1)}, bf16[256,256]{1,0:T(8,128)(2,1)}, u32[]{:S(2)}) copy-start(bf16[256,256]{1,0:T(8,128)(2,1)} %get-tuple-element.1243) | copy-start | bytes 393220 | tf_op jit(solution)/shard_map/cond
  157.5 5.5 %copy-start.6 = (bf16[256,256]{1,0:T(8,128)(2,1)S(1)}, bf16[256,256]{1,0:T(8,128)(2,1)}, u32[]{:S(2)}) copy-start(bf16[256,256]{1,0:T(8,128)(2,1)} %get-tuple-element.1250) | copy-start | bytes 393220 | tf_op jit(solution)/shard_map/cond
  169.0 5.5 %copy-start.7 = (bf16[256,256]{1,0:T(8,128)(2,1)S(1)}, bf16[256,256]{1,0:T(8,128)(2,1)}, u32[]{:S(2)}) copy-start(bf16[256,256]{1,0:T(8,128)(2,1)} %get-tuple-element.1257) | copy-start | bytes 393220 | tf_op jit(solution)/shard_map/cond
  180.6 5.5 %copy-start.8 = (bf16[256,256]{1,0:T(8,128)(2,1)S(1)}, bf16[256,256]{1,0:T(8,128)(2,1)}, u32[]{:S(2)}) copy-start(bf16[256,256]{1,0:T(8,128)(2,1)} %get-tuple-element.1264) | copy-start | bytes 393220 | tf_op jit(solution)/shard_map/cond
  192.0 5.5 %copy-start.9 = (bf16[256,256]{1,0:T(8,128)(2,1)S(1)}, bf16[256,256]{1,0:T(8,128)(2,1)}, u32[]{:S(2)}) copy-start(bf16[256,256]{1,0:T(8,128)(2,1)} %get-tuple-element.1271) | copy-start | bytes 393220 | tf_op jit(solution)/shard_map/cond
  203.1 5.5 %copy-start.10 = (bf16[256,256]{1,0:T(8,128)(2,1)S(1)}, bf16[256,256]{1,0:T(8,128)(2,1)}, u32[]{:S(2)}) copy-start(bf16[256,256]{1,0:T(8,128)(2,1)} %get-tuple-element.1278) | copy-start | bytes 393220 | tf_op jit(solution)/shard_map/cond
  215.1 5.5 %copy-start.11 = (bf16[256,256]{1,0:T(8,128)(2,1)S(1)}, bf16[256,256]{1,0:T(8,128)(2,1)}, u32[]{:S(2)}) copy-start(bf16[256,256]{1,0:T(8,128)(2,1)} %get-tuple-element.1285) | copy-start | bytes 393220 | tf_op jit(solution)/shard_map/cond
  226.9 5.5 %copy-start.12 = (bf16[256,256]{1,0:T(8,128)(2,1)S(1)}, bf16[256,256]{1,0:T(8,128)(2,1)}, u32[]{:S(2)}) copy-start(bf16[256,256]{1,0:T(8,128)(2,1)} %get-tuple-element.1292) | copy-start | bytes 393220 | tf_op jit(solution)/shard_map/cond
  240.5 5.5 %copy-start.13 = (bf16[256,256]{1,0:T(8,128)(2,1)S(1)}, bf16[256,256]{1,0:T(8,128)(2,1)}, u32[]{:S(2)}) copy-start(bf16[256,256]{1,0:T(8,128)(2,1)} %get-tuple-element.1299) | copy-start | bytes 393220 | tf_op jit(solution)/shard_map/cond
  251.8 5.5 %copy-start.14 = (bf16[256,256]{1,0:T(8,128)(2,1)S(1)}, bf16[256,256]{1,0:T(8,128)(2,1)}, u32[]{:S(2)}) copy-start(bf16[256,256]{1,0:T(8,128)(2,1)} %get-tuple-element.1306) | copy-start | bytes 393220 | tf_op jit(solution)/shard_map/cond
  263.0 5.5 %copy-start.15 = (bf16[256,256]{1,0:T(8,128)(2,1)S(1)}, bf16[256,256]{1,0:T(8,128)(2,1)}, u32[]{:S(2)}) copy-start(bf16[256,256]{1,0:T(8,128)(2,1)} %get-tuple-element.1313) | copy-start | bytes 393220 | tf_op jit(solution)/shard_map/cond
  263.0 5.5 %copy-start.39 = (f32[1,256]{1,0:T(1,128)S(1)}, f32[1,256]{1,0:T(1,128)}, u32[]{:S(2)}) copy-start(f32[1,256]{1,0:T(1,128)} %get-tuple-element.1635) | copy-start | bytes 3076 | tf_op jit(solution)/shard_map/cond
  263.0 5.5 %copy-start.40 = (f32[1,256]{1,0:T(1,128)S(1)}, f32[1,256]{1,0:T(1,128)}, u32[]{:S(2)}) copy-start(f32[1,256]{1,0:T(1,128)} %get-tuple-element.1636) | copy-start | bytes 3076 | tf_op jit(solution)/shard_map/cond
  271.6 3.0 copy-start.17
  271.6 3.1 copy-start.19
  271.6 3.1 copy-start.22
  279.1 99.3 %all-reduce.6.cloned.1.call-start = ((), (), s32[]{:S(2)}) async-start(), calls=%async_computation.3 | async-start | bytes 524288 | tf_op jit(solution)/shard_map/psum | solution.py:77
  (21 other events, 28.8 us)
Sparse Core Ops, SparseCore 0:
  40.4 32.3 all-reduce.3
  279.2 25.1 reduce-scatter.1
  307.8 70.5 all-reduce.5
where the time goes:
time: 390 us; the launch traced here: 387 us
  waiting for transfers between devices  99.2 us (25%)
  local copies, waits for them, and re-layouts  95.8 us (25%)
  other arithmetic  47.2 us (12%)
  loops' own time  40.5 us (10%)
  blocking collectives  39.5 us (10%)
  between operations  34.4 us (9%)
  matrix products  30 us (8%)
    another operation x16, local copies, waits for them, and re-layouts  87.2 us
    psum x1, waiting for transfers between devices, local(): return lax.psum(summed, 'row')  73.9 us
    another operation x16, loops' own time, local(): row_term, col_term = lax.cond(inside, compute, skipped, col_vectors)  40.5 us
    all_gather x1, blocking collectives, local(): col_block = lax.all_gather(pieces, 'row', axis=1, tiled=True)  32.3 us
    reduce_scatter x1, waiting for transfers between devices, local(): summed = lax.psum_scatter(result, 'col', scatter_dimension=0, tiled=True)  25.3 us
    dot_general x16, matrix products, tile_terms(): lax.dot_general(row_vectors, col_vectors, (((1,), (1,)), ((), ())), prefe...  20.7 us
    scatter-add x10, other arithmetic, local(): visit_col_terms = visit_col_terms.at[k].add(col_term)  17.1 us
    eq x8, other arithmetic, local(): block_ids == visited[dense_k]  14 us
  transfers between devices with their start and end apart: 3, of which 2 were waited for; matrix products, arithmetic and copies ran while one was open for 5% of the time, Pallas kernels for 0%

commit v1 on v0

v1 whole, which is shorter than its diff:
```python
import functools
import math

import jax
import jax.numpy as jnp
from jax import lax
from jax.experimental import pallas as pl
from jax.experimental.pallas import tpu as pltpu
from jax.sharding import Mesh, PartitionSpec as P

LOSS_SCALE = 0.0625
ROW = ("far", "near")
COL = ("chip", "core")
NT = (((1,), (1,)), ((), ()))
TN = (((0,), (0,)), ((), ()))
VMEM = pl.BlockSpec(memory_space=pltpu.VMEM)


MIB = 1024 * 1024


def count_kernel(tiles, visits_ref, counts_ref, roots_ref, logs_ref, live_ref, tiles_ref, visits, held, visits_sem, sems):
    size = counts_ref.shape[1]
    step = 32

    def fetch(k):
        return pltpu.make_async_copy(counts_ref.at[k], held.at[k], sems.at[k])

    fetch_visits = pltpu.make_async_copy(visits_ref, visits, visits_sem)
    fetch_visits.start()
    for k in range(tiles):
        fetch(k).start()
    for ref in (roots_ref, logs_ref, live_ref):
        ref[...] = jnp.zeros_like(ref)
    fetch_visits.wait()
    for v in range(tiles_ref.shape[0]):
        visited = 0
        for k in range(tiles):
            visited += (visits[0, 0, k] == v).astype(jnp.int32)
        tiles_ref[v : v + 1] = jnp.full((1, tiles_ref.shape[1]), visited.astype(jnp.float32))

    def add_tile(k, carry):
        fetch(k).wait()
        v = visits[0, 0, k]
        for first in range(0, size, step):
            rows = pl.ds(first, step)
            n = held[k, rows].astype(jnp.float32)
            clipped = jnp.maximum(n, 1.0)
            root = n * lax.rsqrt(clipped)
            roots_ref[v, rows] += root
            logs_ref[v, rows] += (root + 0.4) * jnp.log(clipped)
            live_ref[v, rows] += jnp.minimum(n, 1.0).astype(jnp.bfloat16)
        return carry

    lax.fori_loop(0, tiles, add_tile, 0)


def sum_counts(blocks, visits, counts):
    tiles, size = counts.shape[:2]
    hbm = pl.BlockSpec(memory_space=pltpu.HBM)
    return pl.pallas_call(
        functools.partial(count_kernel, tiles),
        out_shape=[
            jax.ShapeDtypeStruct((blocks, size, size), jnp.float32),
            jax.ShapeDtypeStruct((blocks, size, size), jnp.float32),
            jax.ShapeDtypeStruct((blocks, size, size), jnp.bfloat16),
            jax.ShapeDtypeStruct((blocks, size), jnp.float32),
        ],
        in_specs=[hbm, hbm],
        out_specs=[VMEM] * 4,
        scratch_shapes=[
            pltpu.SMEM(visits.shape, jnp.int32),
            pltpu.VMEM(counts.shape, jnp.int32),
            pltpu.SemaphoreType.DMA,
            pltpu.SemaphoreType.DMA((tiles,)),
        ],
        compiler_params=pltpu.CompilerParams(vmem_limit_bytes=(12 + 2 * blocks) * MIB),
        cost_estimate=pl.CostEstimate(
            flops=10 * counts.size, bytes_accessed=4 * counts.size, transcendentals=2 * counts.size
        ),
        name="sum_counts",
    )(pltpu.with_memory_space_constraint(visits, pltpu.HBM), pltpu.with_memory_space_constraint(counts, pltpu.HBM))


def stack_kernel(places, *refs):
    *parts, out_ref = refs
    for j, part in zip(places, parts):
        out_ref[j] = part[...].astype(out_ref.dtype)


def stack(parts):
    places = [0, *range(2, len(parts)), 1]
    return pl.pallas_call(
        functools.partial(stack_kernel, places),
        out_shape=jax.ShapeDtypeStruct((len(parts), *parts[0].shape), jnp.bfloat16),
        in_specs=[VMEM] * len(parts),
        out_specs=VMEM,
        compiler_params=pltpu.CompilerParams(vmem_limit_bytes=MIB),
        name="stack_parts",
    )(*[parts[j] for j in places])


def gradient_kernel(groups, marginals_ref, roots_ref, logs_ref, live_ref, tiles_ref, *refs):
    parts, (last_ref, *out_refs, table, grads, terms) = list(refs[: groups + 1]), refs[groups + 1 :]
    parts += [last_ref.at[j] for j in range(groups - 1)]
    far, chunk, width = parts[0].shape
    blocks, size = groups, grads.shape[0]
    here, core = lax.axis_index("chip"), lax.axis_index("core")
    z, near = lax.axis_index("far"), lax.axis_index("near")
    own = lax.rem(z * 2 + near, blocks)
    for other in range(2):
        for j in range(groups):
            block = jnp.bitwise_xor(here, j // 2) * 2 + jnp.bitwise_xor(core, other)
            for i in range(far):
                row = jnp.bitwise_xor(z, i) * 2 + jnp.bitwise_xor(near, j % 2)
                rows = pl.ds(pl.multiple_of(block * size + row * chunk, chunk), chunk)
                table[rows] = parts[other * groups + j][i].astype(table.dtype)

    marginals = marginals_ref[...].astype(jnp.float32)
    log_marg = jnp.log(marginals)
    log_total = jnp.log(jnp.sum(marginals, keepdims=True))
    own_rows = pl.ds(pl.multiple_of(own * size, size), size)
    own_vectors = table[own_rows].astype(jnp.bfloat16)
    own_log = jnp.log(marginals_ref[pl.ds(own, 1), :].astype(jnp.float32)) - log_total
    log_rows = jnp.transpose(jnp.broadcast_to(own_log, (128, size)))
    step = 64
    for v in range(blocks):
        vectors = table[v * size : (v + 1) * size].astype(jnp.bfloat16)
        visited = LOSS_SCALE * tiles_ref[v : v + 1]
        for first in range(0, size, step):
            rows = slice(first, first + step)
            logits = lax.dot_general(own_vectors[rows], vectors, NT, preferred_element_type=jnp.float32)
            log_row = jnp.concatenate([log_rows[rows]] * (size // 128), axis=1)
            margin = logits + log_row + log_marg[v : v + 1]
            live = live_ref[v, rows].astype(jnp.float32)
            weight = (0.25 * LOSS_SCALE) * roots_ref[v, rows] + (0.1 * LOSS_SCALE) * live
            zeros = visited - LOSS_SCALE * live
            grad = weight * margin - (0.25 * LOSS_SCALE) * logs_ref[v, rows] + zeros * jax.nn.sigmoid(margin)
            grads[rows, v * size : (v + 1) * size] = grad.astype(jnp.bfloat16)
    terms[...] = lax.dot_general(grads[...], own_vectors, TN, preferred_element_type=jnp.float32)
    terms[own_rows] += jnp.dot(
        grads[...], table[...].astype(jnp.bfloat16), preferred_element_type=jnp.float32
    )
    for j in range(blocks // 2):
        chip = jnp.bitwise_xor(here, j)
        first = 0
        for kept_ref, sent_ref in (out_refs[:2], out_refs[2:]):
            count = kept_ref.shape[1]
            stay = pl.multiple_of((2 * chip + core) * size + first, 16)
            leave = pl.multiple_of((2 * chip + 1 - core) * size + first, 16)
            kept_ref[j] = terms[pl.ds(stay, count)]
            sent_ref[j] = terms[pl.ds(leave, count)].astype(jnp.bfloat16)
            first += count


def swap(value, axis, bits):
    axes, bits = (axis, bits) if isinstance(axis, tuple) else ((axis,), (bits,))
    sizes = [lax.axis_size(name) for name in axes]
    both = 0
    for length, bit in zip(sizes, bits):
        both = both * length + bit
    return lax.ppermute(value, axes, [(i, i ^ both) for i in range(math.prod(sizes))])


def others(ask, count):
    order = sorted(range(1, count), key=lambda i: (-(i & -2), i))
    answers = {i: ask(i) for i in order}
    return [answers[i] for i in range(1, count)]


def tree_sum(values):
    while len(values) > 1:
        values = [one + two for one, two in zip(values[0::2], values[1::2])]
    return values[0]


def reduce_half(kept, sent, steps):
    bf16, f32 = jnp.bfloat16, jnp.float32
    total = kept + swap(sent, "core", 1).astype(f32)
    while total.shape[0] > 1:
        half = total.shape[0] // 2
        total = total[:half] + swap(total[half:].astype(bf16), "chip", half).astype(f32)
    total = total[0]
    for axis, bit in steps:
        mine = total.astype(bf16)
        total = mine.astype(f32) + swap(mine, axis, bit).astype(f32)
    return total


def local(table, marginals, visits, counts):
    chips, far = lax.axis_size("chip"), lax.axis_size("far")
    groups = blocks = 2 * chips
    size = counts.shape[3]
    width = table.shape[2]
    bf16, f32 = jnp.bfloat16, jnp.float32

    sums = sum_counts(blocks, visits, counts[0, 0])
    piece = table[0]
    pieces = others(lambda i: swap(piece, "far", i), far)
    column = stack([piece.astype(bf16)] + pieces)
    parts = others(lambda j: swap(column, ("near", "chip"), (j % 2, j // 2)), groups)
    other_column = swap(column, "core", 1)
    other_column, *parts, sums = lax.optimization_barrier((other_column, *parts, sums))
    parts = [column] + parts + [other_column, swap(stack(parts), "core", 1)]

    heights = (size // 2, size // 2)
    halves = pl.pallas_call(
        functools.partial(gradient_kernel, groups),
        out_shape=[
            jax.ShapeDtypeStruct((chips, rows, width), dtype) for rows in heights for dtype in (f32, bf16)
        ],
        in_specs=[VMEM] * (7 + groups),
        out_specs=[VMEM] * 4,
        scratch_shapes=[
            pltpu.VMEM((blocks * size, width), f32 if column.shape[1] % 16 else bf16),
            pltpu.VMEM((size, blocks * size), bf16),
            pltpu.VMEM((blocks * size, width), f32),
        ],
        compiler_params=pltpu.CompilerParams(vmem_limit_bytes=(6 + 3 * blocks) * MIB),
        cost_estimate=pl.CostEstimate(
            flops=10 * blocks * size * size * width,
            bytes_accessed=12 * blocks * size * size,
            transcendentals=blocks * size * size,
        ),
        name="swivel_gradient",
    )(marginals.reshape(blocks, size), *sums, *parts)

    steps = [("near", 1)] + [("far", 1 << i) for i in range(far.bit_length() - 1)]
    orders = (steps, steps[-1:] + steps[:-1])
    streams = [
        reduce_half(kept, sent, order) for kept, sent, order in zip(halves[0::2], halves[1::2], orders)
    ]
    return jnp.concatenate(streams, axis=0)[None]


def solution(mesh):
    rows, cols = mesh.shape["row"], mesh.shape["col"]
    split = Mesh(mesh.devices.reshape(rows // 2, 2, cols // 2, 2), ROW + COL)
    return jax.shard_map(
        local,
        mesh=split,
        in_specs=(
            P(COL, ROW, None),
            P(),
            P(ROW, COL, None),
            P(ROW, COL, None, None, None),
        ),
        out_specs=P(COL, None, None),
        check_vma=False,
    )
```

time: 390 us -> 43.1 us (0.11)
  local copies, waits for them, and re-layouts: 95.8 us -> 0.03 us
  waiting for transfers between devices: 99.2 us -> 18.2 us
  other arithmetic: 47.2 us -> 1.71 us
  loops' own time: 40.5 us -> 0 us
  blocking collectives: 39.5 us -> 0 us
  between operations: 34.4 us -> 0.14 us
  matrix products: 30 us -> 0 us
  starting transfers between devices: 0.09 us -> 18.7 us
  Pallas kernels: 0 us -> 4.17 us
    another operation x16 -> x0, local copies, waits for them, and re-layouts: 87.2 us -> none
    psum x2 -> x0, waiting for transfers between devices: 73.9 us -> none  [the longest x1 73.9 us: local(): return lax.psum(summed, 'row')]
    another operation x16 -> x0, loops' own time: 40.5 us -> none  [local(): row_term, col_term = lax.cond(inside, compute, skipped, col_vectors)]
    all_gather x2 -> x0, blocking collectives: 39.5 us -> none  [the longest x1 32.3 us: local(): col_block = lax.all_gather(pieces, 'row', axis=1, tiled=True)]
    dot_general x48 -> x0, matrix products: 30 us -> none  [the longest x16 20.7 us: tile_terms(): lax.dot_general(row_vectors, col_vectors, (((1,), (1,)), ((), ())), prefe...]
    reduce_scatter x1 -> x0, waiting for transfers between devices: 25.3 us -> none  [local(): summed = lax.psum_scatter(result, 'col', scatter_dimension=0, tiled=True)]
    ppermute x0 -> x18, starting transfers between devices: none -> 18.7 us  [swap(): lax.ppermute(value, axes, [(i, i ^ both) for i in range(math.prod(sizes))])]
    ppermute x0 -> x18, waiting for transfers between devices: none -> 18.2 us  [swap(): lax.ppermute(value, axes, [(i, i ^ both) for i in range(math.prod(sizes))])]
  transfers between devices with their start and end apart: 3 -> 18, of which waited for: 2 -> 13; matrix products, arithmetic and copies ran while one was open for 5% -> 2% of each run, Pallas kernels for 0% -> 7%
where the time goes in v1:
time: 43.1 us; the launch traced here: 42.9 us
  starting transfers between devices  18.7 us (43%)
  waiting for transfers between devices  18.2 us (42%)
  Pallas kernels  4.17 us (10%)
  other arithmetic  1.71 us (4%)
    ppermute x18, starting transfers between devices, swap(): lax.ppermute(value, axes, [(i, i ^ both) for i in range(math.prod(sizes))])  18.7 us
    ppermute x18, waiting for transfers between devices, swap(): lax.ppermute(value, axes, [(i, i ^ both) for i in range(math.prod(sizes))])  18.2 us
    pallas_call x1, Pallas kernels, sum_counts(): pl.pallas_call(functools.partial(count_kernel, tiles), out_shape=[jax.Sha...  2.82 us
    pallas_call x1, Pallas kernels, local(): pl.pallas_call(functools.partial(gradient_kernel, groups), out_shape=[jax...  1.33 us
  transfers between devices with their start and end apart: 18, of which 13 were waited for; matrix products, arithmetic and copies ran while one was open for 2% of the time, Pallas kernels for 7%

profile of v1, /device:TPU:0, one launch (start us, length us, event | category | flops | bytes accessed | tf_op | source)
XLA Modules:
  0.0 42.9 jit_solution(16399340906423590558)
XLA Ops:
  0.0 5.0 %collective-permute-start.1 = (f32[32,256]{1,0:T(8,128)}, f32[32,256]{1,0:T(8,128)S(1)}, u32[]{:S(2)}, u32[]{:S(2)}) collective-permute-start(f32[32,256]{1,0:T(8,128)} %bitcast.10), channel_id=1, source_target_pairs={{0,24},{8,16},{16,8},{24,0},{1,25},{9,17},{17,9},{25,1},{2,26},{10... | collective-permute-start | bytes 98312 | tf_op jit(solution)/shard_map/ppermute | solution.py:162
  5.1 0.6 %collective-permute-start.2 = (f32[32,256]{1,0:T(8,128)}, f32[32,256]{1,0:T(8,128)S(1)}, u32[]{:S(2)}, u32[]{:S(2)}) collective-permute-start(f32[32,256]{1,0:T(8,128)} %bitcast.12), channel_id=1, source_target_pairs={{0,8},{8,0},{16,24},{24,16},{1,9},{9,1},{17,25},{25,17},{2,10},{10... | collective-permute-start | bytes 98312 | tf_op jit(solution)/shard_map/ppermute | solution.py:162
  5.7 0.8 %bitcast_convert_fusion.refs_0_ = bf16[32,256]{1,0:T(8,128)(2,1)S(1)} fusion(f32[1,32,256]{2,1,0:T(8,128)} %param.4), kind=kLoop, calls=%fused_computation.17 | loop fusion | flops 8192 | bytes 49152 | tf_op jit(solution)/shard_map/convert_element_type | solution.py:200
  6.5 0.7 %collective-permute-done.1.refs_2_ = f32[32,256]{1,0:T(8,128)S(1)} collective-permute-done((f32[32,256]{1,0:T(8,128)}, f32[32,256]{1,0:T(8,128)S(1)}, u32[]{:S(2)}, u32[]{:S(2)}) %collective-permute-start.1) | collective-permute-done | bytes 32800 | tf_op jit(solution)/shard_map/ppermute | solution.py:162
  7.2 2.9 %collective-permute-done.refs_1_ = f32[32,256]{1,0:T(8,128)S(1)} collective-permute-done((f32[32,256]{1,0:T(8,128)}, f32[32,256]{1,0:T(8,128)S(1)}, u32[]{:S(2)}, u32[]{:S(2)}) %collective-permute-start) | collective-permute-done | bytes 32800 | tf_op jit(solution)/shard_map/ppermute | solution.py:162
  10.1 2.5 %collective-permute-start.6 = (bf16[4,32,256]{2,1,0:T(8,128)(2,1)S(1)}, bf16[4,32,256]{2,1,0:T(8,128)(2,1)S(1)}, u32[]{:S(2)}, u32[]{:S(2)}) collective-permute-start(bf16[4,32,256]{2,1,0:T(8,128)(2,1)S(1)} %stack_parts.2.refs_0_), channel_id=1, source_target_pairs={{0,6},{2,4},{4,2},{6,0},{1,7},{3,5},{5,3},{7,1},{8,14},{10,12},{12... | collective-permute-start | bytes 196616 | tf_op jit(solution)/shard_map/ppermute | solution.py:162
  13.7 2.8 %sum_counts.1 = (f32[4,256,256]{2,1,0:T(8,128)S(1)}, f32[4,256,256]{2,1,0:T(8,128)S(1)}, bf16[4,256,256]{2,1,0:T(8,128)(2,1)S(1)}, f32[4,256]{1,0:T(4,128)S(1)}) custom-call(s32[1,1,16]{2,1,0:T(1,128)} %visits_ref.1, s32[16,256,256]{2,1,0:T(8,128)} %bitcast.9), custom_call_target="tpu_custom_call" | custom-call | flops 10485760 | bytes 4194304 | tf_op jit(solution)/shard_map/sum_counts/pallas_call | solution.py:61
  16.9 0.5 %collective-permute-done.4.refs_0_.refs_1_ = bf16[4,32,256]{2,1,0:T(8,128)(2,1)S(1)} collective-permute-done((bf16[4,32,256]{2,1,0:T(8,128)(2,1)S(1)}, bf16[4,32,256]{2,1,0:T(8,128)(2,1)S(1)}, u32[]{:S(2)}, u32[]{:S(2)}) %collective-permute-start.4) | collective-permute-done | bytes 65568 | tf_op jit(solution)/shard_map/ppermute | solution.py:162
  17.5 1.4 %collective-permute-done.7.refs_5_ = bf16[3,4,32,256]{3,2,1,0:T(8,128)(2,1)S(1)} collective-permute-done((bf16[3,4,32,256]{3,2,1,0:T(8,128)(2,1)S(1)}, bf16[3,4,32,256]{3,2,1,0:T(8,128)(2,1)S(1)}, u32[]{:S(2)}, u32[]{:S(2)}) %collective-permute-start.7) | collective-permute-done | bytes 196640 | tf_op jit(solution)/shard_map/ppermute | solution.py:162
  18.9 1.3 %swivel_gradient.1 = (f32[2,128,256]{2,1,0:T(8,128)S(1)}, bf16[2,128,256]{2,1,0:T(8,128)(2,1)S(1)}, f32[2,128,256]{2,1,0:T(8,128)S(1)}, bf16[2,128,256]{2,1,0:T(8,128)(2,1)S(1)}) custom-call(s32[4,256]{1,0:T(4,128)S(1)} %reshape.5.marginals_ref, f32[4,256,256]{2,1,0:T(8,128)S(1)} %get-tuple-element.25.roots_ref, ...), custom_call_target="tpu_custom_call" | custom-call | flops 671088640 | bytes 3145728 | tf_op jit(solution)/shard_map/swivel_gradient/pallas_call | solution.py:207
  20.8 0.8 %collective-permute-done.8 = bf16[2,128,256]{2,1,0:T(8,128)(2,1)S(1)} collective-permute-done((bf16[2,128,256]{2,1,0:T(8,128)(2,1)S(1)}, bf16[2,128,256]{2,1,0:T(8,128)(2,1)S(1)}, u32[]{:S(2)}, u32[]{:S(2)}) %collective-permute-start.8) | collective-permute-done | bytes 131104 | tf_op jit(solution)/shard_map/ppermute | solution.py:162
  21.7 1.6 %collective-permute-start.9 = (bf16[1,128,256]{2,1,0:T(8,128)(2,1)S(1)}, bf16[1,128,256]{2,1,0:T(8,128)(2,1)S(1)}, u32[]{:S(2)}, u32[]{:S(2)}) collective-permute-start(bf16[1,128,256]{2,1,0:T(8,128)(2,1)S(1)} %slice.35), channel_id=1, source_target_pairs={{0,2},{2,0},{1,3},{3,1},{4,6},{6,4},{5,7},{7,5},{8,10},{10,8},{9,1... | collective-permute-start | bytes 196616 | tf_op jit(solution)/shard_map/ppermute | solution.py:162
  23.3 0.6 %collective-permute-start.14 = (bf16[1,128,256]{2,1,0:T(8,128)(2,1)S(1)}, bf16[1,128,256]{2,1,0:T(8,128)(2,1)S(1)}, u32[]{:S(2)}, u32[]{:S(2)}) collective-permute-start(bf16[1,128,256]{2,1,0:T(8,128)(2,1)S(1)} %slice.34), channel_id=1, source_target_pairs={{0,2},{2,0},{1,3},{3,1},{4,6},{6,4},{5,7},{7,5},{8,10},{10,8},{9,1... | collective-permute-start | bytes 196616 | tf_op jit(solution)/shard_map/ppermute | solution.py:162
  23.9 2.4 %collective-permute-done.9 = bf16[1,128,256]{2,1,0:T(8,128)(2,1)S(1)} collective-permute-done((bf16[1,128,256]{2,1,0:T(8,128)(2,1)S(1)}, bf16[1,128,256]{2,1,0:T(8,128)(2,1)S(1)}, u32[]{:S(2)}, u32[]{:S(2)}) %collective-permute-start.9) | collective-permute-done | bytes 65568 | tf_op jit(solution)/shard_map/ppermute | solution.py:162
  26.4 0.8 %collective-permute-start.10 = (bf16[128,256]{1,0:T(8,128)(2,1)S(1)}, bf16[128,256]{1,0:T(8,128)(2,1)S(1)}, u32[]{:S(2)}, u32[]{:S(2)}) collective-permute-start(bf16[128,256]{1,0:T(8,128)(2,1)S(1)} %fusion.2), channel_id=1, source_target_pairs={{0,4},{4,0},{1,5},{5,1},{2,6},{6,2},{3,7},{7,3},{8,12},{12,8},{9,1... | collective-permute-start | bytes 196616 | tf_op jit(solution)/shard_map/ppermute | solution.py:162
  27.7 2.1 %collective-permute-start.15 = (bf16[128,256]{1,0:T(8,128)(2,1)S(1)}, bf16[128,256]{1,0:T(8,128)(2,1)S(1)}, u32[]{:S(2)}, u32[]{:S(2)}) collective-permute-start(bf16[128,256]{1,0:T(8,128)(2,1)S(1)} %fusion.3), channel_id=1, source_target_pairs={{0,16},{8,24},{16,0},{24,8},{1,17},{9,25},{17,1},{25,9},{2,18},{10... | collective-permute-start | bytes 196616 | tf_op jit(solution)/shard_map/ppermute | solution.py:162
  29.8 0.9 %collective-permute-done.10 = bf16[128,256]{1,0:T(8,128)(2,1)S(1)} collective-permute-done((bf16[128,256]{1,0:T(8,128)(2,1)S(1)}, bf16[128,256]{1,0:T(8,128)(2,1)S(1)}, u32[]{:S(2)}, u32[]{:S(2)}) %collective-permute-start.10) | collective-permute-done | bytes 65568 | tf_op jit(solution)/shard_map/ppermute | solution.py:162
  30.8 2.2 %collective-permute-done.15 = bf16[128,256]{1,0:T(8,128)(2,1)S(1)} collective-permute-done((bf16[128,256]{1,0:T(8,128)(2,1)S(1)}, bf16[128,256]{1,0:T(8,128)(2,1)S(1)}, u32[]{:S(2)}, u32[]{:S(2)}) %collective-permute-start.15) | collective-permute-done | bytes 65568 | tf_op jit(solution)/shard_map/ppermute | solution.py:162
  33.0 0.9 %collective-permute-start.16 = (bf16[128,256]{1,0:T(8,128)(2,1)S(1)}, bf16[128,256]{1,0:T(8,128)(2,1)S(1)}, u32[]{:S(2)}, u32[]{:S(2)}) collective-permute-start(bf16[128,256]{1,0:T(8,128)(2,1)S(1)} %add_convert_fusion.1), channel_id=1, source_target_pairs={{0,4},{4,0},{1,5},{5,1},{2,6},{6,2},{3,7},{7,3},{8,12},{12,8},{9,1... | collective-permute-start | bytes 196616 | tf_op jit(solution)/shard_map/ppermute | solution.py:162
  33.9 1.2 %collective-permute-done.11 = bf16[128,256]{1,0:T(8,128)(2,1)S(1)} collective-permute-done((bf16[128,256]{1,0:T(8,128)(2,1)S(1)}, bf16[128,256]{1,0:T(8,128)(2,1)S(1)}, u32[]{:S(2)}, u32[]{:S(2)}) %collective-permute-start.11) | collective-permute-done | bytes 65568 | tf_op jit(solution)/shard_map/ppermute | solution.py:162
  35.1 2.8 %collective-permute-start.12 = (bf16[128,256]{1,0:T(8,128)(2,1)S(1)}, bf16[128,256]{1,0:T(8,128)(2,1)S(1)}, u32[]{:S(2)}, u32[]{:S(2)}) collective-permute-start(bf16[128,256]{1,0:T(8,128)(2,1)S(1)} %add_convert_fusion.2), channel_id=1, source_target_pairs={{0,16},{8,24},{16,0},{24,8},{1,17},{9,25},{17,1},{25,9},{2,18},{10... | collective-permute-start | bytes 196616 | tf_op jit(solution)/shard_map/ppermute | solution.py:162
  37.9 2.5 %collective-permute-done.12 = bf16[128,256]{1,0:T(8,128)(2,1)S(1)} collective-permute-done((bf16[128,256]{1,0:T(8,128)(2,1)S(1)}, bf16[128,256]{1,0:T(8,128)(2,1)S(1)}, u32[]{:S(2)}, u32[]{:S(2)}) %collective-permute-start.12) | collective-permute-done | bytes 65568 | tf_op jit(solution)/shard_map/ppermute | solution.py:162
  40.5 1.7 %collective-permute-done.17 = bf16[128,256]{1,0:T(8,128)(2,1)S(1)} collective-permute-done((bf16[128,256]{1,0:T(8,128)(2,1)S(1)}, bf16[128,256]{1,0:T(8,128)(2,1)S(1)}, u32[]{:S(2)}, u32[]{:S(2)}) %collective-permute-start.17) | collective-permute-done | bytes 65568 | tf_op jit(solution)/shard_map/ppermute | solution.py:162
  42.2 0.7 %maximum_bitcast_fusion = f32[1,256,256]{2,1,0:T(8,128)} fusion(f32[128,256]{1,0:T(8,128)S(1)} %convert_add_fusion.2, f32[128,256]{1,0:T(8,128)S(1)} %convert_add_fusion.3), kind=kLoop, calls=%fused_computation | loop fusion | flops 65536 | bytes 524288 | tf_op jit(solution)/shard_map/broadcast_in_dim | solution.py:233
  (33 shorter events, 3.0 us)
Async XLA Ops:
  0.0 17.5 %copy-start = (s32[1024]{0:T(1024)S(1)}, s32[1024]{0:T(1024)}, u32[]{:S(2)}) copy-start(s32[1024]{0:T(1024)} %param.5) | copy-start | bytes 12292
  0.0 7.2 %collective-permute-start.1 = (f32[32,256]{1,0:T(8,128)}, f32[32,256]{1,0:T(8,128)S(1)}, u32[]{:S(2)}, u32[]{:S(2)}) collective-permute-start(f32[32,256]{1,0:T(8,128)} %bitcast.10), channel_id=1, source_target_pairs={{0,24},{8,16},{16,8},{24,0},{1,25},{9,17},{17,9},{25,1},{2,26},{10... | collective-permute-start | bytes 98312 | tf_op jit(solution)/shard_map/ppermute | solution.py:162
  5.1 5.0 %collective-permute-start = (f32[32,256]{1,0:T(8,128)}, f32[32,256]{1,0:T(8,128)S(1)}, u32[]{:S(2)}, u32[]{:S(2)}) collective-permute-start(f32[32,256]{1,0:T(8,128)} %bitcast.11), channel_id=1, source_target_pairs={{0,16},{8,24},{16,0},{24,8},{1,17},{9,25},{17,1},{25,9},{2,18},{10... | collective-permute-start | bytes 98312 | tf_op jit(solution)/shard_map/ppermute | solution.py:162
  5.1 5.0 %collective-permute-start.2 = (f32[32,256]{1,0:T(8,128)}, f32[32,256]{1,0:T(8,128)S(1)}, u32[]{:S(2)}, u32[]{:S(2)}) collective-permute-start(f32[32,256]{1,0:T(8,128)} %bitcast.12), channel_id=1, source_target_pairs={{0,8},{8,0},{16,24},{24,16},{1,9},{9,1},{17,25},{25,17},{2,10},{10... | collective-permute-start | bytes 98312 | tf_op jit(solution)/shard_map/ppermute | solution.py:162
  10.1 6.4 %collective-permute-start.6 = (bf16[4,32,256]{2,1,0:T(8,128)(2,1)S(1)}, bf16[4,32,256]{2,1,0:T(8,128)(2,1)S(1)}, u32[]{:S(2)}, u32[]{:S(2)}) collective-permute-start(bf16[4,32,256]{2,1,0:T(8,128)(2,1)S(1)} %stack_parts.2.refs_0_), channel_id=1, source_target_pairs={{0,6},{2,4},{4,2},{6,0},{1,7},{3,5},{5,3},{7,1},{8,14},{10,12},{12... | collective-permute-start | bytes 196616 | tf_op jit(solution)/shard_map/ppermute | solution.py:162
  12.6 4.3 %collective-permute-start.5 = (bf16[4,32,256]{2,1,0:T(8,128)(2,1)S(1)}, bf16[4,32,256]{2,1,0:T(8,128)(2,1)S(1)}, u32[]{:S(2)}, u32[]{:S(2)}) collective-permute-start(bf16[4,32,256]{2,1,0:T(8,128)(2,1)S(1)} %stack_parts.2.refs_0_), channel_id=1, source_target_pairs={{0,2},{2,0},{4,6},{6,4},{1,3},{3,1},{5,7},{7,5},{8,10},{10,8},{12,... | collective-permute-start | bytes 196616 | tf_op jit(solution)/shard_map/ppermute | solution.py:162
  13.1 4.3 %collective-permute-start.4 = (bf16[4,32,256]{2,1,0:T(8,128)(2,1)S(1)}, bf16[4,32,256]{2,1,0:T(8,128)(2,1)S(1)}, u32[]{:S(2)}, u32[]{:S(2)}) collective-permute-start(bf16[4,32,256]{2,1,0:T(8,128)(2,1)S(1)} %stack_parts.2.refs_0_), channel_id=1, source_target_pairs={{0,4},{2,6},{4,0},{6,2},{1,5},{3,7},{5,1},{7,3},{8,12},{10,14},{12... | collective-permute-start | bytes 196616 | tf_op jit(solution)/shard_map/ppermute | solution.py:162
  13.6 3.8 %collective-permute-start.3 = (bf16[4,32,256]{2,1,0:T(8,128)(2,1)S(1)}, bf16[4,32,256]{2,1,0:T(8,128)(2,1)S(1)}, u32[]{:S(2)}, u32[]{:S(2)}) collective-permute-start(bf16[4,32,256]{2,1,0:T(8,128)(2,1)S(1)} %stack_parts.2.refs_0_), channel_id=1, source_target_pairs={{0,1},{1,0},{2,3},{3,2},{4,5},{5,4},{6,7},{7,6},{8,9},{9,8},{10,11... | collective-permute-start | bytes 196616 | tf_op jit(solution)/shard_map/ppermute | solution.py:162
  17.4 1.5 %collective-permute-start.7 = (bf16[3,4,32,256]{3,2,1,0:T(8,128)(2,1)S(1)}, bf16[3,4,32,256]{3,2,1,0:T(8,128)(2,1)S(1)}, u32[]{:S(2)}, u32[]{:S(2)}) collective-permute-start(bf16[3,4,32,256]{3,2,1,0:T(8,128)(2,1)S(1)} %stack_parts.3), channel_id=1, source_target_pairs={{0,1},{1,0},{2,3},{3,2},{4,5},{5,4},{6,7},{7,6},{8,9},{9,8},{10,11... | collective-permute-start | bytes 589832 | tf_op jit(solution)/shard_map/ppermute | solution.py:162
  20.3 1.4 %collective-permute-start.8 = (bf16[2,128,256]{2,1,0:T(8,128)(2,1)S(1)}, bf16[2,128,256]{2,1,0:T(8,128)(2,1)S(1)}, u32[]{:S(2)}, u32[]{:S(2)}) collective-permute-start(bf16[2,128,256]{2,1,0:T(8,128)(2,1)S(1)} %get-tuple-element.34), channel_id=1, source_target_pairs={{0,1},{1,0},{2,3},{3,2},{4,5},{5,4},{6,7},{7,6},{8,9},{9,8},{10,11... | collective-permute-start | bytes 393224 | tf_op jit(solution)/shard_map/ppermute | solution.py:162
  20.5 2.8 %collective-permute-start.13 = (bf16[2,128,256]{2,1,0:T(8,128)(2,1)S(1)}, bf16[2,128,256]{2,1,0:T(8,128)(2,1)S(1)}, u32[]{:S(2)}, u32[]{:S(2)}) collective-permute-start(bf16[2,128,256]{2,1,0:T(8,128)(2,1)S(1)} %get-tuple-element.36), channel_id=1, source_target_pairs={{0,1},{1,0},{2,3},{3,2},{4,5},{5,4},{6,7},{7,6},{8,9},{9,8},{10,11... | collective-permute-start | bytes 393224 | tf_op jit(solution)/shard_map/ppermute | solution.py:162
  21.7 4.6 %collective-permute-start.9 = (bf16[1,128,256]{2,1,0:T(8,128)(2,1)S(1)}, bf16[1,128,256]{2,1,0:T(8,128)(2,1)S(1)}, u32[]{:S(2)}, u32[]{:S(2)}) collective-permute-start(bf16[1,128,256]{2,1,0:T(8,128)(2,1)S(1)} %slice.35), channel_id=1, source_target_pairs={{0,2},{2,0},{1,3},{3,1},{4,6},{6,4},{5,7},{7,5},{8,10},{10,8},{9,1... | collective-permute-start | bytes 196616 | tf_op jit(solution)/shard_map/ppermute | solution.py:162
  23.3 4.3 %collective-permute-start.14 = (bf16[1,128,256]{2,1,0:T(8,128)(2,1)S(1)}, bf16[1,128,256]{2,1,0:T(8,128)(2,1)S(1)}, u32[]{:S(2)}, u32[]{:S(2)}) collective-permute-start(bf16[1,128,256]{2,1,0:T(8,128)(2,1)S(1)} %slice.34), channel_id=1, source_target_pairs={{0,2},{2,0},{1,3},{3,1},{4,6},{6,4},{5,7},{7,5},{8,10},{10,8},{9,1... | collective-permute-start | bytes 196616 | tf_op jit(solution)/shard_map/ppermute | solution.py:162
  26.4 4.3 %collective-permute-start.10 = (bf16[128,256]{1,0:T(8,128)(2,1)S(1)}, bf16[128,256]{1,0:T(8,128)(2,1)S(1)}, u32[]{:S(2)}, u32[]{:S(2)}) collective-permute-start(bf16[128,256]{1,0:T(8,128)(2,1)S(1)} %fusion.2), channel_id=1, source_target_pairs={{0,4},{4,0},{1,5},{5,1},{2,6},{6,2},{3,7},{7,3},{8,12},{12,8},{9,1... | collective-permute-start | bytes 196616 | tf_op jit(solution)/shard_map/ppermute | solution.py:162
  27.7 5.3 %collective-permute-start.15 = (bf16[128,256]{1,0:T(8,128)(2,1)S(1)}, bf16[128,256]{1,0:T(8,128)(2,1)S(1)}, u32[]{:S(2)}, u32[]{:S(2)}) collective-permute-start(bf16[128,256]{1,0:T(8,128)(2,1)S(1)} %fusion.3), channel_id=1, source_target_pairs={{0,16},{8,24},{16,0},{24,8},{1,17},{9,25},{17,1},{25,9},{2,18},{10... | collective-permute-start | bytes 196616 | tf_op jit(solution)/shard_map/ppermute | solution.py:162
  30.7 4.3 %collective-permute-start.11 = (bf16[128,256]{1,0:T(8,128)(2,1)S(1)}, bf16[128,256]{1,0:T(8,128)(2,1)S(1)}, u32[]{:S(2)}, u32[]{:S(2)}) collective-permute-start(bf16[128,256]{1,0:T(8,128)(2,1)S(1)} %add_convert_fusion.3), channel_id=1, source_target_pairs={{0,8},{8,0},{16,24},{24,16},{1,9},{9,1},{17,25},{25,17},{2,10},{10... | collective-permute-start | bytes 196616 | tf_op jit(solution)/shard_map/ppermute | solution.py:162
  33.0 4.9 %collective-permute-start.16 = (bf16[128,256]{1,0:T(8,128)(2,1)S(1)}, bf16[128,256]{1,0:T(8,128)(2,1)S(1)}, u32[]{:S(2)}, u32[]{:S(2)}) collective-permute-start(bf16[128,256]{1,0:T(8,128)(2,1)S(1)} %add_convert_fusion.1), channel_id=1, source_target_pairs={{0,4},{4,0},{1,5},{5,1},{2,6},{6,2},{3,7},{7,3},{8,12},{12,8},{9,1... | collective-permute-start | bytes 196616 | tf_op jit(solution)/shard_map/ppermute | solution.py:162
  35.1 5.4 %collective-permute-start.12 = (bf16[128,256]{1,0:T(8,128)(2,1)S(1)}, bf16[128,256]{1,0:T(8,128)(2,1)S(1)}, u32[]{:S(2)}, u32[]{:S(2)}) collective-permute-start(bf16[128,256]{1,0:T(8,128)(2,1)S(1)} %add_convert_fusion.2), channel_id=1, source_target_pairs={{0,16},{8,24},{16,0},{24,8},{1,17},{9,25},{17,1},{25,9},{2,18},{10... | collective-permute-start | bytes 196616 | tf_op jit(solution)/shard_map/ppermute | solution.py:162
  37.8 4.3 %collective-permute-start.17 = (bf16[128,256]{1,0:T(8,128)(2,1)S(1)}, bf16[128,256]{1,0:T(8,128)(2,1)S(1)}, u32[]{:S(2)}, u32[]{:S(2)}) collective-permute-start(bf16[128,256]{1,0:T(8,128)(2,1)S(1)} %add_convert_fusion), channel_id=1, source_target_pairs={{0,8},{8,0},{16,24},{24,16},{1,9},{9,1},{17,25},{25,17},{2,10},{10... | collective-permute-start | bytes 196616 | tf_op jit(solution)/shard_map/ppermute | solution.py:162

commit v2 on v1

--- a/solution.py
+++ b/solution.py
@@ -101,7 +101,7 @@
 
 
 def gradient_kernel(groups, marginals_ref, roots_ref, logs_ref, live_ref, tiles_ref, *refs):
-    parts, (last_ref, *out_refs, table, grads, terms) = list(refs[: groups + 1]), refs[groups + 1 :]
+    parts, (last_ref, *out_refs, table, logits, grads, terms) = list(refs[: groups + 1]), refs[groups + 1 :]
     parts += [last_ref.at[j] for j in range(groups - 1)]
     far, chunk, width = parts[0].shape
     blocks, size = groups, grads.shape[0]
@@ -123,15 +123,18 @@
     own_vectors = table[own_rows].astype(jnp.bfloat16)
     own_log = jnp.log(marginals_ref[pl.ds(own, 1), :].astype(jnp.float32)) - log_total
     log_rows = jnp.transpose(jnp.broadcast_to(own_log, (128, size)))
+    for v in range(blocks):
+        vectors = table[v * size : (v + 1) * size].astype(jnp.bfloat16)
+        logits[:, v * size : (v + 1) * size] = lax.dot_general(
+            own_vectors, vectors, NT, preferred_element_type=jnp.float32
+        )
     step = 64
     for v in range(blocks):
-        vectors = table[v * size : (v + 1) * size].astype(jnp.bfloat16)
         visited = LOSS_SCALE * tiles_ref[v : v + 1]
         for first in range(0, size, step):
             rows = slice(first, first + step)
-            logits = lax.dot_general(own_vectors[rows], vectors, NT, preferred_element_type=jnp.float32)
             log_row = jnp.concatenate([log_rows[rows]] * (size // 128), axis=1)
-            margin = logits + log_row + log_marg[v : v + 1]
+            margin = logits[rows, v * size : (v + 1) * size] + log_row + log_marg[v : v + 1]
             live = live_ref[v, rows].astype(jnp.float32)
             weight = (0.25 * LOSS_SCALE) * roots_ref[v, rows] + (0.1 * LOSS_SCALE) * live
             zeros = visited - LOSS_SCALE * live
@@ -213,6 +216,7 @@
         out_specs=[VMEM] * 4,
         scratch_shapes=[
             pltpu.VMEM((blocks * size, width), f32 if column.shape[1] % 16 else bf16),
+            pltpu.VMEM((size, blocks * size), f32),
             pltpu.VMEM((size, blocks * size), bf16),
             pltpu.VMEM((blocks * size, width), f32),
         ],

time: 43.1 us -> 42.9 us (level)
  no operation moved by 1% of the time
where the time goes in v2:
time: 42.9 us; the launch traced here: 42.8 us
  starting transfers between devices  18.7 us (44%)
  waiting for transfers between devices  18.2 us (42%)
  Pallas kernels  4.02 us (9%)
  other arithmetic  1.71 us (4%)
    ppermute x18, starting transfers between devices, swap(): lax.ppermute(value, axes, [(i, i ^ both) for i in range(math.prod(sizes))])  18.7 us
    ppermute x18, waiting for transfers between devices, swap(): lax.ppermute(value, axes, [(i, i ^ both) for i in range(math.prod(sizes))])  18.2 us
    pallas_call x1, Pallas kernels, sum_counts(): pl.pallas_call(functools.partial(count_kernel, tiles), out_shape=[jax.Sha...  2.82 us
    pallas_call x1, Pallas kernels, local(): pl.pallas_call(functools.partial(gradient_kernel, groups), out_shape=[jax...  1.18 us
  transfers between devices with their start and end apart: 18, of which 13 were waited for; matrix products, arithmetic and copies ran while one was open for 2% of the time, Pallas kernels for 7%

profile of v2, /device:TPU:0, one launch (start us, length us, event | category | flops | bytes accessed | tf_op | source)
XLA Modules:
  0.0 42.8 jit_solution(4181707841272073233)
XLA Ops:
  0.0 5.0 %collective-permute-start.1 = (f32[32,256]{1,0:T(8,128)}, f32[32,256]{1,0:T(8,128)S(1)}, u32[]{:S(2)}, u32[]{:S(2)}) collective-permute-start(f32[32,256]{1,0:T(8,128)} %bitcast.10), channel_id=1, source_target_pairs={{0,24},{8,16},{16,8},{24,0},{1,25},{9,17},{17,9},{25,1},{2,26},{10... | collective-permute-start | bytes 98312 | tf_op jit(solution)/shard_map/ppermute | solution.py:165
  5.1 0.6 %collective-permute-start.2 = (f32[32,256]{1,0:T(8,128)}, f32[32,256]{1,0:T(8,128)S(1)}, u32[]{:S(2)}, u32[]{:S(2)}) collective-permute-start(f32[32,256]{1,0:T(8,128)} %bitcast.12), channel_id=1, source_target_pairs={{0,8},{8,0},{16,24},{24,16},{1,9},{9,1},{17,25},{25,17},{2,10},{10... | collective-permute-start | bytes 98312 | tf_op jit(solution)/shard_map/ppermute | solution.py:165
  5.7 0.8 %bitcast_convert_fusion.refs_0_ = bf16[32,256]{1,0:T(8,128)(2,1)S(1)} fusion(f32[1,32,256]{2,1,0:T(8,128)} %param.4), kind=kLoop, calls=%fused_computation.17 | loop fusion | flops 8192 | bytes 49152 | tf_op jit(solution)/shard_map/convert_element_type | solution.py:203
  6.5 0.7 %collective-permute-done.1.refs_2_ = f32[32,256]{1,0:T(8,128)S(1)} collective-permute-done((f32[32,256]{1,0:T(8,128)}, f32[32,256]{1,0:T(8,128)S(1)}, u32[]{:S(2)}, u32[]{:S(2)}) %collective-permute-start.1) | collective-permute-done | bytes 32800 | tf_op jit(solution)/shard_map/ppermute | solution.py:165
  7.2 2.9 %collective-permute-done.refs_1_ = f32[32,256]{1,0:T(8,128)S(1)} collective-permute-done((f32[32,256]{1,0:T(8,128)}, f32[32,256]{1,0:T(8,128)S(1)}, u32[]{:S(2)}, u32[]{:S(2)}) %collective-permute-start) | collective-permute-done | bytes 32800 | tf_op jit(solution)/shard_map/ppermute | solution.py:165
  10.1 2.5 %collective-permute-start.6 = (bf16[4,32,256]{2,1,0:T(8,128)(2,1)S(1)}, bf16[4,32,256]{2,1,0:T(8,128)(2,1)S(1)}, u32[]{:S(2)}, u32[]{:S(2)}) collective-permute-start(bf16[4,32,256]{2,1,0:T(8,128)(2,1)S(1)} %stack_parts.2.refs_0_), channel_id=1, source_target_pairs={{0,6},{2,4},{4,2},{6,0},{1,7},{3,5},{5,3},{7,1},{8,14},{10,12},{12... | collective-permute-start | bytes 196616 | tf_op jit(solution)/shard_map/ppermute | solution.py:165
  13.7 2.8 %sum_counts.1 = (f32[4,256,256]{2,1,0:T(8,128)S(1)}, f32[4,256,256]{2,1,0:T(8,128)S(1)}, bf16[4,256,256]{2,1,0:T(8,128)(2,1)S(1)}, f32[4,256]{1,0:T(4,128)S(1)}) custom-call(s32[1,1,16]{2,1,0:T(1,128)} %visits_ref.1, s32[16,256,256]{2,1,0:T(8,128)} %bitcast.9), custom_call_target="tpu_custom_call" | custom-call | flops 10485760 | bytes 4194304 | tf_op jit(solution)/shard_map/sum_counts/pallas_call | solution.py:61
  16.9 0.5 %collective-permute-done.4.refs_0_.refs_1_ = bf16[4,32,256]{2,1,0:T(8,128)(2,1)S(1)} collective-permute-done((bf16[4,32,256]{2,1,0:T(8,128)(2,1)S(1)}, bf16[4,32,256]{2,1,0:T(8,128)(2,1)S(1)}, u32[]{:S(2)}, u32[]{:S(2)}) %collective-permute-start.4) | collective-permute-done | bytes 65568 | tf_op jit(solution)/shard_map/ppermute | solution.py:165
  17.5 1.4 %collective-permute-done.7.refs_5_ = bf16[3,4,32,256]{3,2,1,0:T(8,128)(2,1)S(1)} collective-permute-done((bf16[3,4,32,256]{3,2,1,0:T(8,128)(2,1)S(1)}, bf16[3,4,32,256]{3,2,1,0:T(8,128)(2,1)S(1)}, u32[]{:S(2)}, u32[]{:S(2)}) %collective-permute-start.7) | collective-permute-done | bytes 196640 | tf_op jit(solution)/shard_map/ppermute | solution.py:165
  18.9 1.2 %swivel_gradient.1 = (f32[2,128,256]{2,1,0:T(8,128)S(1)}, bf16[2,128,256]{2,1,0:T(8,128)(2,1)S(1)}, f32[2,128,256]{2,1,0:T(8,128)S(1)}, bf16[2,128,256]{2,1,0:T(8,128)(2,1)S(1)}) custom-call(s32[4,256]{1,0:T(4,128)S(1)} %reshape.5.marginals_ref, f32[4,256,256]{2,1,0:T(8,128)S(1)} %get-tuple-element.25.roots_ref, ...), custom_call_target="tpu_custom_call" | custom-call | flops 671088640 | bytes 3145728 | tf_op jit(solution)/shard_map/swivel_gradient/pallas_call | solution.py:210
  20.7 0.8 %collective-permute-done.8 = bf16[2,128,256]{2,1,0:T(8,128)(2,1)S(1)} collective-permute-done((bf16[2,128,256]{2,1,0:T(8,128)(2,1)S(1)}, bf16[2,128,256]{2,1,0:T(8,128)(2,1)S(1)}, u32[]{:S(2)}, u32[]{:S(2)}) %collective-permute-start.8) | collective-permute-done | bytes 131104 | tf_op jit(solution)/shard_map/ppermute | solution.py:165
  21.6 1.5 %collective-permute-start.9 = (bf16[1,128,256]{2,1,0:T(8,128)(2,1)S(1)}, bf16[1,128,256]{2,1,0:T(8,128)(2,1)S(1)}, u32[]{:S(2)}, u32[]{:S(2)}) collective-permute-start(bf16[1,128,256]{2,1,0:T(8,128)(2,1)S(1)} %slice.35), channel_id=1, source_target_pairs={{0,2},{2,0},{1,3},{3,1},{4,6},{6,4},{5,7},{7,5},{8,10},{10,8},{9,1... | collective-permute-start | bytes 196616 | tf_op jit(solution)/shard_map/ppermute | solution.py:165
  23.2 0.6 %collective-permute-start.14 = (bf16[1,128,256]{2,1,0:T(8,128)(2,1)S(1)}, bf16[1,128,256]{2,1,0:T(8,128)(2,1)S(1)}, u32[]{:S(2)}, u32[]{:S(2)}) collective-permute-start(bf16[1,128,256]{2,1,0:T(8,128)(2,1)S(1)} %slice.34), channel_id=1, source_target_pairs={{0,2},{2,0},{1,3},{3,1},{4,6},{6,4},{5,7},{7,5},{8,10},{10,8},{9,1... | collective-permute-start | bytes 196616 | tf_op jit(solution)/shard_map/ppermute | solution.py:165
  23.8 2.4 %collective-permute-done.9 = bf16[1,128,256]{2,1,0:T(8,128)(2,1)S(1)} collective-permute-done((bf16[1,128,256]{2,1,0:T(8,128)(2,1)S(1)}, bf16[1,128,256]{2,1,0:T(8,128)(2,1)S(1)}, u32[]{:S(2)}, u32[]{:S(2)}) %collective-permute-start.9) | collective-permute-done | bytes 65568 | tf_op jit(solution)/shard_map/ppermute | solution.py:165
  26.2 0.8 %collective-permute-start.10 = (bf16[128,256]{1,0:T(8,128)(2,1)S(1)}, bf16[128,256]{1,0:T(8,128)(2,1)S(1)}, u32[]{:S(2)}, u32[]{:S(2)}) collective-permute-start(bf16[128,256]{1,0:T(8,128)(2,1)S(1)} %fusion.2), channel_id=1, source_target_pairs={{0,4},{4,0},{1,5},{5,1},{2,6},{6,2},{3,7},{7,3},{8,12},{12,8},{9,1... | collective-permute-start | bytes 196616 | tf_op jit(solution)/shard_map/ppermute | solution.py:165
  27.5 2.1 %collective-permute-start.15 = (bf16[128,256]{1,0:T(8,128)(2,1)S(1)}, bf16[128,256]{1,0:T(8,128)(2,1)S(1)}, u32[]{:S(2)}, u32[]{:S(2)}) collective-permute-start(bf16[128,256]{1,0:T(8,128)(2,1)S(1)} %fusion.3), channel_id=1, source_target_pairs={{0,16},{8,24},{16,0},{24,8},{1,17},{9,25},{17,1},{25,9},{2,18},{10... | collective-permute-start | bytes 196616 | tf_op jit(solution)/shard_map/ppermute | solution.py:165
  29.6 0.9 %collective-permute-done.10 = bf16[128,256]{1,0:T(8,128)(2,1)S(1)} collective-permute-done((bf16[128,256]{1,0:T(8,128)(2,1)S(1)}, bf16[128,256]{1,0:T(8,128)(2,1)S(1)}, u32[]{:S(2)}, u32[]{:S(2)}) %collective-permute-start.10) | collective-permute-done | bytes 65568 | tf_op jit(solution)/shard_map/ppermute | solution.py:165
  30.6 2.2 %collective-permute-done.15 = bf16[128,256]{1,0:T(8,128)(2,1)S(1)} collective-permute-done((bf16[128,256]{1,0:T(8,128)(2,1)S(1)}, bf16[128,256]{1,0:T(8,128)(2,1)S(1)}, u32[]{:S(2)}, u32[]{:S(2)}) %collective-permute-start.15) | collective-permute-done | bytes 65568 | tf_op jit(solution)/shard_map/ppermute | solution.py:165
  32.8 0.9 %collective-permute-start.16 = (bf16[128,256]{1,0:T(8,128)(2,1)S(1)}, bf16[128,256]{1,0:T(8,128)(2,1)S(1)}, u32[]{:S(2)}, u32[]{:S(2)}) collective-permute-start(bf16[128,256]{1,0:T(8,128)(2,1)S(1)} %add_convert_fusion.1), channel_id=1, source_target_pairs={{0,4},{4,0},{1,5},{5,1},{2,6},{6,2},{3,7},{7,3},{8,12},{12,8},{9,1... | collective-permute-start | bytes 196616 | tf_op jit(solution)/shard_map/ppermute | solution.py:165
  33.7 1.2 %collective-permute-done.11 = bf16[128,256]{1,0:T(8,128)(2,1)S(1)} collective-permute-done((bf16[128,256]{1,0:T(8,128)(2,1)S(1)}, bf16[128,256]{1,0:T(8,128)(2,1)S(1)}, u32[]{:S(2)}, u32[]{:S(2)}) %collective-permute-start.11) | collective-permute-done | bytes 65568 | tf_op jit(solution)/shard_map/ppermute | solution.py:165
  34.9 2.8 %collective-permute-start.12 = (bf16[128,256]{1,0:T(8,128)(2,1)S(1)}, bf16[128,256]{1,0:T(8,128)(2,1)S(1)}, u32[]{:S(2)}, u32[]{:S(2)}) collective-permute-start(bf16[128,256]{1,0:T(8,128)(2,1)S(1)} %add_convert_fusion.2), channel_id=1, source_target_pairs={{0,16},{8,24},{16,0},{24,8},{1,17},{9,25},{17,1},{25,9},{2,18},{10... | collective-permute-start | bytes 196616 | tf_op jit(solution)/shard_map/ppermute | solution.py:165
  37.8 2.5 %collective-permute-done.12 = bf16[128,256]{1,0:T(8,128)(2,1)S(1)} collective-permute-done((bf16[128,256]{1,0:T(8,128)(2,1)S(1)}, bf16[128,256]{1,0:T(8,128)(2,1)S(1)}, u32[]{:S(2)}, u32[]{:S(2)}) %collective-permute-start.12) | collective-permute-done | bytes 65568 | tf_op jit(solution)/shard_map/ppermute | solution.py:165
  40.3 1.7 %collective-permute-done.17 = bf16[128,256]{1,0:T(8,128)(2,1)S(1)} collective-permute-done((bf16[128,256]{1,0:T(8,128)(2,1)S(1)}, bf16[128,256]{1,0:T(8,128)(2,1)S(1)}, u32[]{:S(2)}, u32[]{:S(2)}) %collective-permute-start.17) | collective-permute-done | bytes 65568 | tf_op jit(solution)/shard_map/ppermute | solution.py:165
  42.0 0.7 %maximum_bitcast_fusion = f32[1,256,256]{2,1,0:T(8,128)} fusion(f32[128,256]{1,0:T(8,128)S(1)} %convert_add_fusion.2, f32[128,256]{1,0:T(8,128)S(1)} %convert_add_fusion.3), kind=kLoop, calls=%fused_computation | loop fusion | flops 65536 | bytes 524288 | tf_op jit(solution)/shard_map/broadcast_in_dim | solution.py:237
  (33 shorter events, 3.0 us)
Async XLA Ops:
  0.0 17.5 %copy-start = (s32[1024]{0:T(1024)S(1)}, s32[1024]{0:T(1024)}, u32[]{:S(2)}) copy-start(s32[1024]{0:T(1024)} %param.5) | copy-start | bytes 12292
  0.0 7.2 %collective-permute-start.1 = (f32[32,256]{1,0:T(8,128)}, f32[32,256]{1,0:T(8,128)S(1)}, u32[]{:S(2)}, u32[]{:S(2)}) collective-permute-start(f32[32,256]{1,0:T(8,128)} %bitcast.10), channel_id=1, source_target_pairs={{0,24},{8,16},{16,8},{24,0},{1,25},{9,17},{17,9},{25,1},{2,26},{10... | collective-permute-start | bytes 98312 | tf_op jit(solution)/shard_map/ppermute | solution.py:165
  5.1 5.0 %collective-permute-start = (f32[32,256]{1,0:T(8,128)}, f32[32,256]{1,0:T(8,128)S(1)}, u32[]{:S(2)}, u32[]{:S(2)}) collective-permute-start(f32[32,256]{1,0:T(8,128)} %bitcast.11), channel_id=1, source_target_pairs={{0,16},{8,24},{16,0},{24,8},{1,17},{9,25},{17,1},{25,9},{2,18},{10... | collective-permute-start | bytes 98312 | tf_op jit(solution)/shard_map/ppermute | solution.py:165
  5.1 5.0 %collective-permute-start.2 = (f32[32,256]{1,0:T(8,128)}, f32[32,256]{1,0:T(8,128)S(1)}, u32[]{:S(2)}, u32[]{:S(2)}) collective-permute-start(f32[32,256]{1,0:T(8,128)} %bitcast.12), channel_id=1, source_target_pairs={{0,8},{8,0},{16,24},{24,16},{1,9},{9,1},{17,25},{25,17},{2,10},{10... | collective-permute-start | bytes 98312 | tf_op jit(solution)/shard_map/ppermute | solution.py:165
  10.1 6.4 %collective-permute-start.6 = (bf16[4,32,256]{2,1,0:T(8,128)(2,1)S(1)}, bf16[4,32,256]{2,1,0:T(8,128)(2,1)S(1)}, u32[]{:S(2)}, u32[]{:S(2)}) collective-permute-start(bf16[4,32,256]{2,1,0:T(8,128)(2,1)S(1)} %stack_parts.2.refs_0_), channel_id=1, source_target_pairs={{0,6},{2,4},{4,2},{6,0},{1,7},{3,5},{5,3},{7,1},{8,14},{10,12},{12... | collective-permute-start | bytes 196616 | tf_op jit(solution)/shard_map/ppermute | solution.py:165
  12.6 4.3 %collective-permute-start.5 = (bf16[4,32,256]{2,1,0:T(8,128)(2,1)S(1)}, bf16[4,32,256]{2,1,0:T(8,128)(2,1)S(1)}, u32[]{:S(2)}, u32[]{:S(2)}) collective-permute-start(bf16[4,32,256]{2,1,0:T(8,128)(2,1)S(1)} %stack_parts.2.refs_0_), channel_id=1, source_target_pairs={{0,2},{2,0},{4,6},{6,4},{1,3},{3,1},{5,7},{7,5},{8,10},{10,8},{12,... | collective-permute-start | bytes 196616 | tf_op jit(solution)/shard_map/ppermute | solution.py:165
  13.1 4.3 %collective-permute-start.4 = (bf16[4,32,256]{2,1,0:T(8,128)(2,1)S(1)}, bf16[4,32,256]{2,1,0:T(8,128)(2,1)S(1)}, u32[]{:S(2)}, u32[]{:S(2)}) collective-permute-start(bf16[4,32,256]{2,1,0:T(8,128)(2,1)S(1)} %stack_parts.2.refs_0_), channel_id=1, source_target_pairs={{0,4},{2,6},{4,0},{6,2},{1,5},{3,7},{5,1},{7,3},{8,12},{10,14},{12... | collective-permute-start | bytes 196616 | tf_op jit(solution)/shard_map/ppermute | solution.py:165
  13.6 3.8 %collective-permute-start.3 = (bf16[4,32,256]{2,1,0:T(8,128)(2,1)S(1)}, bf16[4,32,256]{2,1,0:T(8,128)(2,1)S(1)}, u32[]{:S(2)}, u32[]{:S(2)}) collective-permute-start(bf16[4,32,256]{2,1,0:T(8,128)(2,1)S(1)} %stack_parts.2.refs_0_), channel_id=1, source_target_pairs={{0,1},{1,0},{2,3},{3,2},{4,5},{5,4},{6,7},{7,6},{8,9},{9,8},{10,11... | collective-permute-start | bytes 196616 | tf_op jit(solution)/shard_map/ppermute | solution.py:165
  17.4 1.5 %collective-permute-start.7 = (bf16[3,4,32,256]{3,2,1,0:T(8,128)(2,1)S(1)}, bf16[3,4,32,256]{3,2,1,0:T(8,128)(2,1)S(1)}, u32[]{:S(2)}, u32[]{:S(2)}) collective-permute-start(bf16[3,4,32,256]{3,2,1,0:T(8,128)(2,1)S(1)} %stack_parts.3), channel_id=1, source_target_pairs={{0,1},{1,0},{2,3},{3,2},{4,5},{5,4},{6,7},{7,6},{8,9},{9,8},{10,11... | collective-permute-start | bytes 589832 | tf_op jit(solution)/shard_map/ppermute | solution.py:165
  20.1 1.4 %collective-permute-start.8 = (bf16[2,128,256]{2,1,0:T(8,128)(2,1)S(1)}, bf16[2,128,256]{2,1,0:T(8,128)(2,1)S(1)}, u32[]{:S(2)}, u32[]{:S(2)}) collective-permute-start(bf16[2,128,256]{2,1,0:T(8,128)(2,1)S(1)} %get-tuple-element.34), channel_id=1, source_target_pairs={{0,1},{1,0},{2,3},{3,2},{4,5},{5,4},{6,7},{7,6},{8,9},{9,8},{10,11... | collective-permute-start | bytes 393224 | tf_op jit(solution)/shard_map/ppermute | solution.py:165
  20.3 2.8 %collective-permute-start.13 = (bf16[2,128,256]{2,1,0:T(8,128)(2,1)S(1)}, bf16[2,128,256]{2,1,0:T(8,128)(2,1)S(1)}, u32[]{:S(2)}, u32[]{:S(2)}) collective-permute-start(bf16[2,128,256]{2,1,0:T(8,128)(2,1)S(1)} %get-tuple-element.36), channel_id=1, source_target_pairs={{0,1},{1,0},{2,3},{3,2},{4,5},{5,4},{6,7},{7,6},{8,9},{9,8},{10,11... | collective-permute-start | bytes 393224 | tf_op jit(solution)/shard_map/ppermute | solution.py:165
  21.6 4.6 %collective-permute-start.9 = (bf16[1,128,256]{2,1,0:T(8,128)(2,1)S(1)}, bf16[1,128,256]{2,1,0:T(8,128)(2,1)S(1)}, u32[]{:S(2)}, u32[]{:S(2)}) collective-permute-start(bf16[1,128,256]{2,1,0:T(8,128)(2,1)S(1)} %slice.35), channel_id=1, source_target_pairs={{0,2},{2,0},{1,3},{3,1},{4,6},{6,4},{5,7},{7,5},{8,10},{10,8},{9,1... | collective-permute-start | bytes 196616 | tf_op jit(solution)/shard_map/ppermute | solution.py:165
  23.2 4.3 %collective-permute-start.14 = (bf16[1,128,256]{2,1,0:T(8,128)(2,1)S(1)}, bf16[1,128,256]{2,1,0:T(8,128)(2,1)S(1)}, u32[]{:S(2)}, u32[]{:S(2)}) collective-permute-start(bf16[1,128,256]{2,1,0:T(8,128)(2,1)S(1)} %slice.34), channel_id=1, source_target_pairs={{0,2},{2,0},{1,3},{3,1},{4,6},{6,4},{5,7},{7,5},{8,10},{10,8},{9,1... | collective-permute-start | bytes 196616 | tf_op jit(solution)/shard_map/ppermute | solution.py:165
  26.2 4.3 %collective-permute-start.10 = (bf16[128,256]{1,0:T(8,128)(2,1)S(1)}, bf16[128,256]{1,0:T(8,128)(2,1)S(1)}, u32[]{:S(2)}, u32[]{:S(2)}) collective-permute-start(bf16[128,256]{1,0:T(8,128)(2,1)S(1)} %fusion.2), channel_id=1, source_target_pairs={{0,4},{4,0},{1,5},{5,1},{2,6},{6,2},{3,7},{7,3},{8,12},{12,8},{9,1... | collective-permute-start | bytes 196616 | tf_op jit(solution)/shard_map/ppermute | solution.py:165
  27.5 5.3 %collective-permute-start.15 = (bf16[128,256]{1,0:T(8,128)(2,1)S(1)}, bf16[128,256]{1,0:T(8,128)(2,1)S(1)}, u32[]{:S(2)}, u32[]{:S(2)}) collective-permute-start(bf16[128,256]{1,0:T(8,128)(2,1)S(1)} %fusion.3), channel_id=1, source_target_pairs={{0,16},{8,24},{16,0},{24,8},{1,17},{9,25},{17,1},{25,9},{2,18},{10... | collective-permute-start | bytes 196616 | tf_op jit(solution)/shard_map/ppermute | solution.py:165
  30.6 4.3 %collective-permute-start.11 = (bf16[128,256]{1,0:T(8,128)(2,1)S(1)}, bf16[128,256]{1,0:T(8,128)(2,1)S(1)}, u32[]{:S(2)}, u32[]{:S(2)}) collective-permute-start(bf16[128,256]{1,0:T(8,128)(2,1)S(1)} %add_convert_fusion.3), channel_id=1, source_target_pairs={{0,8},{8,0},{16,24},{24,16},{1,9},{9,1},{17,25},{25,17},{2,10},{10... | collective-permute-start | bytes 196616 | tf_op jit(solution)/shard_map/ppermute | solution.py:165
  32.8 4.9 %collective-permute-start.16 = (bf16[128,256]{1,0:T(8,128)(2,1)S(1)}, bf16[128,256]{1,0:T(8,128)(2,1)S(1)}, u32[]{:S(2)}, u32[]{:S(2)}) collective-permute-start(bf16[128,256]{1,0:T(8,128)(2,1)S(1)} %add_convert_fusion.1), channel_id=1, source_target_pairs={{0,4},{4,0},{1,5},{5,1},{2,6},{6,2},{3,7},{7,3},{8,12},{12,8},{9,1... | collective-permute-start | bytes 196616 | tf_op jit(solution)/shard_map/ppermute | solution.py:165
  34.9 5.4 %collective-permute-start.12 = (bf16[128,256]{1,0:T(8,128)(2,1)S(1)}, bf16[128,256]{1,0:T(8,128)(2,1)S(1)}, u32[]{:S(2)}, u32[]{:S(2)}) collective-permute-start(bf16[128,256]{1,0:T(8,128)(2,1)S(1)} %add_convert_fusion.2), channel_id=1, source_target_pairs={{0,16},{8,24},{16,0},{24,8},{1,17},{9,25},{17,1},{25,9},{2,18},{10... | collective-permute-start | bytes 196616 | tf_op jit(solution)/shard_map/ppermute | solution.py:165
  37.7 4.3 %collective-permute-start.17 = (bf16[128,256]{1,0:T(8,128)(2,1)S(1)}, bf16[128,256]{1,0:T(8,128)(2,1)S(1)}, u32[]{:S(2)}, u32[]{:S(2)}) collective-permute-start(bf16[128,256]{1,0:T(8,128)(2,1)S(1)} %add_convert_fusion), channel_id=1, source_target_pairs={{0,8},{8,0},{16,24},{24,16},{1,9},{9,1},{17,25},{25,17},{2,10},{10... | collective-permute-start | bytes 196616 | tf_op jit(solution)/shard_map/ppermute | solution.py:165

commit v3 on v2

--- a/solution.py
+++ b/solution.py
@@ -144,16 +144,15 @@
     terms[own_rows] += jnp.dot(
         grads[...], table[...].astype(jnp.bfloat16), preferred_element_type=jnp.float32
     )
-    for j in range(blocks // 2):
-        chip = jnp.bitwise_xor(here, j)
-        first = 0
-        for kept_ref, sent_ref in (out_refs[:2], out_refs[2:]):
-            count = kept_ref.shape[1]
-            stay = pl.multiple_of((2 * chip + core) * size + first, 16)
-            leave = pl.multiple_of((2 * chip + 1 - core) * size + first, 16)
-            kept_ref[j] = terms[pl.ds(stay, count)]
-            sent_ref[j] = terms[pl.ds(leave, count)].astype(jnp.bfloat16)
-            first += count
+    kept_ref, *sent_refs = out_refs
+    half = size // 2
+    for j in range(groups):
+        chip = jnp.bitwise_xor(here, j // 2)
+        first = jnp.bitwise_xor(near, j % 2) * half
+        stay = pl.multiple_of((2 * chip + core) * size + first, half)
+        leave = pl.multiple_of((2 * chip + 1 - core) * size + first, half)
+        kept_ref[j] = terms[pl.ds(stay, half)]
+        sent_refs[j // 2][j % 2] = terms[pl.ds(leave, half)].astype(jnp.bfloat16)
 
 
 def swap(value, axis, bits):
@@ -177,19 +176,6 @@
     return values[0]
 
 
-def reduce_half(kept, sent, steps):
-    bf16, f32 = jnp.bfloat16, jnp.float32
-    total = kept + swap(sent, "core", 1).astype(f32)
-    while total.shape[0] > 1:
-        half = total.shape[0] // 2
-        total = total[:half] + swap(total[half:].astype(bf16), "chip", half).astype(f32)
-    total = total[0]
-    for axis, bit in steps:
-        mine = total.astype(bf16)
-        total = mine.astype(f32) + swap(mine, axis, bit).astype(f32)
-    return total
-
-
 def local(table, marginals, visits, counts):
     chips, far = lax.axis_size("chip"), lax.axis_size("far")
     groups = blocks = 2 * chips
@@ -203,17 +189,16 @@
     column = stack([piece.astype(bf16)] + pieces)
     parts = others(lambda j: swap(column, ("near", "chip"), (j % 2, j // 2)), groups)
     other_column = swap(column, "core", 1)
-    other_column, *parts, sums = lax.optimization_barrier((other_column, *parts, sums))
+    *parts, other_column, sums = lax.optimization_barrier((*parts[::-1], other_column, sums))
+    parts = parts[::-1]
     parts = [column] + parts + [other_column, swap(stack(parts), "core", 1)]
 
-    heights = (size // 2, size // 2)
-    halves = pl.pallas_call(
+    kept, *sent = pl.pallas_call(
         functools.partial(gradient_kernel, groups),
-        out_shape=[
-            jax.ShapeDtypeStruct((chips, rows, width), dtype) for rows in heights for dtype in (f32, bf16)
-        ],
+        out_shape=[jax.ShapeDtypeStruct((groups, size // 2, width), f32)]
+        + [jax.ShapeDtypeStruct((2, size // 2, width), bf16)] * chips,
         in_specs=[VMEM] * (7 + groups),
-        out_specs=[VMEM] * 4,
+        out_specs=[VMEM] * (1 + chips),
         scratch_shapes=[
             pltpu.VMEM((blocks * size, width), f32 if column.shape[1] % 16 else bf16),
             pltpu.VMEM((size, blocks * size), f32),
@@ -229,12 +214,22 @@
         name="swivel_gradient",
     )(marginals.reshape(blocks, size), *sums, *parts)
 
-    steps = [("near", 1)] + [("far", 1 << i) for i in range(far.bit_length() - 1)]
-    orders = (steps, steps[-1:] + steps[:-1])
-    streams = [
-        reduce_half(kept, sent, order) for kept, sent, order in zip(halves[0::2], halves[1::2], orders)
-    ]
-    return jnp.concatenate(streams, axis=0)[None]
+    received = [swap(part, "core", 1) for part in reversed(sent)][::-1]
+    terms = [kept[j] + received[j // 2][j % 2].astype(f32) for j in range(groups)]
+    shares = others(lambda j: swap(terms[j].astype(bf16), ("near", "chip"), (j % 2, j // 2)), groups)
+    total = terms[0]
+    for share in shares:
+        total += share.astype(f32)
+    bit = 1
+    while bit < far:
+        mine = total.astype(bf16)
+        total = mine.astype(f32) + swap(mine, "far", bit).astype(f32)
+        bit *= 2
+    mine = total.astype(bf16)
+    other = swap(mine, "near", 1)
+    first = lax.axis_index("near") == 0
+    both = jnp.stack([jnp.where(first, mine, other), jnp.where(first, other, mine)])
+    return both.reshape(1, size, width).astype(f32)
 
 
 def solution(mesh):

time: 42.9 us -> 44.2 us (1.030)
  waiting for transfers between devices: 18.2 us -> 22.2 us
  starting transfers between devices: 18.7 us -> 16 us
    ppermute x18 -> x16, waiting for transfers between devices: 18.2 us -> 22.2 us  [swap(): lax.ppermute(value, axes, [(i, i ^ both) for i in range(math.prod(sizes))])]
    ppermute x18 -> x16, starting transfers between devices: 18.7 us -> 16 us  [swap(): lax.ppermute(value, axes, [(i, i ^ both) for i in range(math.prod(sizes))])]
    convert_element_type x6 -> x5, other arithmetic: 0.1 us -> 0.86 us  [the longest x1 0.72 us: local(): return both.reshape(1, size, width).astype(f32)]
    broadcast_in_dim x1 -> x0, other arithmetic: 0.72 us -> none  [local(): return jnp.concatenate(streams, axis=0)[None]]
  transfers between devices with their start and end apart: 18 -> 16, of which waited for: 13 -> 13; matrix products, arithmetic and copies ran while one was open for 2% -> 2% of each run, Pallas kernels for 7% -> 6%
where the time goes in v3:
time: 44.2 us; the launch traced here: 44.1 us
  waiting for transfers between devices  22.2 us (50%)
  starting transfers between devices  16 us (36%)
  Pallas kernels  4 us (9%)
  other arithmetic  1.68 us (4%)
    ppermute x16, waiting for transfers between devices, swap(): lax.ppermute(value, axes, [(i, i ^ both) for i in range(math.prod(sizes))])  22.2 us
    ppermute x16, starting transfers between devices, swap(): lax.ppermute(value, axes, [(i, i ^ both) for i in range(math.prod(sizes))])  16 us
    pallas_call x1, Pallas kernels, sum_counts(): pl.pallas_call(functools.partial(count_kernel, tiles), out_shape=[jax.Sha...  2.82 us
    pallas_call x1, Pallas kernels, local(): pl.pallas_call(functools.partial(gradient_kernel, groups), out_shape=[jax...  1.16 us
  transfers between devices with their start and end apart: 16, of which 13 were waited for; matrix products, arithmetic and copies ran while one was open for 2% of the time, Pallas kernels for 6%

profile of v3, /device:TPU:0, one launch (start us, length us, event | category | flops | bytes accessed | tf_op | source)
XLA Modules:
  0.0 44.1 jit_solution(8251274953874872600)
XLA Ops:
  0.0 4.0 %collective-permute-start = (f32[32,256]{1,0:T(8,128)}, f32[32,256]{1,0:T(8,128)S(1)}, u32[]{:S(2)}, u32[]{:S(2)}) collective-permute-start(f32[32,256]{1,0:T(8,128)} %bitcast.27), channel_id=1, source_target_pairs={{0,16},{8,24},{16,0},{24,8},{1,17},{9,25},{17,1},{25,9},{2,18},{10... | collective-permute-start | bytes 98312 | tf_op jit(solution)/shard_map/ppermute | solution.py:164
  4.0 1.3 %collective-permute-start.1 = (f32[32,256]{1,0:T(8,128)}, f32[32,256]{1,0:T(8,128)S(1)}, u32[]{:S(2)}, u32[]{:S(2)}) collective-permute-start(f32[32,256]{1,0:T(8,128)} %bitcast.28), channel_id=1, source_target_pairs={{0,24},{8,16},{16,8},{24,0},{1,25},{9,17},{17,9},{25,1},{2,26},{10... | collective-permute-start | bytes 98312 | tf_op jit(solution)/shard_map/ppermute | solution.py:164
  5.6 0.8 %bitcast_convert_fusion.1.refs_0_ = bf16[32,256]{1,0:T(8,128)(2,1)S(1)} fusion(f32[1,32,256]{2,1,0:T(8,128)} %param.4), kind=kLoop, calls=%fused_computation.16 | loop fusion | flops 8192 | bytes 49152 | tf_op jit(solution)/shard_map/convert_element_type | solution.py:189
  6.5 3.5 %collective-permute-done.1.refs_2_ = f32[32,256]{1,0:T(8,128)S(1)} collective-permute-done((f32[32,256]{1,0:T(8,128)}, f32[32,256]{1,0:T(8,128)S(1)}, u32[]{:S(2)}, u32[]{:S(2)}) %collective-permute-start.1) | collective-permute-done | bytes 32800 | tf_op jit(solution)/shard_map/ppermute | solution.py:164
  10.0 2.5 %collective-permute-start.3 = (bf16[4,32,256]{2,1,0:T(8,128)(2,1)S(1)}, bf16[4,32,256]{2,1,0:T(8,128)(2,1)S(1)}, u32[]{:S(2)}, u32[]{:S(2)}) collective-permute-start(bf16[4,32,256]{2,1,0:T(8,128)(2,1)S(1)} %stack_parts.2.refs_0_), channel_id=1, source_target_pairs={{0,6},{2,4},{4,2},{6,0},{1,7},{3,5},{5,3},{7,1},{8,14},{10,12},{12... | collective-permute-start | bytes 196616 | tf_op jit(solution)/shard_map/ppermute | solution.py:164
  12.5 0.5 %collective-permute-start.4 = (bf16[4,32,256]{2,1,0:T(8,128)(2,1)S(1)}, bf16[4,32,256]{2,1,0:T(8,128)(2,1)S(1)}, u32[]{:S(2)}, u32[]{:S(2)}) collective-permute-start(bf16[4,32,256]{2,1,0:T(8,128)(2,1)S(1)} %stack_parts.2.refs_0_), channel_id=1, source_target_pairs={{0,2},{2,0},{4,6},{6,4},{1,3},{3,1},{5,7},{7,5},{8,10},{10,8},{12,... | collective-permute-start | bytes 196616 | tf_op jit(solution)/shard_map/ppermute | solution.py:164
  13.0 0.5 %collective-permute-start.5 = (bf16[4,32,256]{2,1,0:T(8,128)(2,1)S(1)}, bf16[4,32,256]{2,1,0:T(8,128)(2,1)S(1)}, u32[]{:S(2)}, u32[]{:S(2)}) collective-permute-start(bf16[4,32,256]{2,1,0:T(8,128)(2,1)S(1)} %stack_parts.2.refs_0_), channel_id=1, source_target_pairs={{0,4},{2,6},{4,0},{6,2},{1,5},{3,7},{5,1},{7,3},{8,12},{10,14},{12... | collective-permute-start | bytes 196616 | tf_op jit(solution)/shard_map/ppermute | solution.py:164
  13.5 2.8 %sum_counts.1 = (f32[4,256,256]{2,1,0:T(8,128)S(1)}, f32[4,256,256]{2,1,0:T(8,128)S(1)}, bf16[4,256,256]{2,1,0:T(8,128)(2,1)S(1)}, f32[4,256]{1,0:T(4,128)S(1)}) custom-call(s32[1,1,16]{2,1,0:T(1,128)} %visits_ref.1, s32[16,256,256]{2,1,0:T(8,128)} %bitcast.25), custom_call_target="tpu_custom_call" | custom-call | flops 10485760 | bytes 4194304 | tf_op jit(solution)/shard_map/sum_counts/pallas_call | solution.py:61
  16.8 0.5 %collective-permute-done.5.refs_0_.refs_1_ = bf16[4,32,256]{2,1,0:T(8,128)(2,1)S(1)} collective-permute-done((bf16[4,32,256]{2,1,0:T(8,128)(2,1)S(1)}, bf16[4,32,256]{2,1,0:T(8,128)(2,1)S(1)}, u32[]{:S(2)}, u32[]{:S(2)}) %collective-permute-start.5) | collective-permute-done | bytes 65568 | tf_op jit(solution)/shard_map/ppermute | solution.py:164
  17.4 1.4 %collective-permute-done.7.refs_5_ = bf16[3,4,32,256]{3,2,1,0:T(8,128)(2,1)S(1)} collective-permute-done((bf16[3,4,32,256]{3,2,1,0:T(8,128)(2,1)S(1)}, bf16[3,4,32,256]{3,2,1,0:T(8,128)(2,1)S(1)}, u32[]{:S(2)}, u32[]{:S(2)}) %collective-permute-start.7) | collective-permute-done | bytes 196640 | tf_op jit(solution)/shard_map/ppermute | solution.py:164
  18.8 1.2 %swivel_gradient.1 = (f32[4,128,256]{2,1,0:T(8,128)S(1)}, bf16[2,128,256]{2,1,0:T(8,128)(2,1)S(1)}, bf16[2,128,256]{2,1,0:T(8,128)(2,1)S(1)}) custom-call(s32[4,256]{1,0:T(4,128)S(1)} %reshape.29.marginals_ref, f32[4,256,256]{2,1,0:T(8,128)S(1)} %get-tuple-element.24.roots_ref, f32[4,256,256]{2,1,0:T(8,128)S(1)} %get-tuple-element.25.logs_ref, ...), custom_call_target="tpu_custom_call" | custom-call | flops 671088640 | bytes 3145728 | tf_op jit(solution)/shard_map/swivel_gradient/pallas_call | solution.py:196
  20.6 0.8 %collective-permute-done.10 = bf16[2,128,256]{2,1,0:T(8,128)(2,1)S(1)} collective-permute-done((bf16[2,128,256]{2,1,0:T(8,128)(2,1)S(1)}, bf16[2,128,256]{2,1,0:T(8,128)(2,1)S(1)}, u32[]{:S(2)}, u32[]{:S(2)}) %collective-permute-start.10) | collective-permute-done | bytes 131104 | tf_op jit(solution)/shard_map/ppermute | solution.py:164
  21.6 1.6 %collective-permute-start.11 = (bf16[128,256]{1,0:T(8,128)(2,1)S(1)}, bf16[128,256]{1,0:T(8,128)(2,1)S(1)}, u32[]{:S(2)}, u32[]{:S(2)}) collective-permute-start(bf16[128,256]{1,0:T(8,128)(2,1)S(1)} %get-tuple-element.35), channel_id=1, source_target_pairs={{0,2},{2,0},{4,6},{6,4},{1,3},{3,1},{5,7},{7,5},{8,10},{10,8},{12,... | collective-permute-start | bytes 196616 | tf_op jit(solution)/shard_map/ppermute | solution.py:164
  23.2 0.9 %collective-permute-start.12 = (bf16[128,256]{1,0:T(8,128)(2,1)S(1)}, bf16[128,256]{1,0:T(8,128)(2,1)S(1)}, u32[]{:S(2)}, u32[]{:S(2)}) collective-permute-start(bf16[128,256]{1,0:T(8,128)(2,1)S(1)} %get-tuple-element.36), channel_id=1, source_target_pairs={{0,6},{2,4},{4,2},{6,0},{1,7},{3,5},{5,3},{7,1},{8,14},{10,12},{12... | collective-permute-start | bytes 196616 | tf_op jit(solution)/shard_map/ppermute | solution.py:164
  24.1 1.1 %collective-permute-start.9 = (bf16[128,256]{1,0:T(8,128)(2,1)S(1)}, bf16[128,256]{1,0:T(8,128)(2,1)S(1)}, u32[]{:S(2)}, u32[]{:S(2)}) collective-permute-start(bf16[128,256]{1,0:T(8,128)(2,1)S(1)} %get-tuple-element.37), channel_id=1, source_target_pairs={{0,4},{2,6},{4,0},{6,2},{1,5},{3,7},{5,1},{7,3},{8,12},{10,14},{12... | collective-permute-start | bytes 196616 | tf_op jit(solution)/shard_map/ppermute | solution.py:164
  25.2 0.8 %collective-permute-done.11 = bf16[128,256]{1,0:T(8,128)(2,1)S(1)} collective-permute-done((bf16[128,256]{1,0:T(8,128)(2,1)S(1)}, bf16[128,256]{1,0:T(8,128)(2,1)S(1)}, u32[]{:S(2)}, u32[]{:S(2)}) %collective-permute-start.11) | collective-permute-done | bytes 65568 | tf_op jit(solution)/shard_map/ppermute | solution.py:164
  26.0 2.4 %collective-permute-done.12 = bf16[128,256]{1,0:T(8,128)(2,1)S(1)} collective-permute-done((bf16[128,256]{1,0:T(8,128)(2,1)S(1)}, bf16[128,256]{1,0:T(8,128)(2,1)S(1)}, u32[]{:S(2)}, u32[]{:S(2)}) %collective-permute-start.12) | collective-permute-done | bytes 65568 | tf_op jit(solution)/shard_map/ppermute | solution.py:164
  28.4 0.7 %collective-permute-done.9 = bf16[128,256]{1,0:T(8,128)(2,1)S(1)} collective-permute-done((bf16[128,256]{1,0:T(8,128)(2,1)S(1)}, bf16[128,256]{1,0:T(8,128)(2,1)S(1)}, u32[]{:S(2)}, u32[]{:S(2)}) %collective-permute-start.9) | collective-permute-done | bytes 65568 | tf_op jit(solution)/shard_map/ppermute | solution.py:164
  29.3 4.3 %collective-permute-done.13 = bf16[128,256]{1,0:T(8,128)(2,1)S(1)} collective-permute-done((bf16[128,256]{1,0:T(8,128)(2,1)S(1)}, bf16[128,256]{1,0:T(8,128)(2,1)S(1)}, u32[]{:S(2)}, u32[]{:S(2)}) %collective-permute-start.13) | collective-permute-done | bytes 65568 | tf_op jit(solution)/shard_map/ppermute | solution.py:164
  33.6 1.3 %collective-permute-start.14 = (bf16[128,256]{1,0:T(8,128)(2,1)S(1)}, bf16[128,256]{1,0:T(8,128)(2,1)S(1)}, u32[]{:S(2)}, u32[]{:S(2)}) collective-permute-start(bf16[128,256]{1,0:T(8,128)(2,1)S(1)} %add_convert_fusion.1), channel_id=1, source_target_pairs={{0,16},{8,24},{16,0},{24,8},{1,17},{9,25},{17,1},{25,9},{2,18},{10... | collective-permute-start | bytes 196616 | tf_op jit(solution)/shard_map/ppermute | solution.py:164
  34.9 4.1 %collective-permute-done.14 = bf16[128,256]{1,0:T(8,128)(2,1)S(1)} collective-permute-done((bf16[128,256]{1,0:T(8,128)(2,1)S(1)}, bf16[128,256]{1,0:T(8,128)(2,1)S(1)}, u32[]{:S(2)}, u32[]{:S(2)}) %collective-permute-start.14) | collective-permute-done | bytes 65568 | tf_op jit(solution)/shard_map/ppermute | solution.py:164
  39.0 1.3 %collective-permute-start.15 = (bf16[128,256]{1,0:T(8,128)(2,1)S(1)}, bf16[128,256]{1,0:T(8,128)(2,1)S(1)}, u32[]{:S(2)}, u32[]{:S(2)}) collective-permute-start(bf16[128,256]{1,0:T(8,128)(2,1)S(1)} %add_convert_fusion), channel_id=1, source_target_pairs={{0,4},{4,0},{1,5},{5,1},{2,6},{6,2},{3,7},{7,3},{8,12},{12,8},{9,1... | collective-permute-start | bytes 196616 | tf_op jit(solution)/shard_map/ppermute | solution.py:164
  40.2 3.1 %collective-permute-done.15 = bf16[128,256]{1,0:T(8,128)(2,1)S(1)} collective-permute-done((bf16[128,256]{1,0:T(8,128)(2,1)S(1)}, bf16[128,256]{1,0:T(8,128)(2,1)S(1)}, u32[]{:S(2)}, u32[]{:S(2)}) %collective-permute-start.15) | collective-permute-done | bytes 65568 | tf_op jit(solution)/shard_map/ppermute | solution.py:164
  43.3 0.7 %bitcast_convert_fusion = f32[1,256,256]{2,1,0:T(8,128)} fusion(bf16[1,256,256]{2,1,0:T(8,128)(2,1)S(1)} %bitcast.26), kind=kLoop, calls=%fused_computation.1 | loop fusion | flops 65536 | bytes 393216 | tf_op jit(solution)/shard_map/convert_element_type | solution.py:232
  (23 shorter events, 1.8 us)
Async XLA Ops:
  0.0 17.4 %copy-start = (s32[1024]{0:T(1024)S(1)}, s32[1024]{0:T(1024)}, u32[]{:S(2)}) copy-start(s32[1024]{0:T(1024)} %param.5) | copy-start | bytes 12292
  0.0 6.5 %collective-permute-start = (f32[32,256]{1,0:T(8,128)}, f32[32,256]{1,0:T(8,128)S(1)}, u32[]{:S(2)}, u32[]{:S(2)}) collective-permute-start(f32[32,256]{1,0:T(8,128)} %bitcast.27), channel_id=1, source_target_pairs={{0,16},{8,24},{16,0},{24,8},{1,17},{9,25},{17,1},{25,9},{2,18},{10... | collective-permute-start | bytes 98312 | tf_op jit(solution)/shard_map/ppermute | solution.py:164
  4.0 5.9 %collective-permute-start.1 = (f32[32,256]{1,0:T(8,128)}, f32[32,256]{1,0:T(8,128)S(1)}, u32[]{:S(2)}, u32[]{:S(2)}) collective-permute-start(f32[32,256]{1,0:T(8,128)} %bitcast.28), channel_id=1, source_target_pairs={{0,24},{8,16},{16,8},{24,0},{1,25},{9,17},{17,9},{25,1},{2,26},{10... | collective-permute-start | bytes 98312 | tf_op jit(solution)/shard_map/ppermute | solution.py:164
  5.4 4.6 %collective-permute-start.2 = (f32[32,256]{1,0:T(8,128)}, f32[32,256]{1,0:T(8,128)S(1)}, u32[]{:S(2)}, u32[]{:S(2)}) collective-permute-start(f32[32,256]{1,0:T(8,128)} %bitcast.29), channel_id=1, source_target_pairs={{0,8},{8,0},{16,24},{24,16},{1,9},{9,1},{17,25},{25,17},{2,10},{10... | collective-permute-start | bytes 98312 | tf_op jit(solution)/shard_map/ppermute | solution.py:164
  10.0 6.4 %collective-permute-start.3 = (bf16[4,32,256]{2,1,0:T(8,128)(2,1)S(1)}, bf16[4,32,256]{2,1,0:T(8,128)(2,1)S(1)}, u32[]{:S(2)}, u32[]{:S(2)}) collective-permute-start(bf16[4,32,256]{2,1,0:T(8,128)(2,1)S(1)} %stack_parts.2.refs_0_), channel_id=1, source_target_pairs={{0,6},{2,4},{4,2},{6,0},{1,7},{3,5},{5,3},{7,1},{8,14},{10,12},{12... | collective-permute-start | bytes 196616 | tf_op jit(solution)/shard_map/ppermute | solution.py:164
  12.5 4.3 %collective-permute-start.4 = (bf16[4,32,256]{2,1,0:T(8,128)(2,1)S(1)}, bf16[4,32,256]{2,1,0:T(8,128)(2,1)S(1)}, u32[]{:S(2)}, u32[]{:S(2)}) collective-permute-start(bf16[4,32,256]{2,1,0:T(8,128)(2,1)S(1)} %stack_parts.2.refs_0_), channel_id=1, source_target_pairs={{0,2},{2,0},{4,6},{6,4},{1,3},{3,1},{5,7},{7,5},{8,10},{10,8},{12,... | collective-permute-start | bytes 196616 | tf_op jit(solution)/shard_map/ppermute | solution.py:164
  13.0 4.3 %collective-permute-start.5 = (bf16[4,32,256]{2,1,0:T(8,128)(2,1)S(1)}, bf16[4,32,256]{2,1,0:T(8,128)(2,1)S(1)}, u32[]{:S(2)}, u32[]{:S(2)}) collective-permute-start(bf16[4,32,256]{2,1,0:T(8,128)(2,1)S(1)} %stack_parts.2.refs_0_), channel_id=1, source_target_pairs={{0,4},{2,6},{4,0},{6,2},{1,5},{3,7},{5,1},{7,3},{8,12},{10,14},{12... | collective-permute-start | bytes 196616 | tf_op jit(solution)/shard_map/ppermute | solution.py:164
  13.5 3.8 %collective-permute-start.6 = (bf16[4,32,256]{2,1,0:T(8,128)(2,1)S(1)}, bf16[4,32,256]{2,1,0:T(8,128)(2,1)S(1)}, u32[]{:S(2)}, u32[]{:S(2)}) collective-permute-start(bf16[4,32,256]{2,1,0:T(8,128)(2,1)S(1)} %stack_parts.2.refs_0_), channel_id=1, source_target_pairs={{0,1},{1,0},{2,3},{3,2},{4,5},{5,4},{6,7},{7,6},{8,9},{9,8},{10,11... | collective-permute-start | bytes 196616 | tf_op jit(solution)/shard_map/ppermute | solution.py:164
  17.3 1.5 %collective-permute-start.7 = (bf16[3,4,32,256]{3,2,1,0:T(8,128)(2,1)S(1)}, bf16[3,4,32,256]{3,2,1,0:T(8,128)(2,1)S(1)}, u32[]{:S(2)}, u32[]{:S(2)}) collective-permute-start(bf16[3,4,32,256]{3,2,1,0:T(8,128)(2,1)S(1)} %stack_parts.3), channel_id=1, source_target_pairs={{0,1},{1,0},{2,3},{3,2},{4,5},{5,4},{6,7},{7,6},{8,9},{9,8},{10,11... | collective-permute-start | bytes 589832 | tf_op jit(solution)/shard_map/ppermute | solution.py:164
  20.0 1.4 %collective-permute-start.10 = (bf16[2,128,256]{2,1,0:T(8,128)(2,1)S(1)}, bf16[2,128,256]{2,1,0:T(8,128)(2,1)S(1)}, u32[]{:S(2)}, u32[]{:S(2)}) collective-permute-start(bf16[2,128,256]{2,1,0:T(8,128)(2,1)S(1)} %get-tuple-element.34), channel_id=1, source_target_pairs={{0,1},{1,0},{2,3},{3,2},{4,5},{5,4},{6,7},{7,6},{8,9},{9,8},{10,11... | collective-permute-start | bytes 393224 | tf_op jit(solution)/shard_map/ppermute | solution.py:164
  20.2 1.4 %collective-permute-start.8 = (bf16[2,128,256]{2,1,0:T(8,128)(2,1)S(1)}, bf16[2,128,256]{2,1,0:T(8,128)(2,1)S(1)}, u32[]{:S(2)}, u32[]{:S(2)}) collective-permute-start(bf16[2,128,256]{2,1,0:T(8,128)(2,1)S(1)} %get-tuple-element.33), channel_id=1, source_target_pairs={{0,1},{1,0},{2,3},{3,2},{4,5},{5,4},{6,7},{7,6},{8,9},{9,8},{10,11... | collective-permute-start | bytes 393224 | tf_op jit(solution)/shard_map/ppermute | solution.py:164
  21.6 4.4 %collective-permute-start.11 = (bf16[128,256]{1,0:T(8,128)(2,1)S(1)}, bf16[128,256]{1,0:T(8,128)(2,1)S(1)}, u32[]{:S(2)}, u32[]{:S(2)}) collective-permute-start(bf16[128,256]{1,0:T(8,128)(2,1)S(1)} %get-tuple-element.35), channel_id=1, source_target_pairs={{0,2},{2,0},{4,6},{6,4},{1,3},{3,1},{5,7},{7,5},{8,10},{10,8},{12,... | collective-permute-start | bytes 196616 | tf_op jit(solution)/shard_map/ppermute | solution.py:164
  23.2 5.2 %collective-permute-start.12 = (bf16[128,256]{1,0:T(8,128)(2,1)S(1)}, bf16[128,256]{1,0:T(8,128)(2,1)S(1)}, u32[]{:S(2)}, u32[]{:S(2)}) collective-permute-start(bf16[128,256]{1,0:T(8,128)(2,1)S(1)} %get-tuple-element.36), channel_id=1, source_target_pairs={{0,6},{2,4},{4,2},{6,0},{1,7},{3,5},{5,3},{7,1},{8,14},{10,12},{12... | collective-permute-start | bytes 196616 | tf_op jit(solution)/shard_map/ppermute | solution.py:164
  24.1 5.0 %collective-permute-start.9 = (bf16[128,256]{1,0:T(8,128)(2,1)S(1)}, bf16[128,256]{1,0:T(8,128)(2,1)S(1)}, u32[]{:S(2)}, u32[]{:S(2)}) collective-permute-start(bf16[128,256]{1,0:T(8,128)(2,1)S(1)} %get-tuple-element.37), channel_id=1, source_target_pairs={{0,4},{2,6},{4,0},{6,2},{1,5},{3,7},{5,1},{7,3},{8,12},{10,14},{12... | collective-permute-start | bytes 196616 | tf_op jit(solution)/shard_map/ppermute | solution.py:164
  29.2 4.3 %collective-permute-start.13 = (bf16[128,256]{1,0:T(8,128)(2,1)S(1)}, bf16[128,256]{1,0:T(8,128)(2,1)S(1)}, u32[]{:S(2)}, u32[]{:S(2)}) collective-permute-start(bf16[128,256]{1,0:T(8,128)(2,1)S(1)} %fusion.2), channel_id=1, source_target_pairs={{0,8},{8,0},{16,24},{24,16},{1,9},{9,1},{17,25},{25,17},{2,10},{10... | collective-permute-start | bytes 196616 | tf_op jit(solution)/shard_map/ppermute | solution.py:164
  33.6 5.4 %collective-permute-start.14 = (bf16[128,256]{1,0:T(8,128)(2,1)S(1)}, bf16[128,256]{1,0:T(8,128)(2,1)S(1)}, u32[]{:S(2)}, u32[]{:S(2)}) collective-permute-start(bf16[128,256]{1,0:T(8,128)(2,1)S(1)} %add_convert_fusion.1), channel_id=1, source_target_pairs={{0,16},{8,24},{16,0},{24,8},{1,17},{9,25},{17,1},{25,9},{2,18},{10... | collective-permute-start | bytes 196616 | tf_op jit(solution)/shard_map/ppermute | solution.py:164
  39.0 4.3 %collective-permute-start.15 = (bf16[128,256]{1,0:T(8,128)(2,1)S(1)}, bf16[128,256]{1,0:T(8,128)(2,1)S(1)}, u32[]{:S(2)}, u32[]{:S(2)}) collective-permute-start(bf16[128,256]{1,0:T(8,128)(2,1)S(1)} %add_convert_fusion), channel_id=1, source_target_pairs={{0,4},{4,0},{1,5},{5,1},{2,6},{6,2},{3,7},{7,3},{8,12},{12,8},{9,1... | collective-permute-start | bytes 196616 | tf_op jit(solution)/shard_map/ppermute | solution.py:164

commit v4 on v2

--- a/solution.py
+++ b/solution.py
@@ -203,7 +203,7 @@
     column = stack([piece.astype(bf16)] + pieces)
     parts = others(lambda j: swap(column, ("near", "chip"), (j % 2, j // 2)), groups)
     other_column = swap(column, "core", 1)
-    other_column, *parts, sums = lax.optimization_barrier((other_column, *parts, sums))
+    *parts, other_column, sums = lax.optimization_barrier((*parts, other_column, sums))
     parts = [column] + parts + [other_column, swap(stack(parts), "core", 1)]
 
     heights = (size // 2, size // 2)

time: 42.9 us -> 43 us (level)
  starting transfers between devices: 18.7 us -> 19.3 us
  waiting for transfers between devices: 18.2 us -> 17.6 us
    ppermute x18, starting transfers between devices: 18.7 us -> 19.3 us  [swap(): lax.ppermute(value, axes, [(i, i ^ both) for i in range(math.prod(sizes))])]
    ppermute x18, waiting for transfers between devices: 18.2 us -> 17.6 us  [swap(): lax.ppermute(value, axes, [(i, i ^ both) for i in range(math.prod(sizes))])]
where the time goes in v4:
time: 43 us; the launch traced here: 42.9 us
  starting transfers between devices  19.3 us (45%)
  waiting for transfers between devices  17.6 us (41%)
  Pallas kernels  4.01 us (9%)
  other arithmetic  1.71 us (4%)
    ppermute x18, starting transfers between devices, swap(): lax.ppermute(value, axes, [(i, i ^ both) for i in range(math.prod(sizes))])  19.3 us
    ppermute x18, waiting for transfers between devices, swap(): lax.ppermute(value, axes, [(i, i ^ both) for i in range(math.prod(sizes))])  17.6 us
    pallas_call x1, Pallas kernels, sum_counts(): pl.pallas_call(functools.partial(count_kernel, tiles), out_shape=[jax.Sha...  2.82 us
    pallas_call x1, Pallas kernels, local(): pl.pallas_call(functools.partial(gradient_kernel, groups), out_shape=[jax...  1.17 us
  transfers between devices with their start and end apart: 18, of which 13 were waited for; matrix products, arithmetic and copies ran while one was open for 2% of the time, Pallas kernels for 7%

profile of v4, /device:TPU:0, one launch (start us, length us, event | category | flops | bytes accessed | tf_op | source)
XLA Modules:
  0.0 42.9 jit_solution(14317594880392377440)
XLA Ops:
  0.0 5.0 %collective-permute-start.1 = (f32[32,256]{1,0:T(8,128)}, f32[32,256]{1,0:T(8,128)S(1)}, u32[]{:S(2)}, u32[]{:S(2)}) collective-permute-start(f32[32,256]{1,0:T(8,128)} %bitcast.10), channel_id=1, source_target_pairs={{0,24},{8,16},{16,8},{24,0},{1,25},{9,17},{17,9},{25,1},{2,26},{10... | collective-permute-start | bytes 98312 | tf_op jit(solution)/shard_map/ppermute | solution.py:165
  5.1 0.6 %collective-permute-start.2 = (f32[32,256]{1,0:T(8,128)}, f32[32,256]{1,0:T(8,128)S(1)}, u32[]{:S(2)}, u32[]{:S(2)}) collective-permute-start(f32[32,256]{1,0:T(8,128)} %bitcast.12), channel_id=1, source_target_pairs={{0,8},{8,0},{16,24},{24,16},{1,9},{9,1},{17,25},{25,17},{2,10},{10... | collective-permute-start | bytes 98312 | tf_op jit(solution)/shard_map/ppermute | solution.py:165
  5.7 0.8 %bitcast_convert_fusion.refs_0_ = bf16[32,256]{1,0:T(8,128)(2,1)S(1)} fusion(f32[1,32,256]{2,1,0:T(8,128)} %param.4), kind=kLoop, calls=%fused_computation.17 | loop fusion | flops 8192 | bytes 49152 | tf_op jit(solution)/shard_map/convert_element_type | solution.py:203
  6.5 0.7 %collective-permute-done.1.refs_2_ = f32[32,256]{1,0:T(8,128)S(1)} collective-permute-done((f32[32,256]{1,0:T(8,128)}, f32[32,256]{1,0:T(8,128)S(1)}, u32[]{:S(2)}, u32[]{:S(2)}) %collective-permute-start.1) | collective-permute-done | bytes 32800 | tf_op jit(solution)/shard_map/ppermute | solution.py:165
  7.2 2.9 %collective-permute-done.refs_1_ = f32[32,256]{1,0:T(8,128)S(1)} collective-permute-done((f32[32,256]{1,0:T(8,128)}, f32[32,256]{1,0:T(8,128)S(1)}, u32[]{:S(2)}, u32[]{:S(2)}) %collective-permute-start) | collective-permute-done | bytes 32800 | tf_op jit(solution)/shard_map/ppermute | solution.py:165
  10.2 2.5 %collective-permute-start.5 = (bf16[4,32,256]{2,1,0:T(8,128)(2,1)S(1)}, bf16[4,32,256]{2,1,0:T(8,128)(2,1)S(1)}, u32[]{:S(2)}, u32[]{:S(2)}) collective-permute-start(bf16[4,32,256]{2,1,0:T(8,128)(2,1)S(1)} %stack_parts.2.refs_0_), channel_id=1, source_target_pairs={{0,6},{2,4},{4,2},{6,0},{1,7},{3,5},{5,3},{7,1},{8,14},{10,12},{12... | collective-permute-start | bytes 196616 | tf_op jit(solution)/shard_map/ppermute | solution.py:165
  12.7 0.5 %collective-permute-start.4 = (bf16[4,32,256]{2,1,0:T(8,128)(2,1)S(1)}, bf16[4,32,256]{2,1,0:T(8,128)(2,1)S(1)}, u32[]{:S(2)}, u32[]{:S(2)}) collective-permute-start(bf16[4,32,256]{2,1,0:T(8,128)(2,1)S(1)} %stack_parts.2.refs_0_), channel_id=1, source_target_pairs={{0,2},{2,0},{4,6},{6,4},{1,3},{3,1},{5,7},{7,5},{8,10},{10,8},{12,... | collective-permute-start | bytes 196616 | tf_op jit(solution)/shard_map/ppermute | solution.py:165
  13.7 2.8 %sum_counts.1 = (f32[4,256,256]{2,1,0:T(8,128)S(1)}, f32[4,256,256]{2,1,0:T(8,128)S(1)}, bf16[4,256,256]{2,1,0:T(8,128)(2,1)S(1)}, f32[4,256]{1,0:T(4,128)S(1)}) custom-call(s32[1,1,16]{2,1,0:T(1,128)} %visits_ref.1, s32[16,256,256]{2,1,0:T(8,128)} %bitcast.9), custom_call_target="tpu_custom_call" | custom-call | flops 10485760 | bytes 4194304 | tf_op jit(solution)/shard_map/sum_counts/pallas_call | solution.py:61
  17.6 1.4 %collective-permute-done.7.refs_5_ = bf16[3,4,32,256]{3,2,1,0:T(8,128)(2,1)S(1)} collective-permute-done((bf16[3,4,32,256]{3,2,1,0:T(8,128)(2,1)S(1)}, bf16[3,4,32,256]{3,2,1,0:T(8,128)(2,1)S(1)}, u32[]{:S(2)}, u32[]{:S(2)}) %collective-permute-start.7) | collective-permute-done | bytes 196640 | tf_op jit(solution)/shard_map/ppermute | solution.py:165
  19.0 1.2 %swivel_gradient.1 = (f32[2,128,256]{2,1,0:T(8,128)S(1)}, bf16[2,128,256]{2,1,0:T(8,128)(2,1)S(1)}, f32[2,128,256]{2,1,0:T(8,128)S(1)}, bf16[2,128,256]{2,1,0:T(8,128)(2,1)S(1)}) custom-call(s32[4,256]{1,0:T(4,128)S(1)} %reshape.5.marginals_ref, f32[4,256,256]{2,1,0:T(8,128)S(1)} %get-tuple-element.25.roots_ref, ...), custom_call_target="tpu_custom_call" | custom-call | flops 671088640 | bytes 3145728 | tf_op jit(solution)/shard_map/swivel_gradient/pallas_call | solution.py:210
  20.8 0.8 %collective-permute-done.8 = bf16[2,128,256]{2,1,0:T(8,128)(2,1)S(1)} collective-permute-done((bf16[2,128,256]{2,1,0:T(8,128)(2,1)S(1)}, bf16[2,128,256]{2,1,0:T(8,128)(2,1)S(1)}, u32[]{:S(2)}, u32[]{:S(2)}) %collective-permute-start.8) | collective-permute-done | bytes 131104 | tf_op jit(solution)/shard_map/ppermute | solution.py:165
  21.6 1.6 %collective-permute-start.9 = (bf16[1,128,256]{2,1,0:T(8,128)(2,1)S(1)}, bf16[1,128,256]{2,1,0:T(8,128)(2,1)S(1)}, u32[]{:S(2)}, u32[]{:S(2)}) collective-permute-start(bf16[1,128,256]{2,1,0:T(8,128)(2,1)S(1)} %slice.35), channel_id=1, source_target_pairs={{0,2},{2,0},{1,3},{3,1},{4,6},{6,4},{5,7},{7,5},{8,10},{10,8},{9,1... | collective-permute-start | bytes 196616 | tf_op jit(solution)/shard_map/ppermute | solution.py:165
  23.3 0.6 %collective-permute-start.14 = (bf16[1,128,256]{2,1,0:T(8,128)(2,1)S(1)}, bf16[1,128,256]{2,1,0:T(8,128)(2,1)S(1)}, u32[]{:S(2)}, u32[]{:S(2)}) collective-permute-start(bf16[1,128,256]{2,1,0:T(8,128)(2,1)S(1)} %slice.34), channel_id=1, source_target_pairs={{0,2},{2,0},{1,3},{3,1},{4,6},{6,4},{5,7},{7,5},{8,10},{10,8},{9,1... | collective-permute-start | bytes 196616 | tf_op jit(solution)/shard_map/ppermute | solution.py:165
  23.9 2.4 %collective-permute-done.9 = bf16[1,128,256]{2,1,0:T(8,128)(2,1)S(1)} collective-permute-done((bf16[1,128,256]{2,1,0:T(8,128)(2,1)S(1)}, bf16[1,128,256]{2,1,0:T(8,128)(2,1)S(1)}, u32[]{:S(2)}, u32[]{:S(2)}) %collective-permute-start.9) | collective-permute-done | bytes 65568 | tf_op jit(solution)/shard_map/ppermute | solution.py:165
  26.3 1.1 %collective-permute-start.10 = (bf16[128,256]{1,0:T(8,128)(2,1)S(1)}, bf16[128,256]{1,0:T(8,128)(2,1)S(1)}, u32[]{:S(2)}, u32[]{:S(2)}) collective-permute-start(bf16[128,256]{1,0:T(8,128)(2,1)S(1)} %fusion.2), channel_id=1, source_target_pairs={{0,4},{4,0},{1,5},{5,1},{2,6},{6,2},{3,7},{7,3},{8,12},{12,8},{9,1... | collective-permute-start | bytes 196616 | tf_op jit(solution)/shard_map/ppermute | solution.py:165
  27.6 2.1 %collective-permute-start.15 = (bf16[128,256]{1,0:T(8,128)(2,1)S(1)}, bf16[128,256]{1,0:T(8,128)(2,1)S(1)}, u32[]{:S(2)}, u32[]{:S(2)}) collective-permute-start(bf16[128,256]{1,0:T(8,128)(2,1)S(1)} %fusion.3), channel_id=1, source_target_pairs={{0,16},{8,24},{16,0},{24,8},{1,17},{9,25},{17,1},{25,9},{2,18},{10... | collective-permute-start | bytes 196616 | tf_op jit(solution)/shard_map/ppermute | solution.py:165
  29.7 0.9 %collective-permute-done.10 = bf16[128,256]{1,0:T(8,128)(2,1)S(1)} collective-permute-done((bf16[128,256]{1,0:T(8,128)(2,1)S(1)}, bf16[128,256]{1,0:T(8,128)(2,1)S(1)}, u32[]{:S(2)}, u32[]{:S(2)}) %collective-permute-start.10) | collective-permute-done | bytes 65568 | tf_op jit(solution)/shard_map/ppermute | solution.py:165
  30.7 2.2 %collective-permute-done.15 = bf16[128,256]{1,0:T(8,128)(2,1)S(1)} collective-permute-done((bf16[128,256]{1,0:T(8,128)(2,1)S(1)}, bf16[128,256]{1,0:T(8,128)(2,1)S(1)}, u32[]{:S(2)}, u32[]{:S(2)}) %collective-permute-start.15) | collective-permute-done | bytes 65568 | tf_op jit(solution)/shard_map/ppermute | solution.py:165
  32.9 1.1 %collective-permute-start.16 = (bf16[128,256]{1,0:T(8,128)(2,1)S(1)}, bf16[128,256]{1,0:T(8,128)(2,1)S(1)}, u32[]{:S(2)}, u32[]{:S(2)}) collective-permute-start(bf16[128,256]{1,0:T(8,128)(2,1)S(1)} %add_convert_fusion.1), channel_id=1, source_target_pairs={{0,4},{4,0},{1,5},{5,1},{2,6},{6,2},{3,7},{7,3},{8,12},{12,8},{9,1... | collective-permute-start | bytes 196616 | tf_op jit(solution)/shard_map/ppermute | solution.py:165
  34.0 1.0 %collective-permute-done.11 = bf16[128,256]{1,0:T(8,128)(2,1)S(1)} collective-permute-done((bf16[128,256]{1,0:T(8,128)(2,1)S(1)}, bf16[128,256]{1,0:T(8,128)(2,1)S(1)}, u32[]{:S(2)}, u32[]{:S(2)}) %collective-permute-start.11) | collective-permute-done | bytes 65568 | tf_op jit(solution)/shard_map/ppermute | solution.py:165
  35.0 2.8 %collective-permute-start.12 = (bf16[128,256]{1,0:T(8,128)(2,1)S(1)}, bf16[128,256]{1,0:T(8,128)(2,1)S(1)}, u32[]{:S(2)}, u32[]{:S(2)}) collective-permute-start(bf16[128,256]{1,0:T(8,128)(2,1)S(1)} %add_convert_fusion.2), channel_id=1, source_target_pairs={{0,16},{8,24},{16,0},{24,8},{1,17},{9,25},{17,1},{25,9},{2,18},{10... | collective-permute-start | bytes 196616 | tf_op jit(solution)/shard_map/ppermute | solution.py:165
  37.9 2.5 %collective-permute-done.12 = bf16[128,256]{1,0:T(8,128)(2,1)S(1)} collective-permute-done((bf16[128,256]{1,0:T(8,128)(2,1)S(1)}, bf16[128,256]{1,0:T(8,128)(2,1)S(1)}, u32[]{:S(2)}, u32[]{:S(2)}) %collective-permute-start.12) | collective-permute-done | bytes 65568 | tf_op jit(solution)/shard_map/ppermute | solution.py:165
  40.4 1.8 %collective-permute-done.17 = bf16[128,256]{1,0:T(8,128)(2,1)S(1)} collective-permute-done((bf16[128,256]{1,0:T(8,128)(2,1)S(1)}, bf16[128,256]{1,0:T(8,128)(2,1)S(1)}, u32[]{:S(2)}, u32[]{:S(2)}) %collective-permute-start.17) | collective-permute-done | bytes 65568 | tf_op jit(solution)/shard_map/ppermute | solution.py:165
  42.1 0.7 %maximum_bitcast_fusion = f32[1,256,256]{2,1,0:T(8,128)} fusion(f32[128,256]{1,0:T(8,128)S(1)} %convert_add_fusion.2, f32[128,256]{1,0:T(8,128)S(1)} %convert_add_fusion.3), kind=kLoop, calls=%fused_computation | loop fusion | flops 65536 | bytes 524288 | tf_op jit(solution)/shard_map/broadcast_in_dim | solution.py:237
  (33 shorter events, 2.7 us)
Async XLA Ops:
  0.0 17.6 %copy-start = (s32[1024]{0:T(1024)S(1)}, s32[1024]{0:T(1024)}, u32[]{:S(2)}) copy-start(s32[1024]{0:T(1024)} %param.5) | copy-start | bytes 12292
  0.0 7.2 %collective-permute-start.1 = (f32[32,256]{1,0:T(8,128)}, f32[32,256]{1,0:T(8,128)S(1)}, u32[]{:S(2)}, u32[]{:S(2)}) collective-permute-start(f32[32,256]{1,0:T(8,128)} %bitcast.10), channel_id=1, source_target_pairs={{0,24},{8,16},{16,8},{24,0},{1,25},{9,17},{17,9},{25,1},{2,26},{10... | collective-permute-start | bytes 98312 | tf_op jit(solution)/shard_map/ppermute | solution.py:165
  5.1 5.0 %collective-permute-start = (f32[32,256]{1,0:T(8,128)}, f32[32,256]{1,0:T(8,128)S(1)}, u32[]{:S(2)}, u32[]{:S(2)}) collective-permute-start(f32[32,256]{1,0:T(8,128)} %bitcast.11), channel_id=1, source_target_pairs={{0,16},{8,24},{16,0},{24,8},{1,17},{9,25},{17,1},{25,9},{2,18},{10... | collective-permute-start | bytes 98312 | tf_op jit(solution)/shard_map/ppermute | solution.py:165
  5.1 5.0 %collective-permute-start.2 = (f32[32,256]{1,0:T(8,128)}, f32[32,256]{1,0:T(8,128)S(1)}, u32[]{:S(2)}, u32[]{:S(2)}) collective-permute-start(f32[32,256]{1,0:T(8,128)} %bitcast.12), channel_id=1, source_target_pairs={{0,8},{8,0},{16,24},{24,16},{1,9},{9,1},{17,25},{25,17},{2,10},{10... | collective-permute-start | bytes 98312 | tf_op jit(solution)/shard_map/ppermute | solution.py:165
  10.1 6.5 %collective-permute-start.6 = (bf16[4,32,256]{2,1,0:T(8,128)(2,1)S(1)}, bf16[4,32,256]{2,1,0:T(8,128)(2,1)S(1)}, u32[]{:S(2)}, u32[]{:S(2)}) collective-permute-start(bf16[4,32,256]{2,1,0:T(8,128)(2,1)S(1)} %stack_parts.2.refs_0_), channel_id=1, source_target_pairs={{0,1},{1,0},{2,3},{3,2},{4,5},{5,4},{6,7},{7,6},{8,9},{9,8},{10,11... | collective-permute-start | bytes 196616 | tf_op jit(solution)/shard_map/ppermute | solution.py:165
  10.2 6.4 %collective-permute-start.5 = (bf16[4,32,256]{2,1,0:T(8,128)(2,1)S(1)}, bf16[4,32,256]{2,1,0:T(8,128)(2,1)S(1)}, u32[]{:S(2)}, u32[]{:S(2)}) collective-permute-start(bf16[4,32,256]{2,1,0:T(8,128)(2,1)S(1)} %stack_parts.2.refs_0_), channel_id=1, source_target_pairs={{0,6},{2,4},{4,2},{6,0},{1,7},{3,5},{5,3},{7,1},{8,14},{10,12},{12... | collective-permute-start | bytes 196616 | tf_op jit(solution)/shard_map/ppermute | solution.py:165
  12.7 4.4 %collective-permute-start.4 = (bf16[4,32,256]{2,1,0:T(8,128)(2,1)S(1)}, bf16[4,32,256]{2,1,0:T(8,128)(2,1)S(1)}, u32[]{:S(2)}, u32[]{:S(2)}) collective-permute-start(bf16[4,32,256]{2,1,0:T(8,128)(2,1)S(1)} %stack_parts.2.refs_0_), channel_id=1, source_target_pairs={{0,2},{2,0},{4,6},{6,4},{1,3},{3,1},{5,7},{7,5},{8,10},{10,8},{12,... | collective-permute-start | bytes 196616 | tf_op jit(solution)/shard_map/ppermute | solution.py:165
  13.2 4.3 %collective-permute-start.3 = (bf16[4,32,256]{2,1,0:T(8,128)(2,1)S(1)}, bf16[4,32,256]{2,1,0:T(8,128)(2,1)S(1)}, u32[]{:S(2)}, u32[]{:S(2)}) collective-permute-start(bf16[4,32,256]{2,1,0:T(8,128)(2,1)S(1)} %stack_parts.2.refs_0_), channel_id=1, source_target_pairs={{0,4},{2,6},{4,0},{6,2},{1,5},{3,7},{5,1},{7,3},{8,12},{10,14},{12... | collective-permute-start | bytes 196616 | tf_op jit(solution)/shard_map/ppermute | solution.py:165
  17.5 1.5 %collective-permute-start.7 = (bf16[3,4,32,256]{3,2,1,0:T(8,128)(2,1)S(1)}, bf16[3,4,32,256]{3,2,1,0:T(8,128)(2,1)S(1)}, u32[]{:S(2)}, u32[]{:S(2)}) collective-permute-start(bf16[3,4,32,256]{3,2,1,0:T(8,128)(2,1)S(1)} %stack_parts.3), channel_id=1, source_target_pairs={{0,1},{1,0},{2,3},{3,2},{4,5},{5,4},{6,7},{7,6},{8,9},{9,8},{10,11... | collective-permute-start | bytes 589832 | tf_op jit(solution)/shard_map/ppermute | solution.py:165
  20.2 1.4 %collective-permute-start.8 = (bf16[2,128,256]{2,1,0:T(8,128)(2,1)S(1)}, bf16[2,128,256]{2,1,0:T(8,128)(2,1)S(1)}, u32[]{:S(2)}, u32[]{:S(2)}) collective-permute-start(bf16[2,128,256]{2,1,0:T(8,128)(2,1)S(1)} %get-tuple-element.34), channel_id=1, source_target_pairs={{0,1},{1,0},{2,3},{3,2},{4,5},{5,4},{6,7},{7,6},{8,9},{9,8},{10,11... | collective-permute-start | bytes 393224 | tf_op jit(solution)/shard_map/ppermute | solution.py:165
  20.4 2.8 %collective-permute-start.13 = (bf16[2,128,256]{2,1,0:T(8,128)(2,1)S(1)}, bf16[2,128,256]{2,1,0:T(8,128)(2,1)S(1)}, u32[]{:S(2)}, u32[]{:S(2)}) collective-permute-start(bf16[2,128,256]{2,1,0:T(8,128)(2,1)S(1)} %get-tuple-element.36), channel_id=1, source_target_pairs={{0,1},{1,0},{2,3},{3,2},{4,5},{5,4},{6,7},{7,6},{8,9},{9,8},{10,11... | collective-permute-start | bytes 393224 | tf_op jit(solution)/shard_map/ppermute | solution.py:165
  21.6 4.6 %collective-permute-start.9 = (bf16[1,128,256]{2,1,0:T(8,128)(2,1)S(1)}, bf16[1,128,256]{2,1,0:T(8,128)(2,1)S(1)}, u32[]{:S(2)}, u32[]{:S(2)}) collective-permute-start(bf16[1,128,256]{2,1,0:T(8,128)(2,1)S(1)} %slice.35), channel_id=1, source_target_pairs={{0,2},{2,0},{1,3},{3,1},{4,6},{6,4},{5,7},{7,5},{8,10},{10,8},{9,1... | collective-permute-start | bytes 196616 | tf_op jit(solution)/shard_map/ppermute | solution.py:165
  23.3 4.3 %collective-permute-start.14 = (bf16[1,128,256]{2,1,0:T(8,128)(2,1)S(1)}, bf16[1,128,256]{2,1,0:T(8,128)(2,1)S(1)}, u32[]{:S(2)}, u32[]{:S(2)}) collective-permute-start(bf16[1,128,256]{2,1,0:T(8,128)(2,1)S(1)} %slice.34), channel_id=1, source_target_pairs={{0,2},{2,0},{1,3},{3,1},{4,6},{6,4},{5,7},{7,5},{8,10},{10,8},{9,1... | collective-permute-start | bytes 196616 | tf_op jit(solution)/shard_map/ppermute | solution.py:165
  26.3 4.3 %collective-permute-start.10 = (bf16[128,256]{1,0:T(8,128)(2,1)S(1)}, bf16[128,256]{1,0:T(8,128)(2,1)S(1)}, u32[]{:S(2)}, u32[]{:S(2)}) collective-permute-start(bf16[128,256]{1,0:T(8,128)(2,1)S(1)} %fusion.2), channel_id=1, source_target_pairs={{0,4},{4,0},{1,5},{5,1},{2,6},{6,2},{3,7},{7,3},{8,12},{12,8},{9,1... | collective-permute-start | bytes 196616 | tf_op jit(solution)/shard_map/ppermute | solution.py:165
  27.6 5.3 %collective-permute-start.15 = (bf16[128,256]{1,0:T(8,128)(2,1)S(1)}, bf16[128,256]{1,0:T(8,128)(2,1)S(1)}, u32[]{:S(2)}, u32[]{:S(2)}) collective-permute-start(bf16[128,256]{1,0:T(8,128)(2,1)S(1)} %fusion.3), channel_id=1, source_target_pairs={{0,16},{8,24},{16,0},{24,8},{1,17},{9,25},{17,1},{25,9},{2,18},{10... | collective-permute-start | bytes 196616 | tf_op jit(solution)/shard_map/ppermute | solution.py:165
  30.6 4.3 %collective-permute-start.11 = (bf16[128,256]{1,0:T(8,128)(2,1)S(1)}, bf16[128,256]{1,0:T(8,128)(2,1)S(1)}, u32[]{:S(2)}, u32[]{:S(2)}) collective-permute-start(bf16[128,256]{1,0:T(8,128)(2,1)S(1)} %add_convert_fusion.3), channel_id=1, source_target_pairs={{0,8},{8,0},{16,24},{24,16},{1,9},{9,1},{17,25},{25,17},{2,10},{10... | collective-permute-start | bytes 196616 | tf_op jit(solution)/shard_map/ppermute | solution.py:165
  32.9 4.9 %collective-permute-start.16 = (bf16[128,256]{1,0:T(8,128)(2,1)S(1)}, bf16[128,256]{1,0:T(8,128)(2,1)S(1)}, u32[]{:S(2)}, u32[]{:S(2)}) collective-permute-start(bf16[128,256]{1,0:T(8,128)(2,1)S(1)} %add_convert_fusion.1), channel_id=1, source_target_pairs={{0,4},{4,0},{1,5},{5,1},{2,6},{6,2},{3,7},{7,3},{8,12},{12,8},{9,1... | collective-permute-start | bytes 196616 | tf_op jit(solution)/shard_map/ppermute | solution.py:165
  35.0 5.4 %collective-permute-start.12 = (bf16[128,256]{1,0:T(8,128)(2,1)S(1)}, bf16[128,256]{1,0:T(8,128)(2,1)S(1)}, u32[]{:S(2)}, u32[]{:S(2)}) collective-permute-start(bf16[128,256]{1,0:T(8,128)(2,1)S(1)} %add_convert_fusion.2), channel_id=1, source_target_pairs={{0,16},{8,24},{16,0},{24,8},{1,17},{9,25},{17,1},{25,9},{2,18},{10... | collective-permute-start | bytes 196616 | tf_op jit(solution)/shard_map/ppermute | solution.py:165
  37.8 4.3 %collective-permute-start.17 = (bf16[128,256]{1,0:T(8,128)(2,1)S(1)}, bf16[128,256]{1,0:T(8,128)(2,1)S(1)}, u32[]{:S(2)}, u32[]{:S(2)}) collective-permute-start(bf16[128,256]{1,0:T(8,128)(2,1)S(1)} %add_convert_fusion), channel_id=1, source_target_pairs={{0,8},{8,0},{16,24},{24,16},{1,9},{9,1},{17,25},{25,17},{2,10},{10... | collective-permute-start | bytes 196616 | tf_op jit(solution)/shard_map/ppermute | solution.py:165

commit v5 on v2

--- a/solution.py
+++ b/solution.py
@@ -234,7 +234,9 @@
     streams = [
         reduce_half(kept, sent, order) for kept, sent, order in zip(halves[0::2], halves[1::2], orders)
     ]
-    return jnp.concatenate(streams, axis=0)[None]
+    first, second = streams
+    result = lax.optimization_barrier(jnp.pad(first, ((0, second.shape[0]), (0, 0)))[None])
+    return lax.dynamic_update_slice(result, second[None], (0, first.shape[0], 0))
 
 
 def solution(mesh):

time: 42.9 us -> 42.9 us (level)
  local copies, waits for them, and re-layouts: 0.03 us -> 0.75 us
  waiting for transfers between devices: 18.2 us -> 17.5 us
    broadcast_in_dim x1 -> x0, other arithmetic: 0.72 us -> none  [local(): return jnp.concatenate(streams, axis=0)[None]]
    ppermute x18, waiting for transfers between devices: 18.2 us -> 17.5 us  [swap(): lax.ppermute(value, axes, [(i, i ^ both) for i in range(math.prod(sizes))])]
    broadcast_in_dim x0 -> x1, local copies, waits for them, and re-layouts: none -> 0.72 us  [local(): jnp.pad(first, ((0, second.shape[0]), (0, 0)))[None]]
    dynamic_update_slice x0 -> x1, other arithmetic: none -> 0.67 us  [local(): lax.dynamic_update_slice(result, second[None], (0, first.shape[0], 0))]
  transfers between devices with their start and end apart: 18 -> 18, of which waited for: 13 -> 13; matrix products, arithmetic and copies ran while one was open for 2% -> 4% of each run, Pallas kernels for 7% -> 7%
where the time goes in v5:
time: 42.9 us; the launch traced here: 42.7 us
  starting transfers between devices  18.7 us (44%)
  waiting for transfers between devices  17.5 us (41%)
  Pallas kernels  4.02 us (9%)
  other arithmetic  1.64 us (4%)
  local copies, waits for them, and re-layouts  0.75 us (2%)
    ppermute x18, starting transfers between devices, swap(): lax.ppermute(value, axes, [(i, i ^ both) for i in range(math.prod(sizes))])  18.7 us
    ppermute x18, waiting for transfers between devices, swap(): lax.ppermute(value, axes, [(i, i ^ both) for i in range(math.prod(sizes))])  17.5 us
    pallas_call x1, Pallas kernels, sum_counts(): pl.pallas_call(functools.partial(count_kernel, tiles), out_shape=[jax.Sha...  2.82 us
    pallas_call x1, Pallas kernels, local(): pl.pallas_call(functools.partial(gradient_kernel, groups), out_shape=[jax...  1.18 us
  transfers between devices with their start and end apart: 18, of which 13 were waited for; matrix products, arithmetic and copies ran while one was open for 4% of the time, Pallas kernels for 7%

profile of v5, /device:TPU:0, one launch (start us, length us, event | category | flops | bytes accessed | tf_op | source)
XLA Modules:
  0.0 42.7 jit_solution(14545973264736698570)
XLA Ops:
  0.0 5.0 %collective-permute-start.1 = (f32[32,256]{1,0:T(8,128)}, f32[32,256]{1,0:T(8,128)S(1)}, u32[]{:S(2)}, u32[]{:S(2)}) collective-permute-start(f32[32,256]{1,0:T(8,128)} %bitcast.12), channel_id=1, source_target_pairs={{0,24},{8,16},{16,8},{24,0},{1,25},{9,17},{17,9},{25,1},{2,26},{10... | collective-permute-start | bytes 98312 | tf_op jit(solution)/shard_map/ppermute | solution.py:165
  5.1 0.6 %collective-permute-start.2 = (f32[32,256]{1,0:T(8,128)}, f32[32,256]{1,0:T(8,128)S(1)}, u32[]{:S(2)}, u32[]{:S(2)}) collective-permute-start(f32[32,256]{1,0:T(8,128)} %bitcast.14), channel_id=1, source_target_pairs={{0,8},{8,0},{16,24},{24,16},{1,9},{9,1},{17,25},{25,17},{2,10},{10... | collective-permute-start | bytes 98312 | tf_op jit(solution)/shard_map/ppermute | solution.py:165
  5.7 0.8 %bitcast_convert_fusion.refs_0_ = bf16[32,256]{1,0:T(8,128)(2,1)S(1)} fusion(f32[1,32,256]{2,1,0:T(8,128)} %param.4), kind=kLoop, calls=%fused_computation.17 | loop fusion | flops 8192 | bytes 49152 | tf_op jit(solution)/shard_map/convert_element_type | solution.py:203
  6.5 0.7 %collective-permute-done.1.refs_2_ = f32[32,256]{1,0:T(8,128)S(1)} collective-permute-done((f32[32,256]{1,0:T(8,128)}, f32[32,256]{1,0:T(8,128)S(1)}, u32[]{:S(2)}, u32[]{:S(2)}) %collective-permute-start.1) | collective-permute-done | bytes 32800 | tf_op jit(solution)/shard_map/ppermute | solution.py:165
  7.2 2.9 %collective-permute-done.refs_1_ = f32[32,256]{1,0:T(8,128)S(1)} collective-permute-done((f32[32,256]{1,0:T(8,128)}, f32[32,256]{1,0:T(8,128)S(1)}, u32[]{:S(2)}, u32[]{:S(2)}) %collective-permute-start) | collective-permute-done | bytes 32800 | tf_op jit(solution)/shard_map/ppermute | solution.py:165
  10.1 2.5 %collective-permute-start.6 = (bf16[4,32,256]{2,1,0:T(8,128)(2,1)S(1)}, bf16[4,32,256]{2,1,0:T(8,128)(2,1)S(1)}, u32[]{:S(2)}, u32[]{:S(2)}) collective-permute-start(bf16[4,32,256]{2,1,0:T(8,128)(2,1)S(1)} %stack_parts.2.refs_0_), channel_id=1, source_target_pairs={{0,6},{2,4},{4,2},{6,0},{1,7},{3,5},{5,3},{7,1},{8,14},{10,12},{12... | collective-permute-start | bytes 196616 | tf_op jit(solution)/shard_map/ppermute | solution.py:165
  13.7 2.8 %sum_counts.1 = (f32[4,256,256]{2,1,0:T(8,128)S(1)}, f32[4,256,256]{2,1,0:T(8,128)S(1)}, bf16[4,256,256]{2,1,0:T(8,128)(2,1)S(1)}, f32[4,256]{1,0:T(4,128)S(1)}) custom-call(s32[1,1,16]{2,1,0:T(1,128)} %visits_ref.1, s32[16,256,256]{2,1,0:T(8,128)} %bitcast.11), custom_call_target="tpu_custom_call" | custom-call | flops 10485760 | bytes 4194304 | tf_op jit(solution)/shard_map/sum_counts/pallas_call | solution.py:61
  17.5 1.4 %collective-permute-done.7.refs_5_ = bf16[3,4,32,256]{3,2,1,0:T(8,128)(2,1)S(1)} collective-permute-done((bf16[3,4,32,256]{3,2,1,0:T(8,128)(2,1)S(1)}, bf16[3,4,32,256]{3,2,1,0:T(8,128)(2,1)S(1)}, u32[]{:S(2)}, u32[]{:S(2)}) %collective-permute-start.7) | collective-permute-done | bytes 196640 | tf_op jit(solution)/shard_map/ppermute | solution.py:165
  18.9 1.2 %swivel_gradient.1 = (f32[2,128,256]{2,1,0:T(8,128)S(1)}, bf16[2,128,256]{2,1,0:T(8,128)(2,1)S(1)}, f32[2,128,256]{2,1,0:T(8,128)S(1)}, bf16[2,128,256]{2,1,0:T(8,128)(2,1)S(1)}) custom-call(s32[4,256]{1,0:T(4,128)S(1)} %reshape.5.marginals_ref, f32[4,256,256]{2,1,0:T(8,128)S(1)} %get-tuple-element.25.roots_ref, ...), custom_call_target="tpu_custom_call" | custom-call | flops 671088640 | bytes 3145728 | tf_op jit(solution)/shard_map/swivel_gradient/pallas_call | solution.py:210
  20.7 0.8 %collective-permute-done.8 = bf16[2,128,256]{2,1,0:T(8,128)(2,1)S(1)} collective-permute-done((bf16[2,128,256]{2,1,0:T(8,128)(2,1)S(1)}, bf16[2,128,256]{2,1,0:T(8,128)(2,1)S(1)}, u32[]{:S(2)}, u32[]{:S(2)}) %collective-permute-start.8) | collective-permute-done | bytes 131104 | tf_op jit(solution)/shard_map/ppermute | solution.py:165
  21.6 1.5 %collective-permute-start.9 = (bf16[1,128,256]{2,1,0:T(8,128)(2,1)S(1)}, bf16[1,128,256]{2,1,0:T(8,128)(2,1)S(1)}, u32[]{:S(2)}, u32[]{:S(2)}) collective-permute-start(bf16[1,128,256]{2,1,0:T(8,128)(2,1)S(1)} %slice.35), channel_id=1, source_target_pairs={{0,2},{2,0},{1,3},{3,1},{4,6},{6,4},{5,7},{7,5},{8,10},{10,8},{9,1... | collective-permute-start | bytes 196616 | tf_op jit(solution)/shard_map/ppermute | solution.py:165
  23.2 0.6 %collective-permute-start.14 = (bf16[1,128,256]{2,1,0:T(8,128)(2,1)S(1)}, bf16[1,128,256]{2,1,0:T(8,128)(2,1)S(1)}, u32[]{:S(2)}, u32[]{:S(2)}) collective-permute-start(bf16[1,128,256]{2,1,0:T(8,128)(2,1)S(1)} %slice.34), channel_id=1, source_target_pairs={{0,2},{2,0},{1,3},{3,1},{4,6},{6,4},{5,7},{7,5},{8,10},{10,8},{9,1... | collective-permute-start | bytes 196616 | tf_op jit(solution)/shard_map/ppermute | solution.py:165
  23.8 2.4 %collective-permute-done.9 = bf16[1,128,256]{2,1,0:T(8,128)(2,1)S(1)} collective-permute-done((bf16[1,128,256]{2,1,0:T(8,128)(2,1)S(1)}, bf16[1,128,256]{2,1,0:T(8,128)(2,1)S(1)}, u32[]{:S(2)}, u32[]{:S(2)}) %collective-permute-start.9) | collective-permute-done | bytes 65568 | tf_op jit(solution)/shard_map/ppermute | solution.py:165
  26.2 0.8 %collective-permute-start.10 = (bf16[128,256]{1,0:T(8,128)(2,1)S(1)}, bf16[128,256]{1,0:T(8,128)(2,1)S(1)}, u32[]{:S(2)}, u32[]{:S(2)}) collective-permute-start(bf16[128,256]{1,0:T(8,128)(2,1)S(1)} %fusion.2), channel_id=1, source_target_pairs={{0,4},{4,0},{1,5},{5,1},{2,6},{6,2},{3,7},{7,3},{8,12},{12,8},{9,1... | collective-permute-start | bytes 196616 | tf_op jit(solution)/shard_map/ppermute | solution.py:165
  27.5 2.1 %collective-permute-start.15 = (bf16[128,256]{1,0:T(8,128)(2,1)S(1)}, bf16[128,256]{1,0:T(8,128)(2,1)S(1)}, u32[]{:S(2)}, u32[]{:S(2)}) collective-permute-start(bf16[128,256]{1,0:T(8,128)(2,1)S(1)} %fusion.3), channel_id=1, source_target_pairs={{0,16},{8,24},{16,0},{24,8},{1,17},{9,25},{17,1},{25,9},{2,18},{10... | collective-permute-start | bytes 196616 | tf_op jit(solution)/shard_map/ppermute | solution.py:165
  29.6 0.9 %collective-permute-done.10 = bf16[128,256]{1,0:T(8,128)(2,1)S(1)} collective-permute-done((bf16[128,256]{1,0:T(8,128)(2,1)S(1)}, bf16[128,256]{1,0:T(8,128)(2,1)S(1)}, u32[]{:S(2)}, u32[]{:S(2)}) %collective-permute-start.10) | collective-permute-done | bytes 65568 | tf_op jit(solution)/shard_map/ppermute | solution.py:165
  30.6 2.2 %collective-permute-done.15 = bf16[128,256]{1,0:T(8,128)(2,1)S(1)} collective-permute-done((bf16[128,256]{1,0:T(8,128)(2,1)S(1)}, bf16[128,256]{1,0:T(8,128)(2,1)S(1)}, u32[]{:S(2)}, u32[]{:S(2)}) %collective-permute-start.15) | collective-permute-done | bytes 65568 | tf_op jit(solution)/shard_map/ppermute | solution.py:165
  32.8 0.9 %collective-permute-start.16 = (bf16[128,256]{1,0:T(8,128)(2,1)S(1)}, bf16[128,256]{1,0:T(8,128)(2,1)S(1)}, u32[]{:S(2)}, u32[]{:S(2)}) collective-permute-start(bf16[128,256]{1,0:T(8,128)(2,1)S(1)} %add_convert_fusion.1), channel_id=1, source_target_pairs={{0,4},{4,0},{1,5},{5,1},{2,6},{6,2},{3,7},{7,3},{8,12},{12,8},{9,1... | collective-permute-start | bytes 196616 | tf_op jit(solution)/shard_map/ppermute | solution.py:165
  33.7 1.2 %collective-permute-done.11 = bf16[128,256]{1,0:T(8,128)(2,1)S(1)} collective-permute-done((bf16[128,256]{1,0:T(8,128)(2,1)S(1)}, bf16[128,256]{1,0:T(8,128)(2,1)S(1)}, u32[]{:S(2)}, u32[]{:S(2)}) %collective-permute-start.11) | collective-permute-done | bytes 65568 | tf_op jit(solution)/shard_map/ppermute | solution.py:165
  34.9 2.8 %collective-permute-start.12 = (bf16[128,256]{1,0:T(8,128)(2,1)S(1)}, bf16[128,256]{1,0:T(8,128)(2,1)S(1)}, u32[]{:S(2)}, u32[]{:S(2)}) collective-permute-start(bf16[128,256]{1,0:T(8,128)(2,1)S(1)} %add_convert_fusion.2), channel_id=1, source_target_pairs={{0,16},{8,24},{16,0},{24,8},{1,17},{9,25},{17,1},{25,9},{2,18},{10... | collective-permute-start | bytes 196616 | tf_op jit(solution)/shard_map/ppermute | solution.py:165
  37.8 2.5 %collective-permute-done.12 = bf16[128,256]{1,0:T(8,128)(2,1)S(1)} collective-permute-done((bf16[128,256]{1,0:T(8,128)(2,1)S(1)}, bf16[128,256]{1,0:T(8,128)(2,1)S(1)}, u32[]{:S(2)}, u32[]{:S(2)}) %collective-permute-start.12) | collective-permute-done | bytes 65568 | tf_op jit(solution)/shard_map/ppermute | solution.py:165
  40.3 0.7 %pad_bitcast_fusion = f32[1,256,256]{2,1,0:T(8,128)} fusion(f32[128,256]{1,0:T(8,128)S(1)} %convert_add_fusion.2), kind=kLoop, calls=%fused_computation.1 | loop fusion | bytes 393216 | tf_op jit(solution)/shard_map/broadcast_in_dim | solution.py:238
  41.0 1.0 %collective-permute-done.17 = bf16[128,256]{1,0:T(8,128)(2,1)S(1)} collective-permute-done((bf16[128,256]{1,0:T(8,128)(2,1)S(1)}, bf16[128,256]{1,0:T(8,128)(2,1)S(1)}, u32[]{:S(2)}, u32[]{:S(2)}) %collective-permute-start.17) | collective-permute-done | bytes 65568 | tf_op jit(solution)/shard_map/ppermute | solution.py:165
  42.0 0.7 %bitcast_dynamic-update-slice_fusion = f32[1,256,256]{2,1,0:T(8,128)} fusion(f32[1,256,256]{2,1,0:T(8,128)} %pad_bitcast_fusion, bf16[128,256]{1,0:T(8,128)(2,1)S(1)} %collective-permute-done.17, bf16[128,256]{1,0:T(8,128)(2,1)S(1)} %add_convert_fusion), kind=kLoop, calls=%fused_computation.9 | loop fusion | flops 98304 | bytes 262144 | tf_op jit(solution)/shard_map/dynamic_update_slice | solution.py:239
  (33 shorter events, 3.5 us)
Async XLA Ops:
  0.0 17.5 %copy-start = (s32[1024]{0:T(1024)S(1)}, s32[1024]{0:T(1024)}, u32[]{:S(2)}) copy-start(s32[1024]{0:T(1024)} %param.5) | copy-start | bytes 12292
  0.0 7.2 %collective-permute-start.1 = (f32[32,256]{1,0:T(8,128)}, f32[32,256]{1,0:T(8,128)S(1)}, u32[]{:S(2)}, u32[]{:S(2)}) collective-permute-start(f32[32,256]{1,0:T(8,128)} %bitcast.12), channel_id=1, source_target_pairs={{0,24},{8,16},{16,8},{24,0},{1,25},{9,17},{17,9},{25,1},{2,26},{10... | collective-permute-start | bytes 98312 | tf_op jit(solution)/shard_map/ppermute | solution.py:165
  5.1 5.0 %collective-permute-start = (f32[32,256]{1,0:T(8,128)}, f32[32,256]{1,0:T(8,128)S(1)}, u32[]{:S(2)}, u32[]{:S(2)}) collective-permute-start(f32[32,256]{1,0:T(8,128)} %bitcast.13), channel_id=1, source_target_pairs={{0,16},{8,24},{16,0},{24,8},{1,17},{9,25},{17,1},{25,9},{2,18},{10... | collective-permute-start | bytes 98312 | tf_op jit(solution)/shard_map/ppermute | solution.py:165
  5.1 5.0 %collective-permute-start.2 = (f32[32,256]{1,0:T(8,128)}, f32[32,256]{1,0:T(8,128)S(1)}, u32[]{:S(2)}, u32[]{:S(2)}) collective-permute-start(f32[32,256]{1,0:T(8,128)} %bitcast.14), channel_id=1, source_target_pairs={{0,8},{8,0},{16,24},{24,16},{1,9},{9,1},{17,25},{25,17},{2,10},{10... | collective-permute-start | bytes 98312 | tf_op jit(solution)/shard_map/ppermute | solution.py:165
  10.1 6.4 %collective-permute-start.6 = (bf16[4,32,256]{2,1,0:T(8,128)(2,1)S(1)}, bf16[4,32,256]{2,1,0:T(8,128)(2,1)S(1)}, u32[]{:S(2)}, u32[]{:S(2)}) collective-permute-start(bf16[4,32,256]{2,1,0:T(8,128)(2,1)S(1)} %stack_parts.2.refs_0_), channel_id=1, source_target_pairs={{0,6},{2,4},{4,2},{6,0},{1,7},{3,5},{5,3},{7,1},{8,14},{10,12},{12... | collective-permute-start | bytes 196616 | tf_op jit(solution)/shard_map/ppermute | solution.py:165
  12.6 4.3 %collective-permute-start.5 = (bf16[4,32,256]{2,1,0:T(8,128)(2,1)S(1)}, bf16[4,32,256]{2,1,0:T(8,128)(2,1)S(1)}, u32[]{:S(2)}, u32[]{:S(2)}) collective-permute-start(bf16[4,32,256]{2,1,0:T(8,128)(2,1)S(1)} %stack_parts.2.refs_0_), channel_id=1, source_target_pairs={{0,2},{2,0},{4,6},{6,4},{1,3},{3,1},{5,7},{7,5},{8,10},{10,8},{12,... | collective-permute-start | bytes 196616 | tf_op jit(solution)/shard_map/ppermute | solution.py:165
  13.1 4.3 %collective-permute-start.4 = (bf16[4,32,256]{2,1,0:T(8,128)(2,1)S(1)}, bf16[4,32,256]{2,1,0:T(8,128)(2,1)S(1)}, u32[]{:S(2)}, u32[]{:S(2)}) collective-permute-start(bf16[4,32,256]{2,1,0:T(8,128)(2,1)S(1)} %stack_parts.2.refs_0_), channel_id=1, source_target_pairs={{0,4},{2,6},{4,0},{6,2},{1,5},{3,7},{5,1},{7,3},{8,12},{10,14},{12... | collective-permute-start | bytes 196616 | tf_op jit(solution)/shard_map/ppermute | solution.py:165
  13.6 3.8 %collective-permute-start.3 = (bf16[4,32,256]{2,1,0:T(8,128)(2,1)S(1)}, bf16[4,32,256]{2,1,0:T(8,128)(2,1)S(1)}, u32[]{:S(2)}, u32[]{:S(2)}) collective-permute-start(bf16[4,32,256]{2,1,0:T(8,128)(2,1)S(1)} %stack_parts.2.refs_0_), channel_id=1, source_target_pairs={{0,1},{1,0},{2,3},{3,2},{4,5},{5,4},{6,7},{7,6},{8,9},{9,8},{10,11... | collective-permute-start | bytes 196616 | tf_op jit(solution)/shard_map/ppermute | solution.py:165
  17.4 1.5 %collective-permute-start.7 = (bf16[3,4,32,256]{3,2,1,0:T(8,128)(2,1)S(1)}, bf16[3,4,32,256]{3,2,1,0:T(8,128)(2,1)S(1)}, u32[]{:S(2)}, u32[]{:S(2)}) collective-permute-start(bf16[3,4,32,256]{3,2,1,0:T(8,128)(2,1)S(1)} %stack_parts.3), channel_id=1, source_target_pairs={{0,1},{1,0},{2,3},{3,2},{4,5},{5,4},{6,7},{7,6},{8,9},{9,8},{10,11... | collective-permute-start | bytes 589832 | tf_op jit(solution)/shard_map/ppermute | solution.py:165
  20.1 1.4 %collective-permute-start.8 = (bf16[2,128,256]{2,1,0:T(8,128)(2,1)S(1)}, bf16[2,128,256]{2,1,0:T(8,128)(2,1)S(1)}, u32[]{:S(2)}, u32[]{:S(2)}) collective-permute-start(bf16[2,128,256]{2,1,0:T(8,128)(2,1)S(1)} %get-tuple-element.34), channel_id=1, source_target_pairs={{0,1},{1,0},{2,3},{3,2},{4,5},{5,4},{6,7},{7,6},{8,9},{9,8},{10,11... | collective-permute-start | bytes 393224 | tf_op jit(solution)/shard_map/ppermute | solution.py:165
  20.3 2.8 %collective-permute-start.13 = (bf16[2,128,256]{2,1,0:T(8,128)(2,1)S(1)}, bf16[2,128,256]{2,1,0:T(8,128)(2,1)S(1)}, u32[]{:S(2)}, u32[]{:S(2)}) collective-permute-start(bf16[2,128,256]{2,1,0:T(8,128)(2,1)S(1)} %get-tuple-element.36), channel_id=1, source_target_pairs={{0,1},{1,0},{2,3},{3,2},{4,5},{5,4},{6,7},{7,6},{8,9},{9,8},{10,11... | collective-permute-start | bytes 393224 | tf_op jit(solution)/shard_map/ppermute | solution.py:165
  21.6 4.6 %collective-permute-start.9 = (bf16[1,128,256]{2,1,0:T(8,128)(2,1)S(1)}, bf16[1,128,256]{2,1,0:T(8,128)(2,1)S(1)}, u32[]{:S(2)}, u32[]{:S(2)}) collective-permute-start(bf16[1,128,256]{2,1,0:T(8,128)(2,1)S(1)} %slice.35), channel_id=1, source_target_pairs={{0,2},{2,0},{1,3},{3,1},{4,6},{6,4},{5,7},{7,5},{8,10},{10,8},{9,1... | collective-permute-start | bytes 196616 | tf_op jit(solution)/shard_map/ppermute | solution.py:165
  23.2 4.3 %collective-permute-start.14 = (bf16[1,128,256]{2,1,0:T(8,128)(2,1)S(1)}, bf16[1,128,256]{2,1,0:T(8,128)(2,1)S(1)}, u32[]{:S(2)}, u32[]{:S(2)}) collective-permute-start(bf16[1,128,256]{2,1,0:T(8,128)(2,1)S(1)} %slice.34), channel_id=1, source_target_pairs={{0,2},{2,0},{1,3},{3,1},{4,6},{6,4},{5,7},{7,5},{8,10},{10,8},{9,1... | collective-permute-start | bytes 196616 | tf_op jit(solution)/shard_map/ppermute | solution.py:165
  26.2 4.3 %collective-permute-start.10 = (bf16[128,256]{1,0:T(8,128)(2,1)S(1)}, bf16[128,256]{1,0:T(8,128)(2,1)S(1)}, u32[]{:S(2)}, u32[]{:S(2)}) collective-permute-start(bf16[128,256]{1,0:T(8,128)(2,1)S(1)} %fusion.2), channel_id=1, source_target_pairs={{0,4},{4,0},{1,5},{5,1},{2,6},{6,2},{3,7},{7,3},{8,12},{12,8},{9,1... | collective-permute-start | bytes 196616 | tf_op jit(solution)/shard_map/ppermute | solution.py:165
  27.5 5.3 %collective-permute-start.15 = (bf16[128,256]{1,0:T(8,128)(2,1)S(1)}, bf16[128,256]{1,0:T(8,128)(2,1)S(1)}, u32[]{:S(2)}, u32[]{:S(2)}) collective-permute-start(bf16[128,256]{1,0:T(8,128)(2,1)S(1)} %fusion.3), channel_id=1, source_target_pairs={{0,16},{8,24},{16,0},{24,8},{1,17},{9,25},{17,1},{25,9},{2,18},{10... | collective-permute-start | bytes 196616 | tf_op jit(solution)/shard_map/ppermute | solution.py:165
  30.6 4.3 %collective-permute-start.11 = (bf16[128,256]{1,0:T(8,128)(2,1)S(1)}, bf16[128,256]{1,0:T(8,128)(2,1)S(1)}, u32[]{:S(2)}, u32[]{:S(2)}) collective-permute-start(bf16[128,256]{1,0:T(8,128)(2,1)S(1)} %add_convert_fusion.3), channel_id=1, source_target_pairs={{0,8},{8,0},{16,24},{24,16},{1,9},{9,1},{17,25},{25,17},{2,10},{10... | collective-permute-start | bytes 196616 | tf_op jit(solution)/shard_map/ppermute | solution.py:165
  32.8 4.9 %collective-permute-start.16 = (bf16[128,256]{1,0:T(8,128)(2,1)S(1)}, bf16[128,256]{1,0:T(8,128)(2,1)S(1)}, u32[]{:S(2)}, u32[]{:S(2)}) collective-permute-start(bf16[128,256]{1,0:T(8,128)(2,1)S(1)} %add_convert_fusion.1), channel_id=1, source_target_pairs={{0,4},{4,0},{1,5},{5,1},{2,6},{6,2},{3,7},{7,3},{8,12},{12,8},{9,1... | collective-permute-start | bytes 196616 | tf_op jit(solution)/shard_map/ppermute | solution.py:165
  34.9 5.4 %collective-permute-start.12 = (bf16[128,256]{1,0:T(8,128)(2,1)S(1)}, bf16[128,256]{1,0:T(8,128)(2,1)S(1)}, u32[]{:S(2)}, u32[]{:S(2)}) collective-permute-start(bf16[128,256]{1,0:T(8,128)(2,1)S(1)} %add_convert_fusion.2), channel_id=1, source_target_pairs={{0,16},{8,24},{16,0},{24,8},{1,17},{9,25},{17,1},{25,9},{2,18},{10... | collective-permute-start | bytes 196616 | tf_op jit(solution)/shard_map/ppermute | solution.py:165
  37.7 4.3 %collective-permute-start.17 = (bf16[128,256]{1,0:T(8,128)(2,1)S(1)}, bf16[128,256]{1,0:T(8,128)(2,1)S(1)}, u32[]{:S(2)}, u32[]{:S(2)}) collective-permute-start(bf16[128,256]{1,0:T(8,128)(2,1)S(1)} %add_convert_fusion), channel_id=1, source_target_pairs={{0,8},{8,0},{16,24},{24,16},{1,9},{9,1},{17,25},{25,17},{2,10},{10... | collective-permute-start | bytes 196616 | tf_op jit(solution)/shard_map/ppermute | solution.py:165

commit v6 on v5

--- a/solution.py
+++ b/solution.py
@@ -101,8 +101,9 @@
 
 
 def gradient_kernel(groups, marginals_ref, roots_ref, logs_ref, live_ref, tiles_ref, *refs):
-    parts, (last_ref, *out_refs, table, logits, grads, terms) = list(refs[: groups + 1]), refs[groups + 1 :]
-    parts += [last_ref.at[j] for j in range(groups - 1)]
+    parts, (*others_refs, table, logits, grads, terms) = list(refs[:groups]), refs[groups:]
+    (low_ref, high_ref), out_refs = others_refs[:2], others_refs[2:]
+    parts += [ref.at[j] for ref in (low_ref, high_ref) for j in range(groups // 2)]
     far, chunk, width = parts[0].shape
     blocks, size = groups, grads.shape[0]
     here, core = lax.axis_index("chip"), lax.axis_index("core")
@@ -202,9 +203,9 @@
     pieces = others(lambda i: swap(piece, "far", i), far)
     column = stack([piece.astype(bf16)] + pieces)
     parts = others(lambda j: swap(column, ("near", "chip"), (j % 2, j // 2)), groups)
-    other_column = swap(column, "core", 1)
-    other_column, *parts, sums = lax.optimization_barrier((other_column, *parts, sums))
-    parts = [column] + parts + [other_column, swap(stack(parts), "core", 1)]
+    *parts, sums = lax.optimization_barrier((*parts, sums))
+    parts = [column] + parts
+    parts += [swap(stack(some), "core", 1) for some in (parts[: groups // 2], parts[groups // 2 :])]
 
     heights = (size // 2, size // 2)
     halves = pl.pallas_call(

time: 42.9 us -> 42.7 us (level)
  transfers between devices with their start and end apart: 18 -> 18, of which waited for: 13 -> 14; matrix products, arithmetic and copies ran while one was open for 4% -> 4% of each run, Pallas kernels for 7% -> 7%
where the time goes in v6:
time: 42.7 us; the launch traced here: 42.6 us
  starting transfers between devices  18.8 us (44%)
  waiting for transfers between devices  17.2 us (40%)
  Pallas kernels  4.03 us (9%)
  other arithmetic  1.64 us (4%)
  local copies, waits for them, and re-layouts  0.75 us (2%)
    ppermute x18, starting transfers between devices, swap(): lax.ppermute(value, axes, [(i, i ^ both) for i in range(math.prod(sizes))])  18.8 us
    ppermute x18, waiting for transfers between devices, swap(): lax.ppermute(value, axes, [(i, i ^ both) for i in range(math.prod(sizes))])  17.2 us
    pallas_call x1, Pallas kernels, sum_counts(): pl.pallas_call(functools.partial(count_kernel, tiles), out_shape=[jax.Sha...  2.82 us
    pallas_call x1, Pallas kernels, local(): pl.pallas_call(functools.partial(gradient_kernel, groups), out_shape=[jax...  1.18 us
  transfers between devices with their start and end apart: 18, of which 14 were waited for; matrix products, arithmetic and copies ran while one was open for 4% of the time, Pallas kernels for 7%

profile of v6, /device:TPU:0, one launch (start us, length us, event | category | flops | bytes accessed | tf_op | source)
XLA Modules:
  0.0 42.6 jit_solution(11653376826199448628)
XLA Ops:
  0.0 5.0 %collective-permute-start.1 = (f32[32,256]{1,0:T(8,128)}, f32[32,256]{1,0:T(8,128)S(1)}, u32[]{:S(2)}, u32[]{:S(2)}) collective-permute-start(f32[32,256]{1,0:T(8,128)} %bitcast.12), channel_id=1, source_target_pairs={{0,24},{8,16},{16,8},{24,0},{1,25},{9,17},{17,9},{25,1},{2,26},{10... | collective-permute-start | bytes 98312 | tf_op jit(solution)/shard_map/ppermute | solution.py:166
  5.1 0.6 %collective-permute-start.2 = (f32[32,256]{1,0:T(8,128)}, f32[32,256]{1,0:T(8,128)S(1)}, u32[]{:S(2)}, u32[]{:S(2)}) collective-permute-start(f32[32,256]{1,0:T(8,128)} %bitcast.14), channel_id=1, source_target_pairs={{0,8},{8,0},{16,24},{24,16},{1,9},{9,1},{17,25},{25,17},{2,10},{10... | collective-permute-start | bytes 98312 | tf_op jit(solution)/shard_map/ppermute | solution.py:166
  5.7 0.8 %bitcast_convert_fusion.refs_0_ = bf16[32,256]{1,0:T(8,128)(2,1)S(1)} fusion(f32[1,32,256]{2,1,0:T(8,128)} %param.4), kind=kLoop, calls=%fused_computation.17 | loop fusion | flops 8192 | bytes 49152 | tf_op jit(solution)/shard_map/convert_element_type | solution.py:204
  6.5 0.7 %collective-permute-done.1.refs_2_ = f32[32,256]{1,0:T(8,128)S(1)} collective-permute-done((f32[32,256]{1,0:T(8,128)}, f32[32,256]{1,0:T(8,128)S(1)}, u32[]{:S(2)}, u32[]{:S(2)}) %collective-permute-start.1) | collective-permute-done | bytes 32800 | tf_op jit(solution)/shard_map/ppermute | solution.py:166
  7.2 2.9 %collective-permute-done.refs_1_ = f32[32,256]{1,0:T(8,128)S(1)} collective-permute-done((f32[32,256]{1,0:T(8,128)}, f32[32,256]{1,0:T(8,128)S(1)}, u32[]{:S(2)}, u32[]{:S(2)}) %collective-permute-start) | collective-permute-done | bytes 32800 | tf_op jit(solution)/shard_map/ppermute | solution.py:166
  10.1 2.5 %collective-permute-start.5 = (bf16[4,32,256]{2,1,0:T(8,128)(2,1)S(1)}, bf16[4,32,256]{2,1,0:T(8,128)(2,1)S(1)}, u32[]{:S(2)}, u32[]{:S(2)}) collective-permute-start(bf16[4,32,256]{2,1,0:T(8,128)(2,1)S(1)} %stack_parts.3.refs_0_), channel_id=1, source_target_pairs={{0,6},{2,4},{4,2},{6,0},{1,7},{3,5},{5,3},{7,1},{8,14},{10,12},{12... | collective-permute-start | bytes 196616 | tf_op jit(solution)/shard_map/ppermute | solution.py:166
  13.6 2.8 %sum_counts.1 = (f32[4,256,256]{2,1,0:T(8,128)S(1)}, f32[4,256,256]{2,1,0:T(8,128)S(1)}, bf16[4,256,256]{2,1,0:T(8,128)(2,1)S(1)}, f32[4,256]{1,0:T(4,128)S(1)}) custom-call(s32[1,1,16]{2,1,0:T(1,128)} %visits_ref.1, s32[16,256,256]{2,1,0:T(8,128)} %bitcast.11), custom_call_target="tpu_custom_call" | custom-call | flops 10485760 | bytes 4194304 | tf_op jit(solution)/shard_map/sum_counts/pallas_call | solution.py:61
  18.0 0.8 %collective-permute-done.7.refs_5_ = bf16[2,4,32,256]{3,2,1,0:T(8,128)(2,1)S(1)} collective-permute-done((bf16[2,4,32,256]{3,2,1,0:T(8,128)(2,1)S(1)}, bf16[2,4,32,256]{3,2,1,0:T(8,128)(2,1)S(1)}, u32[]{:S(2)}, u32[]{:S(2)}) %collective-permute-start.7) | collective-permute-done | bytes 131104 | tf_op jit(solution)/shard_map/ppermute | solution.py:166
  19.0 1.2 %swivel_gradient.1 = (f32[2,128,256]{2,1,0:T(8,128)S(1)}, bf16[2,128,256]{2,1,0:T(8,128)(2,1)S(1)}, f32[2,128,256]{2,1,0:T(8,128)S(1)}, bf16[2,128,256]{2,1,0:T(8,128)(2,1)S(1)}) custom-call(s32[4,256]{1,0:T(4,128)S(1)} %reshape.5.marginals_ref, f32[4,256,256]{2,1,0:T(8,128)S(1)} %get-tuple-element.24.roots_ref, ...), custom_call_target="tpu_custom_call" | custom-call | flops 671088640 | bytes 3145728 | tf_op jit(solution)/shard_map/swivel_gradient/pallas_call | solution.py:211
  20.8 0.8 %collective-permute-done.8 = bf16[2,128,256]{2,1,0:T(8,128)(2,1)S(1)} collective-permute-done((bf16[2,128,256]{2,1,0:T(8,128)(2,1)S(1)}, bf16[2,128,256]{2,1,0:T(8,128)(2,1)S(1)}, u32[]{:S(2)}, u32[]{:S(2)}) %collective-permute-start.8) | collective-permute-done | bytes 131104 | tf_op jit(solution)/shard_map/ppermute | solution.py:166
  21.7 1.5 %collective-permute-start.9 = (bf16[1,128,256]{2,1,0:T(8,128)(2,1)S(1)}, bf16[1,128,256]{2,1,0:T(8,128)(2,1)S(1)}, u32[]{:S(2)}, u32[]{:S(2)}) collective-permute-start(bf16[1,128,256]{2,1,0:T(8,128)(2,1)S(1)} %slice.35), channel_id=1, source_target_pairs={{0,2},{2,0},{1,3},{3,1},{4,6},{6,4},{5,7},{7,5},{8,10},{10,8},{9,1... | collective-permute-start | bytes 196616 | tf_op jit(solution)/shard_map/ppermute | solution.py:166
  23.9 2.3 %collective-permute-done.9 = bf16[1,128,256]{2,1,0:T(8,128)(2,1)S(1)} collective-permute-done((bf16[1,128,256]{2,1,0:T(8,128)(2,1)S(1)}, bf16[1,128,256]{2,1,0:T(8,128)(2,1)S(1)}, u32[]{:S(2)}, u32[]{:S(2)}) %collective-permute-start.9) | collective-permute-done | bytes 65568 | tf_op jit(solution)/shard_map/ppermute | solution.py:166
  26.2 0.7 %collective-permute-start.10 = (bf16[128,256]{1,0:T(8,128)(2,1)S(1)}, bf16[128,256]{1,0:T(8,128)(2,1)S(1)}, u32[]{:S(2)}, u32[]{:S(2)}) collective-permute-start(bf16[128,256]{1,0:T(8,128)(2,1)S(1)} %fusion.2), channel_id=1, source_target_pairs={{0,4},{4,0},{1,5},{5,1},{2,6},{6,2},{3,7},{7,3},{8,12},{12,8},{9,1... | collective-permute-start | bytes 196616 | tf_op jit(solution)/shard_map/ppermute | solution.py:166
  26.9 0.7 %collective-permute-done.14 = bf16[1,128,256]{2,1,0:T(8,128)(2,1)S(1)} collective-permute-done((bf16[1,128,256]{2,1,0:T(8,128)(2,1)S(1)}, bf16[1,128,256]{2,1,0:T(8,128)(2,1)S(1)}, u32[]{:S(2)}, u32[]{:S(2)}) %collective-permute-start.14) | collective-permute-done | bytes 65568 | tf_op jit(solution)/shard_map/ppermute | solution.py:166
  27.6 2.1 %collective-permute-start.15 = (bf16[128,256]{1,0:T(8,128)(2,1)S(1)}, bf16[128,256]{1,0:T(8,128)(2,1)S(1)}, u32[]{:S(2)}, u32[]{:S(2)}) collective-permute-start(bf16[128,256]{1,0:T(8,128)(2,1)S(1)} %fusion.3), channel_id=1, source_target_pairs={{0,16},{8,24},{16,0},{24,8},{1,17},{9,25},{17,1},{25,9},{2,18},{10... | collective-permute-start | bytes 196616 | tf_op jit(solution)/shard_map/ppermute | solution.py:166
  29.7 0.8 %collective-permute-done.10 = bf16[128,256]{1,0:T(8,128)(2,1)S(1)} collective-permute-done((bf16[128,256]{1,0:T(8,128)(2,1)S(1)}, bf16[128,256]{1,0:T(8,128)(2,1)S(1)}, u32[]{:S(2)}, u32[]{:S(2)}) %collective-permute-start.10) | collective-permute-done | bytes 65568 | tf_op jit(solution)/shard_map/ppermute | solution.py:166
  30.6 2.3 %collective-permute-done.15 = bf16[128,256]{1,0:T(8,128)(2,1)S(1)} collective-permute-done((bf16[128,256]{1,0:T(8,128)(2,1)S(1)}, bf16[128,256]{1,0:T(8,128)(2,1)S(1)}, u32[]{:S(2)}, u32[]{:S(2)}) %collective-permute-start.15) | collective-permute-done | bytes 65568 | tf_op jit(solution)/shard_map/ppermute | solution.py:166
  32.9 0.7 %collective-permute-start.16 = (bf16[128,256]{1,0:T(8,128)(2,1)S(1)}, bf16[128,256]{1,0:T(8,128)(2,1)S(1)}, u32[]{:S(2)}, u32[]{:S(2)}) collective-permute-start(bf16[128,256]{1,0:T(8,128)(2,1)S(1)} %add_convert_fusion.1), channel_id=1, source_target_pairs={{0,4},{4,0},{1,5},{5,1},{2,6},{6,2},{3,7},{7,3},{8,12},{12,8},{9,1... | collective-permute-start | bytes 196616 | tf_op jit(solution)/shard_map/ppermute | solution.py:166
  33.7 1.2 %collective-permute-done.11 = bf16[128,256]{1,0:T(8,128)(2,1)S(1)} collective-permute-done((bf16[128,256]{1,0:T(8,128)(2,1)S(1)}, bf16[128,256]{1,0:T(8,128)(2,1)S(1)}, u32[]{:S(2)}, u32[]{:S(2)}) %collective-permute-start.11) | collective-permute-done | bytes 65568 | tf_op jit(solution)/shard_map/ppermute | solution.py:166
  34.9 2.6 %collective-permute-start.12 = (bf16[128,256]{1,0:T(8,128)(2,1)S(1)}, bf16[128,256]{1,0:T(8,128)(2,1)S(1)}, u32[]{:S(2)}, u32[]{:S(2)}) collective-permute-start(bf16[128,256]{1,0:T(8,128)(2,1)S(1)} %add_convert_fusion.2), channel_id=1, source_target_pairs={{0,16},{8,24},{16,0},{24,8},{1,17},{9,25},{17,1},{25,9},{2,18},{10... | collective-permute-start | bytes 196616 | tf_op jit(solution)/shard_map/ppermute | solution.py:166
  37.6 2.7 %collective-permute-done.12 = bf16[128,256]{1,0:T(8,128)(2,1)S(1)} collective-permute-done((bf16[128,256]{1,0:T(8,128)(2,1)S(1)}, bf16[128,256]{1,0:T(8,128)(2,1)S(1)}, u32[]{:S(2)}, u32[]{:S(2)}) %collective-permute-start.12) | collective-permute-done | bytes 65568 | tf_op jit(solution)/shard_map/ppermute | solution.py:166
  40.3 0.7 %pad_bitcast_fusion = f32[1,256,256]{2,1,0:T(8,128)} fusion(f32[128,256]{1,0:T(8,128)S(1)} %convert_add_fusion.2), kind=kLoop, calls=%fused_computation.1 | loop fusion | bytes 393216 | tf_op jit(solution)/shard_map/broadcast_in_dim | solution.py:239
  41.0 0.9 %collective-permute-done.17 = bf16[128,256]{1,0:T(8,128)(2,1)S(1)} collective-permute-done((bf16[128,256]{1,0:T(8,128)(2,1)S(1)}, bf16[128,256]{1,0:T(8,128)(2,1)S(1)}, u32[]{:S(2)}, u32[]{:S(2)}) %collective-permute-start.17) | collective-permute-done | bytes 65568 | tf_op jit(solution)/shard_map/ppermute | solution.py:166
  41.9 0.7 %bitcast_dynamic-update-slice_fusion = f32[1,256,256]{2,1,0:T(8,128)} fusion(f32[1,256,256]{2,1,0:T(8,128)} %pad_bitcast_fusion, bf16[128,256]{1,0:T(8,128)(2,1)S(1)} %collective-permute-done.17, bf16[128,256]{1,0:T(8,128)(2,1)S(1)} %add_convert_fusion), kind=kLoop, calls=%fused_computation.9 | loop fusion | flops 98304 | bytes 262144 | tf_op jit(solution)/shard_map/dynamic_update_slice | solution.py:240
  (34 shorter events, 4.3 us)
Async XLA Ops:
  0.0 18.0 %copy-start = (s32[1024]{0:T(1024)S(1)}, s32[1024]{0:T(1024)}, u32[]{:S(2)}) copy-start(s32[1024]{0:T(1024)} %param.5) | copy-start | bytes 12292
  0.0 7.2 %collective-permute-start.1 = (f32[32,256]{1,0:T(8,128)}, f32[32,256]{1,0:T(8,128)S(1)}, u32[]{:S(2)}, u32[]{:S(2)}) collective-permute-start(f32[32,256]{1,0:T(8,128)} %bitcast.12), channel_id=1, source_target_pairs={{0,24},{8,16},{16,8},{24,0},{1,25},{9,17},{17,9},{25,1},{2,26},{10... | collective-permute-start | bytes 98312 | tf_op jit(solution)/shard_map/ppermute | solution.py:166
  5.1 5.0 %collective-permute-start = (f32[32,256]{1,0:T(8,128)}, f32[32,256]{1,0:T(8,128)S(1)}, u32[]{:S(2)}, u32[]{:S(2)}) collective-permute-start(f32[32,256]{1,0:T(8,128)} %bitcast.13), channel_id=1, source_target_pairs={{0,16},{8,24},{16,0},{24,8},{1,17},{9,25},{17,1},{25,9},{2,18},{10... | collective-permute-start | bytes 98312 | tf_op jit(solution)/shard_map/ppermute | solution.py:166
  5.1 5.0 %collective-permute-start.2 = (f32[32,256]{1,0:T(8,128)}, f32[32,256]{1,0:T(8,128)S(1)}, u32[]{:S(2)}, u32[]{:S(2)}) collective-permute-start(f32[32,256]{1,0:T(8,128)} %bitcast.14), channel_id=1, source_target_pairs={{0,8},{8,0},{16,24},{24,16},{1,9},{9,1},{17,25},{25,17},{2,10},{10... | collective-permute-start | bytes 98312 | tf_op jit(solution)/shard_map/ppermute | solution.py:166
  10.1 6.4 %collective-permute-start.5 = (bf16[4,32,256]{2,1,0:T(8,128)(2,1)S(1)}, bf16[4,32,256]{2,1,0:T(8,128)(2,1)S(1)}, u32[]{:S(2)}, u32[]{:S(2)}) collective-permute-start(bf16[4,32,256]{2,1,0:T(8,128)(2,1)S(1)} %stack_parts.3.refs_0_), channel_id=1, source_target_pairs={{0,6},{2,4},{4,2},{6,0},{1,7},{3,5},{5,3},{7,1},{8,14},{10,12},{12... | collective-permute-start | bytes 196616 | tf_op jit(solution)/shard_map/ppermute | solution.py:166
  12.6 4.3 %collective-permute-start.4 = (bf16[4,32,256]{2,1,0:T(8,128)(2,1)S(1)}, bf16[4,32,256]{2,1,0:T(8,128)(2,1)S(1)}, u32[]{:S(2)}, u32[]{:S(2)}) collective-permute-start(bf16[4,32,256]{2,1,0:T(8,128)(2,1)S(1)} %stack_parts.3.refs_0_), channel_id=1, source_target_pairs={{0,2},{2,0},{4,6},{6,4},{1,3},{3,1},{5,7},{7,5},{8,10},{10,8},{12,... | collective-permute-start | bytes 196616 | tf_op jit(solution)/shard_map/ppermute | solution.py:166
  13.1 4.3 %collective-permute-start.3 = (bf16[4,32,256]{2,1,0:T(8,128)(2,1)S(1)}, bf16[4,32,256]{2,1,0:T(8,128)(2,1)S(1)}, u32[]{:S(2)}, u32[]{:S(2)}) collective-permute-start(bf16[4,32,256]{2,1,0:T(8,128)(2,1)S(1)} %stack_parts.3.refs_0_), channel_id=1, source_target_pairs={{0,4},{2,6},{4,0},{6,2},{1,5},{3,7},{5,1},{7,3},{8,12},{10,14},{12... | collective-permute-start | bytes 196616 | tf_op jit(solution)/shard_map/ppermute | solution.py:166
  17.4 1.4 %collective-permute-start.7 = (bf16[2,4,32,256]{3,2,1,0:T(8,128)(2,1)S(1)}, bf16[2,4,32,256]{3,2,1,0:T(8,128)(2,1)S(1)}, u32[]{:S(2)}, u32[]{:S(2)}) collective-permute-start(bf16[2,4,32,256]{3,2,1,0:T(8,128)(2,1)S(1)} %stack_parts.5), channel_id=1, source_target_pairs={{0,1},{1,0},{2,3},{3,2},{4,5},{5,4},{6,7},{7,6},{8,9},{9,8},{10,11... | collective-permute-start | bytes 393224 | tf_op jit(solution)/shard_map/ppermute | solution.py:166
  17.5 1.5 %collective-permute-start.6 = (bf16[2,4,32,256]{3,2,1,0:T(8,128)(2,1)S(1)}, bf16[2,4,32,256]{3,2,1,0:T(8,128)(2,1)S(1)}, u32[]{:S(2)}, u32[]{:S(2)}) collective-permute-start(bf16[2,4,32,256]{3,2,1,0:T(8,128)(2,1)S(1)} %stack_parts.4), channel_id=1, source_target_pairs={{0,1},{1,0},{2,3},{3,2},{4,5},{5,4},{6,7},{7,6},{8,9},{9,8},{10,11... | collective-permute-start | bytes 393224 | tf_op jit(solution)/shard_map/ppermute | solution.py:166
  20.2 1.4 %collective-permute-start.8 = (bf16[2,128,256]{2,1,0:T(8,128)(2,1)S(1)}, bf16[2,128,256]{2,1,0:T(8,128)(2,1)S(1)}, u32[]{:S(2)}, u32[]{:S(2)}) collective-permute-start(bf16[2,128,256]{2,1,0:T(8,128)(2,1)S(1)} %get-tuple-element.32), channel_id=1, source_target_pairs={{0,1},{1,0},{2,3},{3,2},{4,5},{5,4},{6,7},{7,6},{8,9},{9,8},{10,11... | collective-permute-start | bytes 393224 | tf_op jit(solution)/shard_map/ppermute | solution.py:166
  20.6 2.6 %collective-permute-start.13 = (bf16[2,128,256]{2,1,0:T(8,128)(2,1)S(1)}, bf16[2,128,256]{2,1,0:T(8,128)(2,1)S(1)}, u32[]{:S(2)}, u32[]{:S(2)}) collective-permute-start(bf16[2,128,256]{2,1,0:T(8,128)(2,1)S(1)} %get-tuple-element.34), channel_id=1, source_target_pairs={{0,1},{1,0},{2,3},{3,2},{4,5},{5,4},{6,7},{7,6},{8,9},{9,8},{10,11... | collective-permute-start | bytes 393224 | tf_op jit(solution)/shard_map/ppermute | solution.py:166
  21.7 4.5 %collective-permute-start.9 = (bf16[1,128,256]{2,1,0:T(8,128)(2,1)S(1)}, bf16[1,128,256]{2,1,0:T(8,128)(2,1)S(1)}, u32[]{:S(2)}, u32[]{:S(2)}) collective-permute-start(bf16[1,128,256]{2,1,0:T(8,128)(2,1)S(1)} %slice.35), channel_id=1, source_target_pairs={{0,2},{2,0},{1,3},{3,1},{4,6},{6,4},{5,7},{7,5},{8,10},{10,8},{9,1... | collective-permute-start | bytes 196616 | tf_op jit(solution)/shard_map/ppermute | solution.py:166
  23.3 4.3 %collective-permute-start.14 = (bf16[1,128,256]{2,1,0:T(8,128)(2,1)S(1)}, bf16[1,128,256]{2,1,0:T(8,128)(2,1)S(1)}, u32[]{:S(2)}, u32[]{:S(2)}) collective-permute-start(bf16[1,128,256]{2,1,0:T(8,128)(2,1)S(1)} %slice.34), channel_id=1, source_target_pairs={{0,2},{2,0},{1,3},{3,1},{4,6},{6,4},{5,7},{7,5},{8,10},{10,8},{9,1... | collective-permute-start | bytes 196616 | tf_op jit(solution)/shard_map/ppermute | solution.py:166
  26.2 4.3 %collective-permute-start.10 = (bf16[128,256]{1,0:T(8,128)(2,1)S(1)}, bf16[128,256]{1,0:T(8,128)(2,1)S(1)}, u32[]{:S(2)}, u32[]{:S(2)}) collective-permute-start(bf16[128,256]{1,0:T(8,128)(2,1)S(1)} %fusion.2), channel_id=1, source_target_pairs={{0,4},{4,0},{1,5},{5,1},{2,6},{6,2},{3,7},{7,3},{8,12},{12,8},{9,1... | collective-permute-start | bytes 196616 | tf_op jit(solution)/shard_map/ppermute | solution.py:166
  27.6 5.3 %collective-permute-start.15 = (bf16[128,256]{1,0:T(8,128)(2,1)S(1)}, bf16[128,256]{1,0:T(8,128)(2,1)S(1)}, u32[]{:S(2)}, u32[]{:S(2)}) collective-permute-start(bf16[128,256]{1,0:T(8,128)(2,1)S(1)} %fusion.3), channel_id=1, source_target_pairs={{0,16},{8,24},{16,0},{24,8},{1,17},{9,25},{17,1},{25,9},{2,18},{10... | collective-permute-start | bytes 196616 | tf_op jit(solution)/shard_map/ppermute | solution.py:166
  30.6 4.3 %collective-permute-start.11 = (bf16[128,256]{1,0:T(8,128)(2,1)S(1)}, bf16[128,256]{1,0:T(8,128)(2,1)S(1)}, u32[]{:S(2)}, u32[]{:S(2)}) collective-permute-start(bf16[128,256]{1,0:T(8,128)(2,1)S(1)} %add_convert_fusion.3), channel_id=1, source_target_pairs={{0,8},{8,0},{16,24},{24,16},{1,9},{9,1},{17,25},{25,17},{2,10},{10... | collective-permute-start | bytes 196616 | tf_op jit(solution)/shard_map/ppermute | solution.py:166
  32.9 4.6 %collective-permute-start.16 = (bf16[128,256]{1,0:T(8,128)(2,1)S(1)}, bf16[128,256]{1,0:T(8,128)(2,1)S(1)}, u32[]{:S(2)}, u32[]{:S(2)}) collective-permute-start(bf16[128,256]{1,0:T(8,128)(2,1)S(1)} %add_convert_fusion.1), channel_id=1, source_target_pairs={{0,4},{4,0},{1,5},{5,1},{2,6},{6,2},{3,7},{7,3},{8,12},{12,8},{9,1... | collective-permute-start | bytes 196616 | tf_op jit(solution)/shard_map/ppermute | solution.py:166
  34.9 5.4 %collective-permute-start.12 = (bf16[128,256]{1,0:T(8,128)(2,1)S(1)}, bf16[128,256]{1,0:T(8,128)(2,1)S(1)}, u32[]{:S(2)}, u32[]{:S(2)}) collective-permute-start(bf16[128,256]{1,0:T(8,128)(2,1)S(1)} %add_convert_fusion.2), channel_id=1, source_target_pairs={{0,16},{8,24},{16,0},{24,8},{1,17},{9,25},{17,1},{25,9},{2,18},{10... | collective-permute-start | bytes 196616 | tf_op jit(solution)/shard_map/ppermute | solution.py:166
  37.6 4.3 %collective-permute-start.17 = (bf16[128,256]{1,0:T(8,128)(2,1)S(1)}, bf16[128,256]{1,0:T(8,128)(2,1)S(1)}, u32[]{:S(2)}, u32[]{:S(2)}) collective-permute-start(bf16[128,256]{1,0:T(8,128)(2,1)S(1)} %add_convert_fusion), channel_id=1, source_target_pairs={{0,8},{8,0},{16,24},{24,16},{1,9},{9,1},{17,25},{25,17},{2,10},{10... | collective-permute-start | bytes 196616 | tf_op jit(solution)/shard_map/ppermute | solution.py:166

commit v7 on v6

--- a/solution.py
+++ b/solution.py
@@ -129,7 +129,7 @@
         logits[:, v * size : (v + 1) * size] = lax.dot_general(
             own_vectors, vectors, NT, preferred_element_type=jnp.float32
         )
-    step = 64
+    step = 32
     for v in range(blocks):
         visited = LOSS_SCALE * tiles_ref[v : v + 1]
         for first in range(0, size, step):

time: 42.7 us -> 42.7 us (level)
  no operation moved by 1% of the time
where the time goes in v7:
time: 42.7 us; the launch traced here: 42.6 us
  starting transfers between devices  18.8 us (44%)
  waiting for transfers between devices  17.2 us (40%)
  Pallas kernels  4.03 us (9%)
  other arithmetic  1.64 us (4%)
  local copies, waits for them, and re-layouts  0.75 us (2%)
    ppermute x18, starting transfers between devices, swap(): lax.ppermute(value, axes, [(i, i ^ both) for i in range(math.prod(sizes))])  18.8 us
    ppermute x18, waiting for transfers between devices, swap(): lax.ppermute(value, axes, [(i, i ^ both) for i in range(math.prod(sizes))])  17.2 us
    pallas_call x1, Pallas kernels, sum_counts(): pl.pallas_call(functools.partial(count_kernel, tiles), out_shape=[jax.Sha...  2.82 us
    pallas_call x1, Pallas kernels, local(): pl.pallas_call(functools.partial(gradient_kernel, groups), out_shape=[jax...  1.18 us
  transfers between devices with their start and end apart: 18, of which 14 were waited for; matrix products, arithmetic and copies ran while one was open for 4% of the time, Pallas kernels for 7%

profile of v7, /device:TPU:0, one launch (start us, length us, event | category | flops | bytes accessed | tf_op | source)
XLA Modules:
  0.0 42.6 jit_solution(3495562978728948398)
XLA Ops:
  0.0 5.0 %collective-permute-start.1 = (f32[32,256]{1,0:T(8,128)}, f32[32,256]{1,0:T(8,128)S(1)}, u32[]{:S(2)}, u32[]{:S(2)}) collective-permute-start(f32[32,256]{1,0:T(8,128)} %bitcast.12), channel_id=1, source_target_pairs={{0,24},{8,16},{16,8},{24,0},{1,25},{9,17},{17,9},{25,1},{2,26},{10... | collective-permute-start | bytes 98312 | tf_op jit(solution)/shard_map/ppermute | solution.py:166
  5.1 0.6 %collective-permute-start.2 = (f32[32,256]{1,0:T(8,128)}, f32[32,256]{1,0:T(8,128)S(1)}, u32[]{:S(2)}, u32[]{:S(2)}) collective-permute-start(f32[32,256]{1,0:T(8,128)} %bitcast.14), channel_id=1, source_target_pairs={{0,8},{8,0},{16,24},{24,16},{1,9},{9,1},{17,25},{25,17},{2,10},{10... | collective-permute-start | bytes 98312 | tf_op jit(solution)/shard_map/ppermute | solution.py:166
  5.7 0.8 %bitcast_convert_fusion.refs_0_ = bf16[32,256]{1,0:T(8,128)(2,1)S(1)} fusion(f32[1,32,256]{2,1,0:T(8,128)} %param.4), kind=kLoop, calls=%fused_computation.17 | loop fusion | flops 8192 | bytes 49152 | tf_op jit(solution)/shard_map/convert_element_type | solution.py:204
  6.5 0.7 %collective-permute-done.1.refs_2_ = f32[32,256]{1,0:T(8,128)S(1)} collective-permute-done((f32[32,256]{1,0:T(8,128)}, f32[32,256]{1,0:T(8,128)S(1)}, u32[]{:S(2)}, u32[]{:S(2)}) %collective-permute-start.1) | collective-permute-done | bytes 32800 | tf_op jit(solution)/shard_map/ppermute | solution.py:166
  7.2 2.9 %collective-permute-done.refs_1_ = f32[32,256]{1,0:T(8,128)S(1)} collective-permute-done((f32[32,256]{1,0:T(8,128)}, f32[32,256]{1,0:T(8,128)S(1)}, u32[]{:S(2)}, u32[]{:S(2)}) %collective-permute-start) | collective-permute-done | bytes 32800 | tf_op jit(solution)/shard_map/ppermute | solution.py:166
  10.1 2.5 %collective-permute-start.5 = (bf16[4,32,256]{2,1,0:T(8,128)(2,1)S(1)}, bf16[4,32,256]{2,1,0:T(8,128)(2,1)S(1)}, u32[]{:S(2)}, u32[]{:S(2)}) collective-permute-start(bf16[4,32,256]{2,1,0:T(8,128)(2,1)S(1)} %stack_parts.3.refs_0_), channel_id=1, source_target_pairs={{0,6},{2,4},{4,2},{6,0},{1,7},{3,5},{5,3},{7,1},{8,14},{10,12},{12... | collective-permute-start | bytes 196616 | tf_op jit(solution)/shard_map/ppermute | solution.py:166
  13.6 2.8 %sum_counts.1 = (f32[4,256,256]{2,1,0:T(8,128)S(1)}, f32[4,256,256]{2,1,0:T(8,128)S(1)}, bf16[4,256,256]{2,1,0:T(8,128)(2,1)S(1)}, f32[4,256]{1,0:T(4,128)S(1)}) custom-call(s32[1,1,16]{2,1,0:T(1,128)} %visits_ref.1, s32[16,256,256]{2,1,0:T(8,128)} %bitcast.11), custom_call_target="tpu_custom_call" | custom-call | flops 10485760 | bytes 4194304 | tf_op jit(solution)/shard_map/sum_counts/pallas_call | solution.py:61
  18.0 0.8 %collective-permute-done.7.refs_5_ = bf16[2,4,32,256]{3,2,1,0:T(8,128)(2,1)S(1)} collective-permute-done((bf16[2,4,32,256]{3,2,1,0:T(8,128)(2,1)S(1)}, bf16[2,4,32,256]{3,2,1,0:T(8,128)(2,1)S(1)}, u32[]{:S(2)}, u32[]{:S(2)}) %collective-permute-start.7) | collective-permute-done | bytes 131104 | tf_op jit(solution)/shard_map/ppermute | solution.py:166
  19.0 1.2 %swivel_gradient.1 = (f32[2,128,256]{2,1,0:T(8,128)S(1)}, bf16[2,128,256]{2,1,0:T(8,128)(2,1)S(1)}, f32[2,128,256]{2,1,0:T(8,128)S(1)}, bf16[2,128,256]{2,1,0:T(8,128)(2,1)S(1)}) custom-call(s32[4,256]{1,0:T(4,128)S(1)} %reshape.5.marginals_ref, f32[4,256,256]{2,1,0:T(8,128)S(1)} %get-tuple-element.24.roots_ref, ...), custom_call_target="tpu_custom_call" | custom-call | flops 671088640 | bytes 3145728 | tf_op jit(solution)/shard_map/swivel_gradient/pallas_call | solution.py:211
  20.8 0.8 %collective-permute-done.8 = bf16[2,128,256]{2,1,0:T(8,128)(2,1)S(1)} collective-permute-done((bf16[2,128,256]{2,1,0:T(8,128)(2,1)S(1)}, bf16[2,128,256]{2,1,0:T(8,128)(2,1)S(1)}, u32[]{:S(2)}, u32[]{:S(2)}) %collective-permute-start.8) | collective-permute-done | bytes 131104 | tf_op jit(solution)/shard_map/ppermute | solution.py:166
  21.7 1.5 %collective-permute-start.9 = (bf16[1,128,256]{2,1,0:T(8,128)(2,1)S(1)}, bf16[1,128,256]{2,1,0:T(8,128)(2,1)S(1)}, u32[]{:S(2)}, u32[]{:S(2)}) collective-permute-start(bf16[1,128,256]{2,1,0:T(8,128)(2,1)S(1)} %slice.35), channel_id=1, source_target_pairs={{0,2},{2,0},{1,3},{3,1},{4,6},{6,4},{5,7},{7,5},{8,10},{10,8},{9,1... | collective-permute-start | bytes 196616 | tf_op jit(solution)/shard_map/ppermute | solution.py:166
  23.9 2.3 %collective-permute-done.9 = bf16[1,128,256]{2,1,0:T(8,128)(2,1)S(1)} collective-permute-done((bf16[1,128,256]{2,1,0:T(8,128)(2,1)S(1)}, bf16[1,128,256]{2,1,0:T(8,128)(2,1)S(1)}, u32[]{:S(2)}, u32[]{:S(2)}) %collective-permute-start.9) | collective-permute-done | bytes 65568 | tf_op jit(solution)/shard_map/ppermute | solution.py:166
  26.2 0.7 %collective-permute-start.10 = (bf16[128,256]{1,0:T(8,128)(2,1)S(1)}, bf16[128,256]{1,0:T(8,128)(2,1)S(1)}, u32[]{:S(2)}, u32[]{:S(2)}) collective-permute-start(bf16[128,256]{1,0:T(8,128)(2,1)S(1)} %fusion.2), channel_id=1, source_target_pairs={{0,4},{4,0},{1,5},{5,1},{2,6},{6,2},{3,7},{7,3},{8,12},{12,8},{9,1... | collective-permute-start | bytes 196616 | tf_op jit(solution)/shard_map/ppermute | solution.py:166
  26.9 0.7 %collective-permute-done.14 = bf16[1,128,256]{2,1,0:T(8,128)(2,1)S(1)} collective-permute-done((bf16[1,128,256]{2,1,0:T(8,128)(2,1)S(1)}, bf16[1,128,256]{2,1,0:T(8,128)(2,1)S(1)}, u32[]{:S(2)}, u32[]{:S(2)}) %collective-permute-start.14) | collective-permute-done | bytes 65568 | tf_op jit(solution)/shard_map/ppermute | solution.py:166
  27.6 2.1 %collective-permute-start.15 = (bf16[128,256]{1,0:T(8,128)(2,1)S(1)}, bf16[128,256]{1,0:T(8,128)(2,1)S(1)}, u32[]{:S(2)}, u32[]{:S(2)}) collective-permute-start(bf16[128,256]{1,0:T(8,128)(2,1)S(1)} %fusion.3), channel_id=1, source_target_pairs={{0,16},{8,24},{16,0},{24,8},{1,17},{9,25},{17,1},{25,9},{2,18},{10... | collective-permute-start | bytes 196616 | tf_op jit(solution)/shard_map/ppermute | solution.py:166
  29.7 0.8 %collective-permute-done.10 = bf16[128,256]{1,0:T(8,128)(2,1)S(1)} collective-permute-done((bf16[128,256]{1,0:T(8,128)(2,1)S(1)}, bf16[128,256]{1,0:T(8,128)(2,1)S(1)}, u32[]{:S(2)}, u32[]{:S(2)}) %collective-permute-start.10) | collective-permute-done | bytes 65568 | tf_op jit(solution)/shard_map/ppermute | solution.py:166
  30.6 2.3 %collective-permute-done.15 = bf16[128,256]{1,0:T(8,128)(2,1)S(1)} collective-permute-done((bf16[128,256]{1,0:T(8,128)(2,1)S(1)}, bf16[128,256]{1,0:T(8,128)(2,1)S(1)}, u32[]{:S(2)}, u32[]{:S(2)}) %collective-permute-start.15) | collective-permute-done | bytes 65568 | tf_op jit(solution)/shard_map/ppermute | solution.py:166
  32.9 0.7 %collective-permute-start.16 = (bf16[128,256]{1,0:T(8,128)(2,1)S(1)}, bf16[128,256]{1,0:T(8,128)(2,1)S(1)}, u32[]{:S(2)}, u32[]{:S(2)}) collective-permute-start(bf16[128,256]{1,0:T(8,128)(2,1)S(1)} %add_convert_fusion.1), channel_id=1, source_target_pairs={{0,4},{4,0},{1,5},{5,1},{2,6},{6,2},{3,7},{7,3},{8,12},{12,8},{9,1... | collective-permute-start | bytes 196616 | tf_op jit(solution)/shard_map/ppermute | solution.py:166
  33.7 1.2 %collective-permute-done.11 = bf16[128,256]{1,0:T(8,128)(2,1)S(1)} collective-permute-done((bf16[128,256]{1,0:T(8,128)(2,1)S(1)}, bf16[128,256]{1,0:T(8,128)(2,1)S(1)}, u32[]{:S(2)}, u32[]{:S(2)}) %collective-permute-start.11) | collective-permute-done | bytes 65568 | tf_op jit(solution)/shard_map/ppermute | solution.py:166
  34.9 2.6 %collective-permute-start.12 = (bf16[128,256]{1,0:T(8,128)(2,1)S(1)}, bf16[128,256]{1,0:T(8,128)(2,1)S(1)}, u32[]{:S(2)}, u32[]{:S(2)}) collective-permute-start(bf16[128,256]{1,0:T(8,128)(2,1)S(1)} %add_convert_fusion.2), channel_id=1, source_target_pairs={{0,16},{8,24},{16,0},{24,8},{1,17},{9,25},{17,1},{25,9},{2,18},{10... | collective-permute-start | bytes 196616 | tf_op jit(solution)/shard_map/ppermute | solution.py:166
  37.6 2.7 %collective-permute-done.12 = bf16[128,256]{1,0:T(8,128)(2,1)S(1)} collective-permute-done((bf16[128,256]{1,0:T(8,128)(2,1)S(1)}, bf16[128,256]{1,0:T(8,128)(2,1)S(1)}, u32[]{:S(2)}, u32[]{:S(2)}) %collective-permute-start.12) | collective-permute-done | bytes 65568 | tf_op jit(solution)/shard_map/ppermute | solution.py:166
  40.3 0.7 %pad_bitcast_fusion = f32[1,256,256]{2,1,0:T(8,128)} fusion(f32[128,256]{1,0:T(8,128)S(1)} %convert_add_fusion.2), kind=kLoop, calls=%fused_computation.1 | loop fusion | bytes 393216 | tf_op jit(solution)/shard_map/broadcast_in_dim | solution.py:239
  41.0 0.9 %collective-permute-done.17 = bf16[128,256]{1,0:T(8,128)(2,1)S(1)} collective-permute-done((bf16[128,256]{1,0:T(8,128)(2,1)S(1)}, bf16[128,256]{1,0:T(8,128)(2,1)S(1)}, u32[]{:S(2)}, u32[]{:S(2)}) %collective-permute-start.17) | collective-permute-done | bytes 65568 | tf_op jit(solution)/shard_map/ppermute | solution.py:166
  41.9 0.7 %bitcast_dynamic-update-slice_fusion = f32[1,256,256]{2,1,0:T(8,128)} fusion(f32[1,256,256]{2,1,0:T(8,128)} %pad_bitcast_fusion, bf16[128,256]{1,0:T(8,128)(2,1)S(1)} %collective-permute-done.17, bf16[128,256]{1,0:T(8,128)(2,1)S(1)} %add_convert_fusion), kind=kLoop, calls=%fused_computation.9 | loop fusion | flops 98304 | bytes 262144 | tf_op jit(solution)/shard_map/dynamic_update_slice | solution.py:240
  (34 shorter events, 4.3 us)
Async XLA Ops:
  0.0 18.0 %copy-start = (s32[1024]{0:T(1024)S(1)}, s32[1024]{0:T(1024)}, u32[]{:S(2)}) copy-start(s32[1024]{0:T(1024)} %param.5) | copy-start | bytes 12292
  0.0 7.2 %collective-permute-start.1 = (f32[32,256]{1,0:T(8,128)}, f32[32,256]{1,0:T(8,128)S(1)}, u32[]{:S(2)}, u32[]{:S(2)}) collective-permute-start(f32[32,256]{1,0:T(8,128)} %bitcast.12), channel_id=1, source_target_pairs={{0,24},{8,16},{16,8},{24,0},{1,25},{9,17},{17,9},{25,1},{2,26},{10... | collective-permute-start | bytes 98312 | tf_op jit(solution)/shard_map/ppermute | solution.py:166
  5.1 5.0 %collective-permute-start = (f32[32,256]{1,0:T(8,128)}, f32[32,256]{1,0:T(8,128)S(1)}, u32[]{:S(2)}, u32[]{:S(2)}) collective-permute-start(f32[32,256]{1,0:T(8,128)} %bitcast.13), channel_id=1, source_target_pairs={{0,16},{8,24},{16,0},{24,8},{1,17},{9,25},{17,1},{25,9},{2,18},{10... | collective-permute-start | bytes 98312 | tf_op jit(solution)/shard_map/ppermute | solution.py:166
  5.1 5.0 %collective-permute-start.2 = (f32[32,256]{1,0:T(8,128)}, f32[32,256]{1,0:T(8,128)S(1)}, u32[]{:S(2)}, u32[]{:S(2)}) collective-permute-start(f32[32,256]{1,0:T(8,128)} %bitcast.14), channel_id=1, source_target_pairs={{0,8},{8,0},{16,24},{24,16},{1,9},{9,1},{17,25},{25,17},{2,10},{10... | collective-permute-start | bytes 98312 | tf_op jit(solution)/shard_map/ppermute | solution.py:166
  10.1 6.4 %collective-permute-start.5 = (bf16[4,32,256]{2,1,0:T(8,128)(2,1)S(1)}, bf16[4,32,256]{2,1,0:T(8,128)(2,1)S(1)}, u32[]{:S(2)}, u32[]{:S(2)}) collective-permute-start(bf16[4,32,256]{2,1,0:T(8,128)(2,1)S(1)} %stack_parts.3.refs_0_), channel_id=1, source_target_pairs={{0,6},{2,4},{4,2},{6,0},{1,7},{3,5},{5,3},{7,1},{8,14},{10,12},{12... | collective-permute-start | bytes 196616 | tf_op jit(solution)/shard_map/ppermute | solution.py:166
  12.6 4.3 %collective-permute-start.4 = (bf16[4,32,256]{2,1,0:T(8,128)(2,1)S(1)}, bf16[4,32,256]{2,1,0:T(8,128)(2,1)S(1)}, u32[]{:S(2)}, u32[]{:S(2)}) collective-permute-start(bf16[4,32,256]{2,1,0:T(8,128)(2,1)S(1)} %stack_parts.3.refs_0_), channel_id=1, source_target_pairs={{0,2},{2,0},{4,6},{6,4},{1,3},{3,1},{5,7},{7,5},{8,10},{10,8},{12,... | collective-permute-start | bytes 196616 | tf_op jit(solution)/shard_map/ppermute | solution.py:166
  13.1 4.3 %collective-permute-start.3 = (bf16[4,32,256]{2,1,0:T(8,128)(2,1)S(1)}, bf16[4,32,256]{2,1,0:T(8,128)(2,1)S(1)}, u32[]{:S(2)}, u32[]{:S(2)}) collective-permute-start(bf16[4,32,256]{2,1,0:T(8,128)(2,1)S(1)} %stack_parts.3.refs_0_), channel_id=1, source_target_pairs={{0,4},{2,6},{4,0},{6,2},{1,5},{3,7},{5,1},{7,3},{8,12},{10,14},{12... | collective-permute-start | bytes 196616 | tf_op jit(solution)/shard_map/ppermute | solution.py:166
  17.4 1.4 %collective-permute-start.7 = (bf16[2,4,32,256]{3,2,1,0:T(8,128)(2,1)S(1)}, bf16[2,4,32,256]{3,2,1,0:T(8,128)(2,1)S(1)}, u32[]{:S(2)}, u32[]{:S(2)}) collective-permute-start(bf16[2,4,32,256]{3,2,1,0:T(8,128)(2,1)S(1)} %stack_parts.5), channel_id=1, source_target_pairs={{0,1},{1,0},{2,3},{3,2},{4,5},{5,4},{6,7},{7,6},{8,9},{9,8},{10,11... | collective-permute-start | bytes 393224 | tf_op jit(solution)/shard_map/ppermute | solution.py:166
  17.5 1.5 %collective-permute-start.6 = (bf16[2,4,32,256]{3,2,1,0:T(8,128)(2,1)S(1)}, bf16[2,4,32,256]{3,2,1,0:T(8,128)(2,1)S(1)}, u32[]{:S(2)}, u32[]{:S(2)}) collective-permute-start(bf16[2,4,32,256]{3,2,1,0:T(8,128)(2,1)S(1)} %stack_parts.4), channel_id=1, source_target_pairs={{0,1},{1,0},{2,3},{3,2},{4,5},{5,4},{6,7},{7,6},{8,9},{9,8},{10,11... | collective-permute-start | bytes 393224 | tf_op jit(solution)/shard_map/ppermute | solution.py:166
  20.2 1.4 %collective-permute-start.8 = (bf16[2,128,256]{2,1,0:T(8,128)(2,1)S(1)}, bf16[2,128,256]{2,1,0:T(8,128)(2,1)S(1)}, u32[]{:S(2)}, u32[]{:S(2)}) collective-permute-start(bf16[2,128,256]{2,1,0:T(8,128)(2,1)S(1)} %get-tuple-element.32), channel_id=1, source_target_pairs={{0,1},{1,0},{2,3},{3,2},{4,5},{5,4},{6,7},{7,6},{8,9},{9,8},{10,11... | collective-permute-start | bytes 393224 | tf_op jit(solution)/shard_map/ppermute | solution.py:166
  20.6 2.6 %collective-permute-start.13 = (bf16[2,128,256]{2,1,0:T(8,128)(2,1)S(1)}, bf16[2,128,256]{2,1,0:T(8,128)(2,1)S(1)}, u32[]{:S(2)}, u32[]{:S(2)}) collective-permute-start(bf16[2,128,256]{2,1,0:T(8,128)(2,1)S(1)} %get-tuple-element.34), channel_id=1, source_target_pairs={{0,1},{1,0},{2,3},{3,2},{4,5},{5,4},{6,7},{7,6},{8,9},{9,8},{10,11... | collective-permute-start | bytes 393224 | tf_op jit(solution)/shard_map/ppermute | solution.py:166
  21.7 4.5 %collective-permute-start.9 = (bf16[1,128,256]{2,1,0:T(8,128)(2,1)S(1)}, bf16[1,128,256]{2,1,0:T(8,128)(2,1)S(1)}, u32[]{:S(2)}, u32[]{:S(2)}) collective-permute-start(bf16[1,128,256]{2,1,0:T(8,128)(2,1)S(1)} %slice.35), channel_id=1, source_target_pairs={{0,2},{2,0},{1,3},{3,1},{4,6},{6,4},{5,7},{7,5},{8,10},{10,8},{9,1... | collective-permute-start | bytes 196616 | tf_op jit(solution)/shard_map/ppermute | solution.py:166
  23.3 4.3 %collective-permute-start.14 = (bf16[1,128,256]{2,1,0:T(8,128)(2,1)S(1)}, bf16[1,128,256]{2,1,0:T(8,128)(2,1)S(1)}, u32[]{:S(2)}, u32[]{:S(2)}) collective-permute-start(bf16[1,128,256]{2,1,0:T(8,128)(2,1)S(1)} %slice.34), channel_id=1, source_target_pairs={{0,2},{2,0},{1,3},{3,1},{4,6},{6,4},{5,7},{7,5},{8,10},{10,8},{9,1... | collective-permute-start | bytes 196616 | tf_op jit(solution)/shard_map/ppermute | solution.py:166
  26.2 4.3 %collective-permute-start.10 = (bf16[128,256]{1,0:T(8,128)(2,1)S(1)}, bf16[128,256]{1,0:T(8,128)(2,1)S(1)}, u32[]{:S(2)}, u32[]{:S(2)}) collective-permute-start(bf16[128,256]{1,0:T(8,128)(2,1)S(1)} %fusion.2), channel_id=1, source_target_pairs={{0,4},{4,0},{1,5},{5,1},{2,6},{6,2},{3,7},{7,3},{8,12},{12,8},{9,1... | collective-permute-start | bytes 196616 | tf_op jit(solution)/shard_map/ppermute | solution.py:166
  27.6 5.3 %collective-permute-start.15 = (bf16[128,256]{1,0:T(8,128)(2,1)S(1)}, bf16[128,256]{1,0:T(8,128)(2,1)S(1)}, u32[]{:S(2)}, u32[]{:S(2)}) collective-permute-start(bf16[128,256]{1,0:T(8,128)(2,1)S(1)} %fusion.3), channel_id=1, source_target_pairs={{0,16},{8,24},{16,0},{24,8},{1,17},{9,25},{17,1},{25,9},{2,18},{10... | collective-permute-start | bytes 196616 | tf_op jit(solution)/shard_map/ppermute | solution.py:166
  30.6 4.3 %collective-permute-start.11 = (bf16[128,256]{1,0:T(8,128)(2,1)S(1)}, bf16[128,256]{1,0:T(8,128)(2,1)S(1)}, u32[]{:S(2)}, u32[]{:S(2)}) collective-permute-start(bf16[128,256]{1,0:T(8,128)(2,1)S(1)} %add_convert_fusion.3), channel_id=1, source_target_pairs={{0,8},{8,0},{16,24},{24,16},{1,9},{9,1},{17,25},{25,17},{2,10},{10... | collective-permute-start | bytes 196616 | tf_op jit(solution)/shard_map/ppermute | solution.py:166
  32.9 4.6 %collective-permute-start.16 = (bf16[128,256]{1,0:T(8,128)(2,1)S(1)}, bf16[128,256]{1,0:T(8,128)(2,1)S(1)}, u32[]{:S(2)}, u32[]{:S(2)}) collective-permute-start(bf16[128,256]{1,0:T(8,128)(2,1)S(1)} %add_convert_fusion.1), channel_id=1, source_target_pairs={{0,4},{4,0},{1,5},{5,1},{2,6},{6,2},{3,7},{7,3},{8,12},{12,8},{9,1... | collective-permute-start | bytes 196616 | tf_op jit(solution)/shard_map/ppermute | solution.py:166
  34.9 5.4 %collective-permute-start.12 = (bf16[128,256]{1,0:T(8,128)(2,1)S(1)}, bf16[128,256]{1,0:T(8,128)(2,1)S(1)}, u32[]{:S(2)}, u32[]{:S(2)}) collective-permute-start(bf16[128,256]{1,0:T(8,128)(2,1)S(1)} %add_convert_fusion.2), channel_id=1, source_target_pairs={{0,16},{8,24},{16,0},{24,8},{1,17},{9,25},{17,1},{25,9},{2,18},{10... | collective-permute-start | bytes 196616 | tf_op jit(solution)/shard_map/ppermute | solution.py:166
  37.6 4.3 %collective-permute-start.17 = (bf16[128,256]{1,0:T(8,128)(2,1)S(1)}, bf16[128,256]{1,0:T(8,128)(2,1)S(1)}, u32[]{:S(2)}, u32[]{:S(2)}) collective-permute-start(bf16[128,256]{1,0:T(8,128)(2,1)S(1)} %add_convert_fusion), channel_id=1, source_target_pairs={{0,8},{8,0},{16,24},{24,16},{1,9},{9,1},{17,25},{25,17},{2,10},{10... | collective-permute-start | bytes 196616 | tf_op jit(solution)/shard_map/ppermute | solution.py:166

commit v8 on v7

--- a/solution.py
+++ b/solution.py
@@ -21,7 +21,7 @@
 
 def count_kernel(tiles, visits_ref, counts_ref, roots_ref, logs_ref, live_ref, tiles_ref, visits, held, visits_sem, sems):
     size = counts_ref.shape[1]
-    step = 32
+    step = 16
 
     def fetch(k):
         return pltpu.make_async_copy(counts_ref.at[k], held.at[k], sems.at[k])

time: 42.7 us -> 42.7 us (level)
  no operation moved by 1% of the time
where the time goes in v8:
time: 42.7 us; the launch traced here: 42.6 us
  starting transfers between devices  18.8 us (44%)
  waiting for transfers between devices  17.2 us (40%)
  Pallas kernels  4.04 us (9%)
  other arithmetic  1.64 us (4%)
  local copies, waits for them, and re-layouts  0.75 us (2%)
    ppermute x18, starting transfers between devices, swap(): lax.ppermute(value, axes, [(i, i ^ both) for i in range(math.prod(sizes))])  18.8 us
    ppermute x18, waiting for transfers between devices, swap(): lax.ppermute(value, axes, [(i, i ^ both) for i in range(math.prod(sizes))])  17.2 us
    pallas_call x1, Pallas kernels, sum_counts(): pl.pallas_call(functools.partial(count_kernel, tiles), out_shape=[jax.Sha...  2.83 us
    pallas_call x1, Pallas kernels, local(): pl.pallas_call(functools.partial(gradient_kernel, groups), out_shape=[jax...  1.18 us
  transfers between devices with their start and end apart: 18, of which 14 were waited for; matrix products, arithmetic and copies ran while one was open for 4% of the time, Pallas kernels for 7%

profile of v8, /device:TPU:0, one launch (start us, length us, event | category | flops | bytes accessed | tf_op | source)
XLA Modules:
  0.0 42.6 jit_solution(10101728122736780648)
XLA Ops:
  0.0 5.0 %collective-permute-start.1 = (f32[32,256]{1,0:T(8,128)}, f32[32,256]{1,0:T(8,128)S(1)}, u32[]{:S(2)}, u32[]{:S(2)}) collective-permute-start(f32[32,256]{1,0:T(8,128)} %bitcast.12), channel_id=1, source_target_pairs={{0,24},{8,16},{16,8},{24,0},{1,25},{9,17},{17,9},{25,1},{2,26},{10... | collective-permute-start | bytes 98312 | tf_op jit(solution)/shard_map/ppermute | solution.py:166
  5.1 0.6 %collective-permute-start.2 = (f32[32,256]{1,0:T(8,128)}, f32[32,256]{1,0:T(8,128)S(1)}, u32[]{:S(2)}, u32[]{:S(2)}) collective-permute-start(f32[32,256]{1,0:T(8,128)} %bitcast.14), channel_id=1, source_target_pairs={{0,8},{8,0},{16,24},{24,16},{1,9},{9,1},{17,25},{25,17},{2,10},{10... | collective-permute-start | bytes 98312 | tf_op jit(solution)/shard_map/ppermute | solution.py:166
  5.7 0.8 %bitcast_convert_fusion.refs_0_ = bf16[32,256]{1,0:T(8,128)(2,1)S(1)} fusion(f32[1,32,256]{2,1,0:T(8,128)} %param.4), kind=kLoop, calls=%fused_computation.17 | loop fusion | flops 8192 | bytes 49152 | tf_op jit(solution)/shard_map/convert_element_type | solution.py:204
  6.5 0.7 %collective-permute-done.1.refs_2_ = f32[32,256]{1,0:T(8,128)S(1)} collective-permute-done((f32[32,256]{1,0:T(8,128)}, f32[32,256]{1,0:T(8,128)S(1)}, u32[]{:S(2)}, u32[]{:S(2)}) %collective-permute-start.1) | collective-permute-done | bytes 32800 | tf_op jit(solution)/shard_map/ppermute | solution.py:166
  7.2 2.9 %collective-permute-done.refs_1_ = f32[32,256]{1,0:T(8,128)S(1)} collective-permute-done((f32[32,256]{1,0:T(8,128)}, f32[32,256]{1,0:T(8,128)S(1)}, u32[]{:S(2)}, u32[]{:S(2)}) %collective-permute-start) | collective-permute-done | bytes 32800 | tf_op jit(solution)/shard_map/ppermute | solution.py:166
  10.1 2.5 %collective-permute-start.5 = (bf16[4,32,256]{2,1,0:T(8,128)(2,1)S(1)}, bf16[4,32,256]{2,1,0:T(8,128)(2,1)S(1)}, u32[]{:S(2)}, u32[]{:S(2)}) collective-permute-start(bf16[4,32,256]{2,1,0:T(8,128)(2,1)S(1)} %stack_parts.3.refs_0_), channel_id=1, source_target_pairs={{0,6},{2,4},{4,2},{6,0},{1,7},{3,5},{5,3},{7,1},{8,14},{10,12},{12... | collective-permute-start | bytes 196616 | tf_op jit(solution)/shard_map/ppermute | solution.py:166
  13.6 2.8 %sum_counts.1 = (f32[4,256,256]{2,1,0:T(8,128)S(1)}, f32[4,256,256]{2,1,0:T(8,128)S(1)}, bf16[4,256,256]{2,1,0:T(8,128)(2,1)S(1)}, f32[4,256]{1,0:T(4,128)S(1)}) custom-call(s32[1,1,16]{2,1,0:T(1,128)} %visits_ref.1, s32[16,256,256]{2,1,0:T(8,128)} %bitcast.11), custom_call_target="tpu_custom_call" | custom-call | flops 10485760 | bytes 4194304 | tf_op jit(solution)/shard_map/sum_counts/pallas_call | solution.py:61
  18.0 0.8 %collective-permute-done.7.refs_5_ = bf16[2,4,32,256]{3,2,1,0:T(8,128)(2,1)S(1)} collective-permute-done((bf16[2,4,32,256]{3,2,1,0:T(8,128)(2,1)S(1)}, bf16[2,4,32,256]{3,2,1,0:T(8,128)(2,1)S(1)}, u32[]{:S(2)}, u32[]{:S(2)}) %collective-permute-start.7) | collective-permute-done | bytes 131104 | tf_op jit(solution)/shard_map/ppermute | solution.py:166
  19.0 1.2 %swivel_gradient.1 = (f32[2,128,256]{2,1,0:T(8,128)S(1)}, bf16[2,128,256]{2,1,0:T(8,128)(2,1)S(1)}, f32[2,128,256]{2,1,0:T(8,128)S(1)}, bf16[2,128,256]{2,1,0:T(8,128)(2,1)S(1)}) custom-call(s32[4,256]{1,0:T(4,128)S(1)} %reshape.5.marginals_ref, f32[4,256,256]{2,1,0:T(8,128)S(1)} %get-tuple-element.24.roots_ref, ...), custom_call_target="tpu_custom_call" | custom-call | flops 671088640 | bytes 3145728 | tf_op jit(solution)/shard_map/swivel_gradient/pallas_call | solution.py:211
  20.8 0.8 %collective-permute-done.8 = bf16[2,128,256]{2,1,0:T(8,128)(2,1)S(1)} collective-permute-done((bf16[2,128,256]{2,1,0:T(8,128)(2,1)S(1)}, bf16[2,128,256]{2,1,0:T(8,128)(2,1)S(1)}, u32[]{:S(2)}, u32[]{:S(2)}) %collective-permute-start.8) | collective-permute-done | bytes 131104 | tf_op jit(solution)/shard_map/ppermute | solution.py:166
  21.7 1.5 %collective-permute-start.9 = (bf16[1,128,256]{2,1,0:T(8,128)(2,1)S(1)}, bf16[1,128,256]{2,1,0:T(8,128)(2,1)S(1)}, u32[]{:S(2)}, u32[]{:S(2)}) collective-permute-start(bf16[1,128,256]{2,1,0:T(8,128)(2,1)S(1)} %slice.35), channel_id=1, source_target_pairs={{0,2},{2,0},{1,3},{3,1},{4,6},{6,4},{5,7},{7,5},{8,10},{10,8},{9,1... | collective-permute-start | bytes 196616 | tf_op jit(solution)/shard_map/ppermute | solution.py:166
  23.9 2.3 %collective-permute-done.9 = bf16[1,128,256]{2,1,0:T(8,128)(2,1)S(1)} collective-permute-done((bf16[1,128,256]{2,1,0:T(8,128)(2,1)S(1)}, bf16[1,128,256]{2,1,0:T(8,128)(2,1)S(1)}, u32[]{:S(2)}, u32[]{:S(2)}) %collective-permute-start.9) | collective-permute-done | bytes 65568 | tf_op jit(solution)/shard_map/ppermute | solution.py:166
  26.2 0.7 %collective-permute-start.10 = (bf16[128,256]{1,0:T(8,128)(2,1)S(1)}, bf16[128,256]{1,0:T(8,128)(2,1)S(1)}, u32[]{:S(2)}, u32[]{:S(2)}) collective-permute-start(bf16[128,256]{1,0:T(8,128)(2,1)S(1)} %fusion.2), channel_id=1, source_target_pairs={{0,4},{4,0},{1,5},{5,1},{2,6},{6,2},{3,7},{7,3},{8,12},{12,8},{9,1... | collective-permute-start | bytes 196616 | tf_op jit(solution)/shard_map/ppermute | solution.py:166
  26.9 0.7 %collective-permute-done.14 = bf16[1,128,256]{2,1,0:T(8,128)(2,1)S(1)} collective-permute-done((bf16[1,128,256]{2,1,0:T(8,128)(2,1)S(1)}, bf16[1,128,256]{2,1,0:T(8,128)(2,1)S(1)}, u32[]{:S(2)}, u32[]{:S(2)}) %collective-permute-start.14) | collective-permute-done | bytes 65568 | tf_op jit(solution)/shard_map/ppermute | solution.py:166
  27.6 2.1 %collective-permute-start.15 = (bf16[128,256]{1,0:T(8,128)(2,1)S(1)}, bf16[128,256]{1,0:T(8,128)(2,1)S(1)}, u32[]{:S(2)}, u32[]{:S(2)}) collective-permute-start(bf16[128,256]{1,0:T(8,128)(2,1)S(1)} %fusion.3), channel_id=1, source_target_pairs={{0,16},{8,24},{16,0},{24,8},{1,17},{9,25},{17,1},{25,9},{2,18},{10... | collective-permute-start | bytes 196616 | tf_op jit(solution)/shard_map/ppermute | solution.py:166
  29.7 0.8 %collective-permute-done.10 = bf16[128,256]{1,0:T(8,128)(2,1)S(1)} collective-permute-done((bf16[128,256]{1,0:T(8,128)(2,1)S(1)}, bf16[128,256]{1,0:T(8,128)(2,1)S(1)}, u32[]{:S(2)}, u32[]{:S(2)}) %collective-permute-start.10) | collective-permute-done | bytes 65568 | tf_op jit(solution)/shard_map/ppermute | solution.py:166
  30.6 2.3 %collective-permute-done.15 = bf16[128,256]{1,0:T(8,128)(2,1)S(1)} collective-permute-done((bf16[128,256]{1,0:T(8,128)(2,1)S(1)}, bf16[128,256]{1,0:T(8,128)(2,1)S(1)}, u32[]{:S(2)}, u32[]{:S(2)}) %collective-permute-start.15) | collective-permute-done | bytes 65568 | tf_op jit(solution)/shard_map/ppermute | solution.py:166
  32.9 0.7 %collective-permute-start.16 = (bf16[128,256]{1,0:T(8,128)(2,1)S(1)}, bf16[128,256]{1,0:T(8,128)(2,1)S(1)}, u32[]{:S(2)}, u32[]{:S(2)}) collective-permute-start(bf16[128,256]{1,0:T(8,128)(2,1)S(1)} %add_convert_fusion.1), channel_id=1, source_target_pairs={{0,4},{4,0},{1,5},{5,1},{2,6},{6,2},{3,7},{7,3},{8,12},{12,8},{9,1... | collective-permute-start | bytes 196616 | tf_op jit(solution)/shard_map/ppermute | solution.py:166
  33.7 1.2 %collective-permute-done.11 = bf16[128,256]{1,0:T(8,128)(2,1)S(1)} collective-permute-done((bf16[128,256]{1,0:T(8,128)(2,1)S(1)}, bf16[128,256]{1,0:T(8,128)(2,1)S(1)}, u32[]{:S(2)}, u32[]{:S(2)}) %collective-permute-start.11) | collective-permute-done | bytes 65568 | tf_op jit(solution)/shard_map/ppermute | solution.py:166
  34.9 2.6 %collective-permute-start.12 = (bf16[128,256]{1,0:T(8,128)(2,1)S(1)}, bf16[128,256]{1,0:T(8,128)(2,1)S(1)}, u32[]{:S(2)}, u32[]{:S(2)}) collective-permute-start(bf16[128,256]{1,0:T(8,128)(2,1)S(1)} %add_convert_fusion.2), channel_id=1, source_target_pairs={{0,16},{8,24},{16,0},{24,8},{1,17},{9,25},{17,1},{25,9},{2,18},{10... | collective-permute-start | bytes 196616 | tf_op jit(solution)/shard_map/ppermute | solution.py:166
  37.6 2.7 %collective-permute-done.12 = bf16[128,256]{1,0:T(8,128)(2,1)S(1)} collective-permute-done((bf16[128,256]{1,0:T(8,128)(2,1)S(1)}, bf16[128,256]{1,0:T(8,128)(2,1)S(1)}, u32[]{:S(2)}, u32[]{:S(2)}) %collective-permute-start.12) | collective-permute-done | bytes 65568 | tf_op jit(solution)/shard_map/ppermute | solution.py:166
  40.3 0.7 %pad_bitcast_fusion = f32[1,256,256]{2,1,0:T(8,128)} fusion(f32[128,256]{1,0:T(8,128)S(1)} %convert_add_fusion.2), kind=kLoop, calls=%fused_computation.1 | loop fusion | bytes 393216 | tf_op jit(solution)/shard_map/broadcast_in_dim | solution.py:239
  41.0 0.9 %collective-permute-done.17 = bf16[128,256]{1,0:T(8,128)(2,1)S(1)} collective-permute-done((bf16[128,256]{1,0:T(8,128)(2,1)S(1)}, bf16[128,256]{1,0:T(8,128)(2,1)S(1)}, u32[]{:S(2)}, u32[]{:S(2)}) %collective-permute-start.17) | collective-permute-done | bytes 65568 | tf_op jit(solution)/shard_map/ppermute | solution.py:166
  41.9 0.7 %bitcast_dynamic-update-slice_fusion = f32[1,256,256]{2,1,0:T(8,128)} fusion(f32[1,256,256]{2,1,0:T(8,128)} %pad_bitcast_fusion, bf16[128,256]{1,0:T(8,128)(2,1)S(1)} %collective-permute-done.17, bf16[128,256]{1,0:T(8,128)(2,1)S(1)} %add_convert_fusion), kind=kLoop, calls=%fused_computation.9 | loop fusion | flops 98304 | bytes 262144 | tf_op jit(solution)/shard_map/dynamic_update_slice | solution.py:240
  (34 shorter events, 4.3 us)
Async XLA Ops:
  0.0 18.0 %copy-start = (s32[1024]{0:T(1024)S(1)}, s32[1024]{0:T(1024)}, u32[]{:S(2)}) copy-start(s32[1024]{0:T(1024)} %param.5) | copy-start | bytes 12292
  0.0 7.2 %collective-permute-start.1 = (f32[32,256]{1,0:T(8,128)}, f32[32,256]{1,0:T(8,128)S(1)}, u32[]{:S(2)}, u32[]{:S(2)}) collective-permute-start(f32[32,256]{1,0:T(8,128)} %bitcast.12), channel_id=1, source_target_pairs={{0,24},{8,16},{16,8},{24,0},{1,25},{9,17},{17,9},{25,1},{2,26},{10... | collective-permute-start | bytes 98312 | tf_op jit(solution)/shard_map/ppermute | solution.py:166
  5.1 5.0 %collective-permute-start = (f32[32,256]{1,0:T(8,128)}, f32[32,256]{1,0:T(8,128)S(1)}, u32[]{:S(2)}, u32[]{:S(2)}) collective-permute-start(f32[32,256]{1,0:T(8,128)} %bitcast.13), channel_id=1, source_target_pairs={{0,16},{8,24},{16,0},{24,8},{1,17},{9,25},{17,1},{25,9},{2,18},{10... | collective-permute-start | bytes 98312 | tf_op jit(solution)/shard_map/ppermute | solution.py:166
  5.1 5.0 %collective-permute-start.2 = (f32[32,256]{1,0:T(8,128)}, f32[32,256]{1,0:T(8,128)S(1)}, u32[]{:S(2)}, u32[]{:S(2)}) collective-permute-start(f32[32,256]{1,0:T(8,128)} %bitcast.14), channel_id=1, source_target_pairs={{0,8},{8,0},{16,24},{24,16},{1,9},{9,1},{17,25},{25,17},{2,10},{10... | collective-permute-start | bytes 98312 | tf_op jit(solution)/shard_map/ppermute | solution.py:166
  10.1 6.4 %collective-permute-start.5 = (bf16[4,32,256]{2,1,0:T(8,128)(2,1)S(1)}, bf16[4,32,256]{2,1,0:T(8,128)(2,1)S(1)}, u32[]{:S(2)}, u32[]{:S(2)}) collective-permute-start(bf16[4,32,256]{2,1,0:T(8,128)(2,1)S(1)} %stack_parts.3.refs_0_), channel_id=1, source_target_pairs={{0,6},{2,4},{4,2},{6,0},{1,7},{3,5},{5,3},{7,1},{8,14},{10,12},{12... | collective-permute-start | bytes 196616 | tf_op jit(solution)/shard_map/ppermute | solution.py:166
  12.6 4.3 %collective-permute-start.4 = (bf16[4,32,256]{2,1,0:T(8,128)(2,1)S(1)}, bf16[4,32,256]{2,1,0:T(8,128)(2,1)S(1)}, u32[]{:S(2)}, u32[]{:S(2)}) collective-permute-start(bf16[4,32,256]{2,1,0:T(8,128)(2,1)S(1)} %stack_parts.3.refs_0_), channel_id=1, source_target_pairs={{0,2},{2,0},{4,6},{6,4},{1,3},{3,1},{5,7},{7,5},{8,10},{10,8},{12,... | collective-permute-start | bytes 196616 | tf_op jit(solution)/shard_map/ppermute | solution.py:166
  13.1 4.3 %collective-permute-start.3 = (bf16[4,32,256]{2,1,0:T(8,128)(2,1)S(1)}, bf16[4,32,256]{2,1,0:T(8,128)(2,1)S(1)}, u32[]{:S(2)}, u32[]{:S(2)}) collective-permute-start(bf16[4,32,256]{2,1,0:T(8,128)(2,1)S(1)} %stack_parts.3.refs_0_), channel_id=1, source_target_pairs={{0,4},{2,6},{4,0},{6,2},{1,5},{3,7},{5,1},{7,3},{8,12},{10,14},{12... | collective-permute-start | bytes 196616 | tf_op jit(solution)/shard_map/ppermute | solution.py:166
  17.4 1.4 %collective-permute-start.7 = (bf16[2,4,32,256]{3,2,1,0:T(8,128)(2,1)S(1)}, bf16[2,4,32,256]{3,2,1,0:T(8,128)(2,1)S(1)}, u32[]{:S(2)}, u32[]{:S(2)}) collective-permute-start(bf16[2,4,32,256]{3,2,1,0:T(8,128)(2,1)S(1)} %stack_parts.5), channel_id=1, source_target_pairs={{0,1},{1,0},{2,3},{3,2},{4,5},{5,4},{6,7},{7,6},{8,9},{9,8},{10,11... | collective-permute-start | bytes 393224 | tf_op jit(solution)/shard_map/ppermute | solution.py:166
  17.5 1.5 %collective-permute-start.6 = (bf16[2,4,32,256]{3,2,1,0:T(8,128)(2,1)S(1)}, bf16[2,4,32,256]{3,2,1,0:T(8,128)(2,1)S(1)}, u32[]{:S(2)}, u32[]{:S(2)}) collective-permute-start(bf16[2,4,32,256]{3,2,1,0:T(8,128)(2,1)S(1)} %stack_parts.4), channel_id=1, source_target_pairs={{0,1},{1,0},{2,3},{3,2},{4,5},{5,4},{6,7},{7,6},{8,9},{9,8},{10,11... | collective-permute-start | bytes 393224 | tf_op jit(solution)/shard_map/ppermute | solution.py:166
  20.2 1.4 %collective-permute-start.8 = (bf16[2,128,256]{2,1,0:T(8,128)(2,1)S(1)}, bf16[2,128,256]{2,1,0:T(8,128)(2,1)S(1)}, u32[]{:S(2)}, u32[]{:S(2)}) collective-permute-start(bf16[2,128,256]{2,1,0:T(8,128)(2,1)S(1)} %get-tuple-element.32), channel_id=1, source_target_pairs={{0,1},{1,0},{2,3},{3,2},{4,5},{5,4},{6,7},{7,6},{8,9},{9,8},{10,11... | collective-permute-start | bytes 393224 | tf_op jit(solution)/shard_map/ppermute | solution.py:166
  20.6 2.6 %collective-permute-start.13 = (bf16[2,128,256]{2,1,0:T(8,128)(2,1)S(1)}, bf16[2,128,256]{2,1,0:T(8,128)(2,1)S(1)}, u32[]{:S(2)}, u32[]{:S(2)}) collective-permute-start(bf16[2,128,256]{2,1,0:T(8,128)(2,1)S(1)} %get-tuple-element.34), channel_id=1, source_target_pairs={{0,1},{1,0},{2,3},{3,2},{4,5},{5,4},{6,7},{7,6},{8,9},{9,8},{10,11... | collective-permute-start | bytes 393224 | tf_op jit(solution)/shard_map/ppermute | solution.py:166
  21.7 4.5 %collective-permute-start.9 = (bf16[1,128,256]{2,1,0:T(8,128)(2,1)S(1)}, bf16[1,128,256]{2,1,0:T(8,128)(2,1)S(1)}, u32[]{:S(2)}, u32[]{:S(2)}) collective-permute-start(bf16[1,128,256]{2,1,0:T(8,128)(2,1)S(1)} %slice.35), channel_id=1, source_target_pairs={{0,2},{2,0},{1,3},{3,1},{4,6},{6,4},{5,7},{7,5},{8,10},{10,8},{9,1... | collective-permute-start | bytes 196616 | tf_op jit(solution)/shard_map/ppermute | solution.py:166
  23.3 4.3 %collective-permute-start.14 = (bf16[1,128,256]{2,1,0:T(8,128)(2,1)S(1)}, bf16[1,128,256]{2,1,0:T(8,128)(2,1)S(1)}, u32[]{:S(2)}, u32[]{:S(2)}) collective-permute-start(bf16[1,128,256]{2,1,0:T(8,128)(2,1)S(1)} %slice.34), channel_id=1, source_target_pairs={{0,2},{2,0},{1,3},{3,1},{4,6},{6,4},{5,7},{7,5},{8,10},{10,8},{9,1... | collective-permute-start | bytes 196616 | tf_op jit(solution)/shard_map/ppermute | solution.py:166
  26.2 4.3 %collective-permute-start.10 = (bf16[128,256]{1,0:T(8,128)(2,1)S(1)}, bf16[128,256]{1,0:T(8,128)(2,1)S(1)}, u32[]{:S(2)}, u32[]{:S(2)}) collective-permute-start(bf16[128,256]{1,0:T(8,128)(2,1)S(1)} %fusion.2), channel_id=1, source_target_pairs={{0,4},{4,0},{1,5},{5,1},{2,6},{6,2},{3,7},{7,3},{8,12},{12,8},{9,1... | collective-permute-start | bytes 196616 | tf_op jit(solution)/shard_map/ppermute | solution.py:166
  27.6 5.3 %collective-permute-start.15 = (bf16[128,256]{1,0:T(8,128)(2,1)S(1)}, bf16[128,256]{1,0:T(8,128)(2,1)S(1)}, u32[]{:S(2)}, u32[]{:S(2)}) collective-permute-start(bf16[128,256]{1,0:T(8,128)(2,1)S(1)} %fusion.3), channel_id=1, source_target_pairs={{0,16},{8,24},{16,0},{24,8},{1,17},{9,25},{17,1},{25,9},{2,18},{10... | collective-permute-start | bytes 196616 | tf_op jit(solution)/shard_map/ppermute | solution.py:166
  30.6 4.3 %collective-permute-start.11 = (bf16[128,256]{1,0:T(8,128)(2,1)S(1)}, bf16[128,256]{1,0:T(8,128)(2,1)S(1)}, u32[]{:S(2)}, u32[]{:S(2)}) collective-permute-start(bf16[128,256]{1,0:T(8,128)(2,1)S(1)} %add_convert_fusion.3), channel_id=1, source_target_pairs={{0,8},{8,0},{16,24},{24,16},{1,9},{9,1},{17,25},{25,17},{2,10},{10... | collective-permute-start | bytes 196616 | tf_op jit(solution)/shard_map/ppermute | solution.py:166
  32.9 4.6 %collective-permute-start.16 = (bf16[128,256]{1,0:T(8,128)(2,1)S(1)}, bf16[128,256]{1,0:T(8,128)(2,1)S(1)}, u32[]{:S(2)}, u32[]{:S(2)}) collective-permute-start(bf16[128,256]{1,0:T(8,128)(2,1)S(1)} %add_convert_fusion.1), channel_id=1, source_target_pairs={{0,4},{4,0},{1,5},{5,1},{2,6},{6,2},{3,7},{7,3},{8,12},{12,8},{9,1... | collective-permute-start | bytes 196616 | tf_op jit(solution)/shard_map/ppermute | solution.py:166
  34.9 5.4 %collective-permute-start.12 = (bf16[128,256]{1,0:T(8,128)(2,1)S(1)}, bf16[128,256]{1,0:T(8,128)(2,1)S(1)}, u32[]{:S(2)}, u32[]{:S(2)}) collective-permute-start(bf16[128,256]{1,0:T(8,128)(2,1)S(1)} %add_convert_fusion.2), channel_id=1, source_target_pairs={{0,16},{8,24},{16,0},{24,8},{1,17},{9,25},{17,1},{25,9},{2,18},{10... | collective-permute-start | bytes 196616 | tf_op jit(solution)/shard_map/ppermute | solution.py:166
  37.6 4.3 %collective-permute-start.17 = (bf16[128,256]{1,0:T(8,128)(2,1)S(1)}, bf16[128,256]{1,0:T(8,128)(2,1)S(1)}, u32[]{:S(2)}, u32[]{:S(2)}) collective-permute-start(bf16[128,256]{1,0:T(8,128)(2,1)S(1)} %add_convert_fusion), channel_id=1, source_target_pairs={{0,8},{8,0},{16,24},{24,16},{1,9},{9,1},{17,25},{25,17},{2,10},{10... | collective-permute-start | bytes 196616 | tf_op jit(solution)/shard_map/ppermute | solution.py:166
